TPU v7x, 256 devices: a whole 4x4x8 slice. The times are simulated.
256 devices in a mesh: expert: 128 (over z, x, y), dp: 2 (over core).
Axes of the slice: x: 4, y: 4, z: 8, core: 2. Of those that a mesh axis runs over, the one named last changes fastest.
Arguments:
- tokens: bfloat16 [32768, 2048], P(('dp', 'expert')), parts along dimension 0, may hold values from -24 to 24
- logits: float32 [32768, 128], P(('dp', 'expert')), parts along dimension 0, may hold values from -4 to 350
- weights: bfloat16 [128, 2048, 1024], P('expert'), may hold values from -0.125 to 0.125
- router_weight: bfloat16 [2048, 128], replicated, may hold values from -0.125 to 0.125
- expert_picks: int32 [256, 256], P(('dp', 'expert')), parts along dimension 0, may hold values from 0 to 16383, as said below
- cotangent: bfloat16 [256, 256, 1024], P(('dp', 'expert')), parts along dimension 0, may hold values from -1.5 to 1.5
Outputs:
- token_grad: bfloat16 [32768, 2048], P(('dp', 'expert')), parts along dimension 0
- weight_grad: bfloat16 [256, 2048, 1024], P(('dp', 'expert')), parts along dimension 0
- router_grad: float32 [4096, 128], P(('dp', 'expert')), parts along dimension 0
There are 2 independent parts, one for each index of `dp`. A program takes and returns all parts, laid end to end along the dimension named above; an argument that names none is the same for every part. Nothing has to cross between parts.
Inputs may be any that keep to these rules, and one draw needn't show every extreme that they name: `expert_picks`: each expert's list is ascending and names no token twice. Among the tokens of one device (indices k * 128 to (k + 1) * 128 - 1) an expert takes at most 4, and in every draw each expert takes exactly 4 from some devices' tokens.
All inputs are finite; a program needn't handle non-finite values.
Results may differ from a plain program's by a relative error of at most 0.0062.
Values may be sent and summed in bfloat16 or wider, within the bound.
No kernel may reach another device: no remote copies, remote signals or barrier semaphores. Data moves between devices by JAX's collectives and lax.ppermute only.
A program may use at most 64 MiB of HBM per device.

v0:
```python
import jax
import jax.numpy as jnp
from jax import lax
from jax.sharding import PartitionSpec as P


def local(tokens, logits, weights, router_weight, expert_picks, cotangent):
    experts = lax.axis_size("expert")
    tok_rows = tokens.shape[0]
    width = tokens.shape[1]
    capacity = expert_picks.shape[1]
    slot_most = 2 * capacity // experts
    slot_total = experts * slot_most
    device_index = lax.axis_index("expert")
    wanted = expert_picks[0]
    owners = wanted // tok_rows
    owner_ids = jnp.arange(experts, dtype=jnp.int32)
    owner_hot = (owners[:, None] == owner_ids[None, :]).astype(jnp.int32)
    counts = jnp.sum(owner_hot, axis=0)
    starts = jnp.cumsum(counts) - counts
    offset = jnp.sum(owner_hot * starts[None, :], axis=1)
    placed = owners * slot_most + jnp.arange(capacity, dtype=jnp.int32) - offset
    all_lists = lax.all_gather(expert_picks, "expert", axis=0, tiled=True)
    slice_low = device_index * tok_rows
    in_slice = (all_lists >= slice_low) & (all_lists < slice_low + tok_rows)
    first_pos = jnp.sum((all_lists < slice_low).astype(jnp.int32), axis=1)
    in_count = jnp.sum(in_slice.astype(jnp.int32), axis=1)
    columns = jnp.arange(slot_most, dtype=jnp.int32)
    positions = jnp.minimum(first_pos[:, None] + columns[None, :], capacity - 1)
    located = jnp.take_along_axis(all_lists, positions, axis=1) - slice_low
    requested = jnp.where(columns[None, :] < in_count[:, None], located, -1)
    filled = requested >= 0
    flat_rows = jnp.maximum(requested, 0).reshape(slot_total)
    gate_probs = jax.nn.softmax(logits, axis=-1)
    send_rows = jnp.take(tokens, flat_rows, axis=0).reshape(experts, slot_most, width)
    send_rows = jnp.where(filled[:, :, None], send_rows, jnp.zeros((), jnp.bfloat16))
    prob_rows = jnp.take(gate_probs, flat_rows, axis=0).reshape(experts, slot_most, experts)
    identity = jnp.eye(experts, dtype=jnp.float32)
    send_gate = jnp.einsum("ejk,ek->ej", prob_rows, identity)
    send_gate = jnp.where(filled, send_gate, 0.0).astype(jnp.bfloat16)
    weight = weights[0]
    upstream = cotangent[0]
    got_rows, got_gate = (
        lax.all_to_all(send_rows, "expert", split_axis=0, concat_axis=0, tiled=True),
        lax.all_to_all(send_gate, "expert", split_axis=0, concat_axis=0, tiled=True),
    )
    picked_rows = jnp.take(got_rows.reshape(slot_total, width), placed, axis=0)
    gate_vals = jnp.take(got_gate.reshape(slot_total), placed).astype(jnp.float32)
    active = jnp.dot(picked_rows, weight, preferred_element_type=jnp.float32)
    gate_grad = jnp.sum(upstream.astype(jnp.float32) * active, axis=1).astype(jnp.bfloat16)
    back_gate = (
        jnp.zeros((slot_total,), jnp.bfloat16).at[placed].set(gate_grad).reshape(experts, slot_most)
    )
    scaled = (gate_vals[:, None] * upstream.astype(jnp.float32)).astype(jnp.bfloat16)
    weight_grad = lax.dot_general(
        picked_rows, scaled, (((0,), (0,)), ((), ())), preferred_element_type=jnp.float32
    ).astype(jnp.bfloat16)
    row_grad = lax.dot_general(
        scaled, weight, (((1,), (1,)), ((), ())), preferred_element_type=jnp.float32
    ).astype(jnp.bfloat16)
    back_rows = (
        jnp.zeros((slot_total, width), jnp.bfloat16)
        .at[placed]
        .set(row_grad)
        .reshape(experts, slot_most, width)
    )
    got_row_grad, got_gate_grad = (
        lax.all_to_all(back_rows, "expert", split_axis=0, concat_axis=0, tiled=True),
        lax.all_to_all(back_gate, "expert", split_axis=0, concat_axis=0, tiled=True),
    )
    token_ids = jnp.arange(tok_rows, dtype=jnp.int32)
    selector = (token_ids[:, None] == requested.reshape(slot_total)[None, :]).astype(jnp.bfloat16)
    expert_part = jnp.dot(
        selector, got_row_grad.reshape(slot_total, width), preferred_element_type=jnp.float32
    )
    matches = (token_ids[:, None, None] == requested[None, :, :]).astype(jnp.float32)
    score_grad = jnp.einsum("tej,ej->te", matches, got_gate_grad.astype(jnp.float32))
    inner_sum = jnp.sum(gate_probs * score_grad, axis=1, keepdims=True)
    logit_grad = (gate_probs * (score_grad - inner_sum)).astype(jnp.bfloat16)
    router_part = lax.dot_general(
        logit_grad, router_weight, (((1,), (1,)), ((), ())), preferred_element_type=jnp.float32
    )
    token_grad = (expert_part + router_part).astype(jnp.bfloat16)
    router_grad = lax.psum_scatter(
        lax.dot_general(
            tokens, logit_grad, (((0,), (0,)), ((), ())), preferred_element_type=jnp.float32
        ),
        "expert",
        scatter_dimension=0,
        tiled=True,
    )
    return (token_grad, weight_grad[None], router_grad)


def solution(mesh):
    in_specs = (
        P(("dp", "expert"), None),
        P(("dp", "expert"), None),
        P("expert", None, None),
        P(),
        P(("dp", "expert"), None),
        P(("dp", "expert"), None, None),
    )
    out_specs = (
        P(("dp", "expert"), None),
        P(("dp", "expert"), None, None),
        P(("dp", "expert"), None),
    )
    return jax.shard_map(local, mesh=mesh, in_specs=in_specs, out_specs=out_specs, check_vma=False)
```

profile of v0, /device:TPU:0, one launch (start us, length us, event | category | flops | bytes accessed | tf_op | source)
XLA Modules:
  0.0 1189.1 jit_solution(2794369931555448073)
XLA Ops:
  7.2 0.1 lt.173
  7.3 349.4 %all-gather = s32[128,1,256]{2,1,0:T(1,128)S(1)} all-gather(s32[1,1,256]{2,1,0:T(1,128)} %bitcast.98), channel_id=1, replica_groups=mesh['expert'=128,'dp'=2] {'expert'}, dimensions={0}, use_global_device_ids=true | all-gather | bytes 132096 | tf_op jit(solution)/shard_map/all_gather | solution.py:23
  356.8 0.1 convert_reduce_fusion.2
  357.1 0.1 add.200
  357.2 0.1 reshape.529
  357.3 4.5 gather_fusion.4
  361.9 0.1 maximum_compare_fusion
  362.1 0.1 lt.171
  362.2 2.5 gather_fusion.2
  364.7 2.2 gather.35
  366.9 3.6 select_select_fusion
  370.5 7.5 all-to-all-start.2
  378.0 0.1 convert_reduce_fusion
  378.1 0.1 copy.19
  378.3 0.2 reduce-window.8
  378.4 0.1 reduce.1
  378.7 0.2 select_reduce_fusion.1
  378.9 0.2 fusion.43
  379.1 30.8 %all-to-all-done.2 = bf16[128,4,2048]{2,1,0:T(4,128)(2,1)} async-done(((bf16[128,4,2048]{2,1,0:T(4,128)(2,1)}), bf16[128,4,2048]{2,1,0:T(4,128)(2,1)}, u32[]{:S(2)}, u32[]{:S(2)}) %all-to-all-start.2) | async-done | bytes 2097184 | tf_op jit(solution)/shard_map/all_to_all | solution.py:44
  409.9 2.5 reshape.495
  412.5 2.3 gather_fusion.3
  414.8 3.9 fusion.12
  418.7 2.2 scatter_custom_fusion.1
  420.9 0.8 all_to_all.27
  421.6 7.3 all-to-all-start.3
  429.1 11.9 all-to-all-done.3
  441.1 0.2 fusion.35
  441.3 1.1 gather_fusion
  442.4 0.3 fusion.24
  442.8 18.1 %all_to_all.32 = bf16[128,1,4]{2,1,0:T(2,128)(2,1)S(1)} all-to-all(bf16[128,1,4]{2,1,0:T(2,128)(2,1)S(1)} %copy.20), channel_id=1, replica_groups=mesh['expert'=128,'dp'=2] {'expert'}, dimensions={0} | all-to-all | bytes 2048 | tf_op jit(solution)/shard_map/all_to_all | solution.py:45
  460.9 0.2 reduce.2
  461.1 0.1 reshape.492
  461.2 1.9 gather_fusion.1
  463.1 4.5 fusion.4
  467.7 3.5 scatter_custom_fusion
  471.2 2.2 reshape.493
  473.4 6.2 all-to-all-start.1
  479.8 1.3 convolution_bitcast_fusion
  481.1 2.5 copy.32
  483.6 0.1 add.185
  483.7 0.1 lt.157
  483.9 0.1 lt.160
  484.0 4.7 convert_bitcast_fusion
  488.7 22.6 %all-to-all-done.1 = bf16[128,4,2048]{2,1,0:T(4,128)(2,1)S(1)} async-done(((bf16[128,4,2048]{2,1,0:T(4,128)(2,1)}), bf16[128,4,2048]{2,1,0:T(4,128)(2,1)S(1)}, u32[]{:S(2)}, u32[]{:S(2)}) %all-to-all-start.1) | async-done | bytes 2097184 | tf_op jit(solution)/shard_map/all_to_all | solution.py:68
  511.3 2.1 reshape.494
  513.3 2.1 fusion.26
  515.4 1.1 fusion.7
  516.5 665.7 %reduce-scatter.4.cloned.1.call-done = f32[16,128]{1,0:T(8,128)} async-done(((f32[2048,128]{1,0:T(8,128)}), f32[16,128]{1,0:T(8,128)}) %reduce-scatter.4.cloned.1.call-update) | async-done | bytes 8208
  (37 shorter events, 1.0 us)
Async XLA Ops:
  7.2 355.1 %copy-start = (bf16[128,2048]{1,0:T(8,128)(2,1)S(1)}, bf16[128,2048]{1,0:T(8,128)(2,1)}, u32[]{:S(2)}) copy-start(bf16[128,2048]{1,0:T(8,128)(2,1)} %param.6) | copy-start | bytes 1572868
  370.5 7.5 copy-start.3
  370.5 8.0 copy-start.1
  370.5 39.4 %all-to-all-start.2 = ((bf16[128,4,2048]{2,1,0:T(4,128)(2,1)}), bf16[128,4,2048]{2,1,0:T(4,128)(2,1)}, u32[]{:S(2)}, u32[]{:S(2)}) async-start(bf16[128,4,2048]{2,1,0:T(4,128)(2,1)} %select_select_fusion), calls=%async_computation.2 | async-start | bytes 4194304 | tf_op jit(solution)/shard_map/all_to_all | solution.py:44
  412.5 2.4 copy-start.4
  421.6 19.3 %all-to-all-start.3 = ((bf16[128,1,4]{2,1,0:T(2,128)(2,1)}), bf16[128,1,4]{2,1,0:T(2,128)(2,1)S(1)}, u32[]{:S(2)}, u32[]{:S(2)}) async-start(bf16[128,1,4]{2,1,0:T(2,128)(2,1)} %all_to_all.27), calls=%async_computation.3 | async-start | bytes 131072 | tf_op jit(solution)/shard_map/all_to_all | solution.py:69
  473.4 37.9 %all-to-all-start.1 = ((bf16[128,4,2048]{2,1,0:T(4,128)(2,1)}), bf16[128,4,2048]{2,1,0:T(4,128)(2,1)S(1)}, u32[]{:S(2)}, u32[]{:S(2)}) async-start(bf16[128,4,2048]{2,1,0:T(4,128)(2,1)} %reshape.493), calls=%async_computation.1 | async-start | bytes 4194304 | tf_op jit(solution)/shard_map/all_to_all | solution.py:68
  479.6 702.6 %reduce-scatter.4.cloned.1.call-start = ((), (), s32[]{:S(2)}) async-start(), calls=%async_computation.5 | async-start | bytes 1056768
  513.3 2.1 copy-start.2
Sparse Core Ops, SparseCore 0:
  483.7 698.4 reduce-scatter.3
where the time goes:
time: 1190 us
  waiting for transfers between devices  731 us (61%)
  blocking collectives  368 us (31%)
  local copies, waits for them, and re-layouts  31.8 us (3%)
  starting transfers between devices  21.1 us (2%)
  matrix products  17.9 us (2%)
  between operations  14.4 us (1%)
    unnamed x2, waiting for transfers between devices  666 us
    all_gather x1, blocking collectives, local(): all_lists = lax.all_gather(expert_picks, 'expert', axis=0, tiled=True)  349 us
    all_to_all x1, waiting for transfers between devices, local(): lax.all_to_all(send_rows, 'expert', split_axis=0, concat_axis=0, tiled=True)  30.8 us
  transfers between devices with their start and end apart: 4, of which 4 were waited for; matrix products, arithmetic and copies ran while one was open for 1% of the time, Pallas kernels for 0%

commit v1 on v0

v1 whole, which is shorter than its diff:
```python
import jax
import jax.numpy as jnp
from jax import lax
from jax.sharding import PartitionSpec as P

F32 = jnp.float32
BF16 = jnp.bfloat16


def matmul(a, b, dims):
    return lax.dot_general(a, b, (dims, ((), ())), preferred_element_type=F32)


def exchange(x):
    return lax.all_to_all(x, "expert", split_axis=0, concat_axis=0, tiled=True)


def local(tokens, logits, weights, router_weight, expert_picks, cotangent):
    experts = lax.axis_size("expert")
    tok_rows, width = tokens.shape
    capacity = expert_picks.shape[1]
    most = 2 * capacity // experts
    slots = experts * most
    weight, upstream, wanted = weights[0], cotangent[0], expert_picks[0]

    owners = wanted // tok_rows
    rank = jnp.zeros_like(owners)
    for back in range(1, most):
        rank = rank + jnp.pad((owners[back:] == owners[:-back]).astype(jnp.int32), (back, 0))
    placed = owners * most + rank
    place = jnp.arange(slots, dtype=jnp.int32)[:, None] == placed[None, :]
    ids = jnp.sum(jnp.where(place, (wanted % tok_rows)[None, :] + 1, 0), axis=1) - 1
    requested = exchange(ids.reshape(experts, most)).reshape(slots)
    up_slots = matmul(place.astype(BF16), upstream, ((1,), (0,))).astype(BF16)
    raw_grad = matmul(up_slots, weight, ((1,), (1,))).astype(BF16)
    got_raw = exchange(raw_grad.reshape(experts, most, width)).reshape(slots, width)

    probs = jax.nn.softmax(logits, axis=-1)
    chosen = jnp.arange(tok_rows, dtype=jnp.int32)[:, None] == requested[None, :]
    slot_ids = jnp.arange(slots, dtype=jnp.int32)
    of_expert = slot_ids[:, None] // most == jnp.arange(experts, dtype=jnp.int32)[None, :]
    of_expert = of_expert.astype(BF16)
    gates = matmul(probs.astype(BF16), of_expert, ((1,), (1,)))
    gated = jnp.where(chosen, gates, 0.0).astype(BF16)
    send_rows = matmul(gated, tokens, ((0,), (0,))).astype(BF16)
    got_rows = exchange(send_rows.reshape(experts, most, width)).reshape(slots, width)

    products = matmul(tokens, got_raw, ((1,), (1,)))
    picked = jnp.where(chosen, products, 0.0).astype(BF16)
    score_grad = matmul(picked, of_expert, ((1,), (0,)))
    inner_sum = jnp.sum(probs * score_grad, axis=1, keepdims=True)
    logit_grad = (probs * (score_grad - inner_sum)).astype(BF16)
    router_part = matmul(tokens, logit_grad, ((0,), (0,)))
    shares = exchange(router_part.reshape(experts, width // experts, experts))
    token_grad = (
        matmul(gated, got_raw, ((1,), (0,))) + matmul(logit_grad, router_weight, ((1,), (1,)))
    ).astype(BF16)

    weight_grad = matmul(got_rows, up_slots, ((0,), (0,))).astype(BF16)
    router_grad = jnp.sum(shares, axis=0)
    return (token_grad, weight_grad[None], router_grad)


def solution(mesh):
    in_specs = (
        P(("dp", "expert"), None),
        P(("dp", "expert"), None),
        P("expert", None, None),
        P(),
        P(("dp", "expert"), None),
        P(("dp", "expert"), None, None),
    )
    out_specs = (
        P(("dp", "expert"), None),
        P(("dp", "expert"), None, None),
        P(("dp", "expert"), None),
    )
    return jax.shard_map(local, mesh=mesh, in_specs=in_specs, out_specs=out_specs, check_vma=False)
```

time: 1190 us -> 194 us (0.16)
  the two profiles are of different devices: /device:TPU:0 before, /device:TPU:1 now
where the time goes in v1:
time: 194 us; the launch traced here: 191 us
  waiting for transfers between devices  95 us (49%)
  starting transfers between devices  48.9 us (25%)
  matrix products  21.7 us (11%)
  local copies, waits for them, and re-layouts  18.7 us (10%)
  other arithmetic  5.51 us (3%)
    all_to_all x4, waiting for transfers between devices, exchange(): return lax.all_to_all(x, 'expert', split_axis=0, concat_axis=0, tiled=True)  95 us
    all_to_all x4, starting transfers between devices, exchange(): return lax.all_to_all(x, 'expert', split_axis=0, concat_axis=0, tiled=True)  48.9 us
    dot_general x9, matrix products, matmul(): return lax.dot_general(a, b, (dims, ((), ())), preferred_element_type=F32)  21.7 us
    reshape x1, local copies, waits for them, and re-layouts, local(): send_rows.reshape(experts, most, width)  4.12 us
    reshape x1, local copies, waits for them, and re-layouts, local(): exchange(raw_grad.reshape(experts, most, width)).reshape(slots, width)  3.96 us
  transfers between devices with their start and end apart: 4, of which 4 were waited for; matrix products, arithmetic and copies ran while one was open for 20% of the time, Pallas kernels for 0%

profile of v1, /device:TPU:1, one launch (start us, length us, event | category | flops | bytes accessed | tf_op | source)
XLA Modules:
  0.0 190.6 jit_solution(15979821759662185445)
XLA Ops:
  0.6 0.0 copy-start
  0.6 0.7 and_select_fusion.1
  1.4 0.1 slice_compare_fusion.2
  1.5 0.1 slice_compare_fusion.1
  1.5 0.1 slice_compare_fusion
  1.6 0.7 fusion.25
  2.3 0.8 fusion.24
  3.1 0.2 select_reduce_fusion
  3.2 0.7 sub.38
  4.0 16.3 %all-to-all-start = ((s32[128,1,4]{2,1,0:T(1,128)}), s32[128,1,4]{2,1,0:T(1,128)S(1)}, u32[]{:S(2)}, u32[]{:S(2)}) async-start(s32[128,1,4]{2,1,0:T(1,128)} %bitcast.2), calls=%async_computation | async-start | bytes 131072 | tf_op jit(solution)/shard_map/all_to_all | solution.py:15
  20.3 1.5 convolution_convert_fusion.1
  21.8 0.0 copy-start.2
  21.8 1.0 copy-done.2
  22.8 4.6 %fusion.2 = bf16[512,2048]{1,0:T(8,128)(2,1)S(1)} fusion(bf16[512,1024]{1,0:T(8,128)(2,1)S(1)} %convolution_convert_fusion.1, bf16[1,2048,1024]{2,1,0:T(8,128)(2,1)} %param.8), kind=kOutput, calls=%fused_computation.3 | convolution fusion | flops 2148532224 | bytes 7340032 | tf_op jit(solution)/shard_map/dot_general | solution.py:11
  27.3 2.2 %reshape.81 = bf16[128,4,2048]{2,1,0:T(4,128)(2,1)} reshape(bf16[512,2048]{1,0:T(8,128)(2,1)S(1)} %fusion.2) | data formatting | bytes 4194304 | tf_op jit(solution)/shard_map/reshape | solution.py:36
  29.5 0.0 copy-start.4
  29.5 1.4 all-to-all-done
  31.0 11.9 %all-to-all-start.1 = ((bf16[128,4,2048]{2,1,0:T(4,128)(2,1)}), bf16[128,4,2048]{2,1,0:T(4,128)(2,1)S(1)}, u32[]{:S(2)}, u32[]{:S(2)}) async-start(bf16[128,4,2048]{2,1,0:T(4,128)(2,1)} %reshape.81), calls=%async_computation.1 | async-start | bytes 4194304 | tf_op jit(solution)/shard_map/all_to_all | solution.py:15
  42.9 0.0 copy-done.4
  42.9 0.1 copy.17
  43.0 0.1 reduce_max.9
  43.1 0.5 broadcast.92
  43.6 0.8 reduce.3
  44.5 0.1 eq.65
  44.6 0.3 fusion.7
  44.9 0.0 copy-done
  44.9 2.1 %convolution_convert_fusion = bf16[512,2048]{1,0:T(8,128)(2,1)} fusion(bf16[128,512]{1,0:T(8,128)(2,1)S(1)} %fusion.7, bf16[128,2048]{1,0:T(8,128)(2,1)S(1)} %copy-done), kind=kOutput, calls=%fused_computation.4 | convolution fusion | flops 269484032 | bytes 2752512 | tf_op jit(solution)/shard_map/dot_general | solution.py:11
  47.0 4.1 %reshape.83 = bf16[128,4,2048]{2,1,0:T(4,128)(2,1)} reshape(bf16[512,2048]{1,0:T(8,128)(2,1)} %convolution_convert_fusion) | data formatting | bytes 4194304 | tf_op jit(solution)/shard_map/reshape | solution.py:46
  51.1 40.6 %all-to-all-done.1 = bf16[128,4,2048]{2,1,0:T(4,128)(2,1)S(1)} async-done(((bf16[128,4,2048]{2,1,0:T(4,128)(2,1)}), bf16[128,4,2048]{2,1,0:T(4,128)(2,1)S(1)}, u32[]{:S(2)}, u32[]{:S(2)}) %all-to-all-start.1) | async-done | bytes 2097184 | tf_op jit(solution)/shard_map/all_to_all | solution.py:15
  91.7 0.0 copy-start.1
  91.7 1.3 copy-done.1
  93.0 9.9 %all-to-all-start.2 = ((bf16[128,4,2048]{2,1,0:T(4,128)(2,1)}), bf16[128,4,2048]{2,1,0:T(4,128)(2,1)S(1)}, u32[]{:S(2)}, u32[]{:S(2)}) async-start(bf16[128,4,2048]{2,1,0:T(4,128)(2,1)} %reshape.83), calls=%async_computation.2 | async-start | bytes 4194304 | tf_op jit(solution)/shard_map/all_to_all | solution.py:15
  103.0 4.0 %reshape.82 = bf16[512,2048]{1,0:T(8,128)(2,1)} reshape(bf16[128,4,2048]{2,1,0:T(4,128)(2,1)} %copy-done.1) | data formatting | bytes 4194304 | tf_op jit(solution)/shard_map/reshape | solution.py:36
  106.9 2.6 %multiply_reduce_fusion = (f32[128]{0:T(128)S(1)}, f32[128,128]{0,1:T(8,128)S(1)}) fusion(f32[128]{0:T(128)S(1)} %fusion.17, f32[128,128]{0,1:T(8,128)S(1)} %copy.17, f32[128]{0:T(128)S(1)} %reduce_max.9, s32[512]{0:T(512)S(1)} %add_select_fusion, bf16[512,2048]{1,0:T(8,128)(2,1)} %reshape.82, bf16[128,2048]{1,0:T(8,128)(2,1)S(1)} %copy-done, s32[512]{0:T(512)S(1)} %eq.65), kind=kOutput, calls=%fused_computation.26 | convolution fusion | flops 285540224 | bytes 2758144 | tf_op jit(solution)/shard_map/dot_general | solution.py:11
  109.5 1.3 convolution_bitcast_fusion
  110.8 2.6 %copy.19 = f32[2048,128]{1,0:T(8,128)} copy(f32[2048,128]{0,1:T(8,128)} %convolution_bitcast_fusion) | data formatting | bytes 2097152 | tf_op jit(solution)/shard_map/dot_general | solution.py:11
  113.4 38.0 %all-to-all-done.2 = bf16[128,4,2048]{2,1,0:T(4,128)(2,1)S(1)} async-done(((bf16[128,4,2048]{2,1,0:T(4,128)(2,1)}), bf16[128,4,2048]{2,1,0:T(4,128)(2,1)S(1)}, u32[]{:S(2)}, u32[]{:S(2)}) %all-to-all-start.2) | async-done | bytes 2097184 | tf_op jit(solution)/shard_map/all_to_all | solution.py:15
  151.4 10.7 %all-to-all-start.3 = ((f32[128,16,128]{2,1,0:T(8,128)}), f32[128,16,128]{2,1,0:T(8,128)}, u32[]{:S(2)}, u32[]{:S(2)}) async-start(f32[128,16,128]{2,1,0:T(8,128)} %bitcast.39), calls=%async_computation.3 | async-start | bytes 2097152 | tf_op jit(solution)/shard_map/all_to_all | solution.py:15
  162.1 0.0 copy-start.3
  162.1 2.1 %fusion.29 = f32[128,2048]{1,0:T(8,128)S(1)} fusion(bf16[128,512]{1,0:T(8,128)(2,1)S(1)} %fusion.7, bf16[512,2048]{1,0:T(8,128)(2,1)} %reshape.82), kind=kOutput, calls=%fused_computation.58 | convolution fusion | flops 268435456 | bytes 3276800 | tf_op jit(solution)/shard_map/dot_general | solution.py:11
  164.2 0.0 copy-done.3
  164.2 1.1 fusion.5
  165.3 2.1 %reshape.84 = bf16[512,2048]{1,0:T(8,128)(2,1)} reshape(bf16[128,4,2048]{2,1,0:T(4,128)(2,1)S(1)} %all-to-all-done.2) | data formatting | bytes 4194304 | tf_op jit(solution)/shard_map/reshape | solution.py:46
  167.4 6.2 %convert_bitcast_fusion = bf16[1,2048,1024]{2,1,0:T(8,128)(2,1)} fusion(bf16[512,2048]{1,0:T(8,128)(2,1)} %reshape.84, bf16[512,1024]{1,0:T(8,128)(2,1)} %copy-done.2), kind=kOutput, calls=%fused_computation.2 | convolution fusion | flops 2149580800 | bytes 7340032 | tf_op jit(solution)/shard_map/dot_general | solution.py:11
  173.6 15.0 %all-to-all-done.3 = f32[128,16,128]{2,1,0:T(8,128)} async-done(((f32[128,16,128]{2,1,0:T(8,128)}), f32[128,16,128]{2,1,0:T(8,128)}, u32[]{:S(2)}, u32[]{:S(2)}) %all-to-all-start.3) | async-done | bytes 1048608 | tf_op jit(solution)/shard_map/all_to_all | solution.py:15
  188.7 2.0 %reduce_sum.39 = f32[16,128]{1,0:T(8,128)} reduce(f32[128,16,128]{2,1,0:T(8,128)} %all-to-all-done.3, f32[]{:T(128)} %constant.53.clone.1), dimensions={0}, to_apply=%region_4.5 | reduce | flops 260096 | bytes 1056772 | tf_op jit(solution)/shard_map/reduce_sum | solution.py:60
  (4 shorter events, 0.1 us)
Async XLA Ops:
  0.6 44.2 %copy-start = (bf16[128,2048]{1,0:T(8,128)(2,1)S(1)}, bf16[128,2048]{1,0:T(8,128)(2,1)}, u32[]{:S(2)}) copy-start(bf16[128,2048]{1,0:T(8,128)(2,1)} %param.6) | copy-start | bytes 1572868
  4.0 27.0 %all-to-all-start = ((s32[128,1,4]{2,1,0:T(1,128)}), s32[128,1,4]{2,1,0:T(1,128)S(1)}, u32[]{:S(2)}, u32[]{:S(2)}) async-start(s32[128,1,4]{2,1,0:T(1,128)} %bitcast.2), calls=%async_computation | async-start | bytes 131072 | tf_op jit(solution)/shard_map/all_to_all | solution.py:15
  21.8 1.0 copy-start.2
  29.5 13.3 %copy-start.4 = (f32[128,128]{1,0:T(8,128)S(1)}, f32[128,128]{1,0:T(8,128)}, u32[]{:S(2)}) copy-start(f32[128,128]{1,0:T(8,128)} %param.7) | copy-start | bytes 196612
  31.0 60.7 %all-to-all-start.1 = ((bf16[128,4,2048]{2,1,0:T(4,128)(2,1)}), bf16[128,4,2048]{2,1,0:T(4,128)(2,1)S(1)}, u32[]{:S(2)}, u32[]{:S(2)}) async-start(bf16[128,4,2048]{2,1,0:T(4,128)(2,1)} %reshape.81), calls=%async_computation.1 | async-start | bytes 4194304 | tf_op jit(solution)/shard_map/all_to_all | solution.py:15
  91.7 1.3 copy-start.1
  93.0 58.3 %all-to-all-start.2 = ((bf16[128,4,2048]{2,1,0:T(4,128)(2,1)}), bf16[128,4,2048]{2,1,0:T(4,128)(2,1)S(1)}, u32[]{:S(2)}, u32[]{:S(2)}) async-start(bf16[128,4,2048]{2,1,0:T(4,128)(2,1)} %reshape.83), calls=%async_computation.2 | async-start | bytes 4194304 | tf_op jit(solution)/shard_map/all_to_all | solution.py:15
  151.4 37.3 %all-to-all-start.3 = ((f32[128,16,128]{2,1,0:T(8,128)}), f32[128,16,128]{2,1,0:T(8,128)}, u32[]{:S(2)}, u32[]{:S(2)}) async-start(f32[128,16,128]{2,1,0:T(8,128)} %bitcast.39), calls=%async_computation.3 | async-start | bytes 2097152 | tf_op jit(solution)/shard_map/all_to_all | solution.py:15
  162.1 2.1 %copy-start.3 = (bf16[2048,128]{1,0:T(8,128)(2,1)S(1)}, bf16[2048,128]{1,0:T(8,128)(2,1)}, u32[]{:S(2)}) copy-start(bf16[2048,128]{1,0:T(8,128)(2,1)} %param.9) | copy-start | bytes 1572868

commit v2 on v1

--- a/solution.py
+++ b/solution.py
@@ -5,6 +5,8 @@
 
 F32 = jnp.float32
 BF16 = jnp.bfloat16
+LANES = 128
+SIDES = (8, 4, 4)
 
 
 def matmul(a, b, dims):
@@ -13,6 +15,32 @@
 
 def exchange(x):
     return lax.all_to_all(x, "expert", split_axis=0, concat_axis=0, tiled=True)
+
+
+def sum_shares(parts):
+    index = lax.axis_index("expert")
+    count = lax.axis_size("expert")
+    for side in (2, 1, 0):
+        size = SIDES[side]
+        stride = 1
+        for later in SIDES[side + 1 :]:
+            stride *= later
+        here = index // stride % size
+
+        def pick(step):
+            return lax.dynamic_index_in_dim(parts, (here + step) % size, side, keepdims=False)
+
+        def moved(i, step):
+            at = i // stride % size
+            return i + ((at + step) % size - at) * stride
+
+        total = pick(0)
+        for step in range(1, size):
+            total = total + lax.ppermute(
+                pick(step), "expert", [(i, moved(i, step)) for i in range(count)]
+            )
+        parts = total
+    return parts
 
 
 def local(tokens, logits, weights, router_weight, expert_picks, cotangent):
@@ -29,11 +57,13 @@
         rank = rank + jnp.pad((owners[back:] == owners[:-back]).astype(jnp.int32), (back, 0))
     placed = owners * most + rank
     place = jnp.arange(slots, dtype=jnp.int32)[:, None] == placed[None, :]
-    ids = jnp.sum(jnp.where(place, (wanted % tok_rows)[None, :] + 1, 0), axis=1) - 1
-    requested = exchange(ids.reshape(experts, most)).reshape(slots)
+    ids = jnp.sum(jnp.where(place, (wanted % tok_rows)[None, :] + 1, 0), axis=1)
     up_slots = matmul(place.astype(BF16), upstream, ((1,), (0,))).astype(BF16)
     raw_grad = matmul(up_slots, weight, ((1,), (1,))).astype(BF16)
-    got_raw = exchange(raw_grad.reshape(experts, most, width)).reshape(slots, width)
+    marks = jnp.broadcast_to(ids.astype(BF16).reshape(experts, most, 1), (experts, most, LANES))
+    got = exchange(jnp.concatenate([raw_grad.reshape(experts, most, width), marks], axis=2))
+    got_raw = got[:, :, :width].reshape(slots, width)
+    requested = got[:, :, width].astype(jnp.int32).reshape(slots) - 1
 
     probs = jax.nn.softmax(logits, axis=-1)
     chosen = jnp.arange(tok_rows, dtype=jnp.int32)[:, None] == requested[None, :]
@@ -51,13 +81,12 @@
     inner_sum = jnp.sum(probs * score_grad, axis=1, keepdims=True)
     logit_grad = (probs * (score_grad - inner_sum)).astype(BF16)
     router_part = matmul(tokens, logit_grad, ((0,), (0,)))
-    shares = exchange(router_part.reshape(experts, width // experts, experts))
+    router_grad = sum_shares(router_part.reshape(*SIDES, width // experts, experts))
     token_grad = (
         matmul(gated, got_raw, ((1,), (0,))) + matmul(logit_grad, router_weight, ((1,), (1,)))
     ).astype(BF16)
 
     weight_grad = matmul(got_rows, up_slots, ((0,), (0,))).astype(BF16)
-    router_grad = jnp.sum(shares, axis=0)
     return (token_grad, weight_grad[None], router_grad)
 
 

time: 194 us -> 184 us (0.948)
  the two profiles are of different devices: /device:TPU:1 before, /device:TPU:32 now
where the time goes in v2:
time: 184 us; the launch traced here: 183 us
  waiting for transfers between devices  84 us (46%)
  starting transfers between devices  47.4 us (26%)
  local copies, waits for them, and re-layouts  21.2 us (12%)
  matrix products  19.2 us (10%)
  other arithmetic  10.2 us (6%)
    all_to_all x2, waiting for transfers between devices, exchange(): return lax.all_to_all(x, 'expert', split_axis=0, concat_axis=0, tiled=True)  55.9 us
    ppermute x13, waiting for transfers between devices, sum_shares(): lax.ppermute(pick(step), 'expert', [(i, moved(i, step)) for i in range(co...  28.1 us
    ppermute x13, starting transfers between devices, sum_shares(): lax.ppermute(pick(step), 'expert', [(i, moved(i, step)) for i in range(co...  25.3 us
    all_to_all x2, starting transfers between devices, exchange(): return lax.all_to_all(x, 'expert', split_axis=0, concat_axis=0, tiled=True)  22.1 us
    dot_general x9, matrix products, matmul(): return lax.dot_general(a, b, (dims, ((), ())), preferred_element_type=F32)  19.2 us
    reshape x1, local copies, waits for them, and re-layouts, local(): send_rows.reshape(experts, most, width)  4.11 us
  transfers between devices with their start and end apart: 15, of which 8 were waited for; matrix products, arithmetic and copies ran while one was open for 9% of the time, Pallas kernels for 0%

profile of v2, /device:TPU:32, one launch (start us, length us, event | category | flops | bytes accessed | tf_op | source)
XLA Modules:
  0.0 182.9 jit_solution(1265790919000988756)
XLA Ops:
  0.6 0.7 and_select_fusion.1
  1.6 0.7 fusion.35
  2.3 0.8 fusion.34
  3.4 1.5 convolution_convert_fusion.1
  4.9 1.0 copy-done.1
  5.8 5.9 %fusion.2 = bf16[512,2048]{1,0:T(8,128)(2,1)} fusion(bf16[512,1024]{1,0:T(8,128)(2,1)S(1)} %convolution_convert_fusion.1, bf16[1,2048,1024]{2,1,0:T(8,128)(2,1)} %param.8), kind=kOutput, calls=%fused_computation.3 | convolution fusion | flops 2148532224 | bytes 7340032 | tf_op jit(solution)/shard_map/dot_general | solution.py:13
  11.7 2.7 %reshape.81 = bf16[128,4,2048]{2,1,0:T(4,128)(2,1)S(1)} reshape(bf16[512,2048]{1,0:T(8,128)(2,1)} %fusion.2) | data formatting | bytes 4194304 | tf_op jit(solution)/shard_map/reshape | solution.py:64
  14.6 2.5 %pad_maximum_fusion = bf16[128,4,2176]{2,1,0:T(4,128)(2,1)} fusion(bf16[128,4,128]{2,1,0:T(4,128)(2,1)S(1)} %broadcast_in_dim.40, bf16[128,4,2048]{2,1,0:T(4,128)(2,1)S(1)} %reshape.81), kind=kLoop, calls=%fused_computation.8 | loop fusion | flops 4456448 | bytes 4456448 | tf_op jit(solution)/shard_map/concatenate | solution.py:64
  17.1 15.1 %all-to-all-start = ((bf16[128,4,2176]{2,1,0:T(4,128)(2,1)}), bf16[128,4,2176]{2,1,0:T(4,128)(2,1)S(1)}, u32[]{:S(2)}, u32[]{:S(2)}) async-start(bf16[128,4,2176]{2,1,0:T(4,128)(2,1)} %pad_maximum_fusion), calls=%async_computation | async-start | bytes 4456448 | tf_op jit(solution)/shard_map/all_to_all | solution.py:17
  32.6 55.9 %all-to-all-done = bf16[128,4,2176]{2,1,0:T(4,128)(2,1)S(1)} async-done(((bf16[128,4,2176]{2,1,0:T(4,128)(2,1)}), bf16[128,4,2176]{2,1,0:T(4,128)(2,1)S(1)}, u32[]{:S(2)}, u32[]{:S(2)}) %all-to-all-start) | async-done | bytes 2228256 | tf_op jit(solution)/shard_map/all_to_all | solution.py:17
  88.4 2.2 %add_reduce_fusion = s32[128,4]{1,0:T(8,128)S(1)} fusion(bf16[128,4,2176]{2,1,0:T(4,128)(2,1)S(1)} %all-to-all-done), kind=kLoop, calls=%fused_computation.26 | loop fusion | flops 1024 | bytes 3072 | tf_op jit(solution)/shard_map/sub | solution.py:66
  90.8 0.3 fusion.7
  91.1 2.1 %convolution_convert_fusion = bf16[512,2048]{1,0:T(8,128)(2,1)} fusion(bf16[128,512]{1,0:T(8,128)(2,1)S(1)} %fusion.7, bf16[128,2048]{1,0:T(8,128)(2,1)S(1)} %copy-done), kind=kOutput, calls=%fused_computation.4 | convolution fusion | flops 269484032 | bytes 2752512 | tf_op jit(solution)/shard_map/dot_general | solution.py:13
  93.2 4.1 %reshape.83 = bf16[128,4,2048]{2,1,0:T(4,128)(2,1)} reshape(bf16[512,2048]{1,0:T(8,128)(2,1)} %convolution_convert_fusion) | data formatting | bytes 4194304 | tf_op jit(solution)/shard_map/reshape | solution.py:76
  97.3 7.0 %all-to-all-start.1 = ((bf16[128,4,2048]{2,1,0:T(4,128)(2,1)}), bf16[128,4,2048]{2,1,0:T(4,128)(2,1)}, u32[]{:S(2)}, u32[]{:S(2)}) async-start(bf16[128,4,2048]{2,1,0:T(4,128)(2,1)} %reshape.83), calls=%async_computation.1 | async-start | bytes 4194304 | tf_op jit(solution)/shard_map/all_to_all | solution.py:17
  104.3 2.5 %slice.33 = bf16[128,4,2048]{2,1,0:T(4,128)(2,1)} slice(bf16[128,4,2176]{2,1,0:T(4,128)(2,1)S(1)} %all-to-all-done), slice={[0:128], [0:4], [0:2048]} | slice | bytes 4194304 | tf_op jit(solution)/shard_map/slice | solution.py:65
  106.8 2.5 %reshape.82 = bf16[512,2048]{1,0:T(8,128)(2,1)S(1)} reshape(bf16[128,4,2048]{2,1,0:T(4,128)(2,1)} %slice.33) | data formatting | bytes 4194304 | tf_op jit(solution)/shard_map/reshape | solution.py:65
  109.4 1.0 multiply_reduce_fusion
  110.4 1.3 convolution_bitcast_fusion
  111.7 2.5 %copy.22 = f32[2048,128]{1,0:T(8,128)} copy(f32[2048,128]{0,1:T(8,128)} %convolution_bitcast_fusion) | data formatting | bytes 2097152 | tf_op jit(solution)/shard_map/dot_general | solution.py:13
  114.2 2.0 %dynamic-slice_bitcast_fusion.2 = (f32[8,4,16,128]{3,2,1,0:T(8,128)}, f32[8,4,16,128]{3,2,1,0:T(8,128)}, f32[8,4,16,128]{3,2,1,0:T(8,128)S(1)}) fusion(f32[8,4,4,16,128]{4,3,2,1,0:T(8,128)} %bitcast.90, s32[]{:T(128)S(6)} %select_n.183, s32[]{:T(128)S(6)} %select_n.187, s32[]{:T(128)S(6)} %select_n.185), kind=kLoop, calls=%fused_computation.24 | loop fusion | bytes 1572876 | tf_op jit(solution)/shard_map/jit(dynamic_index_in_dim)/squeeze | solution.py:31
  116.2 1.5 collective-permute-start
  117.7 1.8 collective-permute-start.2
  119.5 1.8 collective-permute-start.1
  121.2 9.8 %collective-permute-done = f32[8,4,16,128]{3,2,1,0:T(8,128)S(1)} collective-permute-done((f32[8,4,16,128]{3,2,1,0:T(8,128)}, f32[8,4,16,128]{3,2,1,0:T(8,128)S(1)}, u32[]{:S(2)}, u32[]{:S(2)}) %collective-permute-start) | collective-permute-done | bytes 262176 | tf_op jit(solution)/shard_map/ppermute | solution.py:39
  131.0 0.3 collective-permute-done.2
  131.4 9.2 %collective-permute-done.1 = f32[8,4,16,128]{3,2,1,0:T(8,128)} collective-permute-done((f32[8,4,16,128]{3,2,1,0:T(8,128)S(1)}, f32[8,4,16,128]{3,2,1,0:T(8,128)}, u32[]{:S(2)}, u32[]{:S(2)}) %collective-permute-start.1) | collective-permute-done | bytes 262176 | tf_op jit(solution)/shard_map/ppermute | solution.py:39
  140.6 1.2 fusion.12
  141.7 0.7 dynamic-slice_bitcast_fusion.5
  142.4 1.5 collective-permute-start.3
  143.9 1.8 collective-permute-start.5
  145.7 1.1 collective-permute-start.4
  146.8 2.3 %collective-permute-done.3 = f32[8,16,128]{2,1,0:T(8,128)} collective-permute-done((f32[8,16,128]{2,1,0:T(8,128)}, f32[8,16,128]{2,1,0:T(8,128)}, u32[]{:S(2)}, u32[]{:S(2)}) %collective-permute-start.3) | collective-permute-done | bytes 65568 | tf_op jit(solution)/shard_map/ppermute | solution.py:39
  149.1 2.8 %collective-permute-done.4 = f32[8,16,128]{2,1,0:T(8,128)} collective-permute-done((f32[8,16,128]{2,1,0:T(8,128)}, f32[8,16,128]{2,1,0:T(8,128)}, u32[]{:S(2)}, u32[]{:S(2)}) %collective-permute-start.4) | collective-permute-done | bytes 65568 | tf_op jit(solution)/shard_map/ppermute | solution.py:39
  152.0 0.9 fusion.19
  152.9 1.0 collective-permute-start.6
  153.9 1.1 collective-permute-start.12
  155.0 0.4 fusion.39
  155.5 3.7 %collective-permute-start.11 = (f32[16,128]{1,0:T(8,128)S(1)}, f32[16,128]{1,0:T(8,128)S(1)}, u32[]{:S(2)}, u32[]{:S(2)}) collective-permute-start(f32[16,128]{1,0:T(8,128)S(1)} %get-tuple-element.11), channel_id=1, source_target_pairs={{0,192},{2,194},{4,196},{6,198},{8,200},{10,202},{12,204},{14,206}... | collective-permute-start | bytes 24584 | tf_op jit(solution)/shard_map/ppermute | solution.py:39
  159.2 4.7 %collective-permute-start.10 = (f32[16,128]{1,0:T(8,128)S(1)}, f32[16,128]{1,0:T(8,128)S(1)}, u32[]{:S(2)}, u32[]{:S(2)}) collective-permute-start(f32[16,128]{1,0:T(8,128)S(1)} %get-tuple-element.12), channel_id=1, source_target_pairs={{0,160},{2,162},{4,164},{6,166},{8,168},{10,170},{12,172},{14,174}... | collective-permute-start | bytes 24584 | tf_op jit(solution)/shard_map/ppermute | solution.py:39
  163.8 4.5 %collective-permute-start.8 = (f32[16,128]{1,0:T(8,128)S(1)}, f32[16,128]{1,0:T(8,128)S(1)}, u32[]{:S(2)}, u32[]{:S(2)}) collective-permute-start(f32[16,128]{1,0:T(8,128)S(1)} %get-tuple-element.14), channel_id=1, source_target_pairs={{0,96},{2,98},{4,100},{6,102},{8,104},{10,106},{12,108},{14,110},{... | collective-permute-start | bytes 24584 | tf_op jit(solution)/shard_map/ppermute | solution.py:39
  168.3 1.0 collective-permute-start.7
  169.3 1.1 fusion.5
  170.5 0.9 collective-permute-done.9
  171.4 2.7 %collective-permute-done.7 = f32[16,128]{1,0:T(8,128)S(1)} collective-permute-done((f32[16,128]{1,0:T(8,128)S(1)}, f32[16,128]{1,0:T(8,128)S(1)}, u32[]{:S(2)}, u32[]{:S(2)}) %collective-permute-start.7) | collective-permute-done | bytes 8224 | tf_op jit(solution)/shard_map/ppermute | solution.py:39
  174.1 0.6 fusion.28
  174.7 2.5 %reshape.84 = bf16[512,2048]{1,0:T(8,128)(2,1)S(1)} reshape(bf16[128,4,2048]{2,1,0:T(4,128)(2,1)} %all-to-all-done.1) | data formatting | bytes 4194304 | tf_op jit(solution)/shard_map/reshape | solution.py:76
  177.2 5.6 %convert_bitcast_fusion = bf16[1,2048,1024]{2,1,0:T(8,128)(2,1)} fusion(bf16[512,2048]{1,0:T(8,128)(2,1)S(1)} %reshape.84, bf16[512,1024]{1,0:T(8,128)(2,1)} %copy-done.1), kind=kOutput, calls=%fused_computation.2 | convolution fusion | flops 2149580800 | bytes 7340032 | tf_op jit(solution)/shard_map/dot_general | solution.py:13
  (33 shorter events, 1.2 us)
Async XLA Ops:
  0.6 90.5 %copy-start = (bf16[128,2048]{1,0:T(8,128)(2,1)S(1)}, bf16[128,2048]{1,0:T(8,128)(2,1)}, u32[]{:S(2)}) copy-start(bf16[128,2048]{1,0:T(8,128)(2,1)} %param.6) | copy-start | bytes 1572868
  4.8 1.0 copy-start.1
  17.1 15.2 %copy-start.5 = (f32[128,128]{1,0:T(8,128)S(1)}, f32[128,128]{1,0:T(8,128)}, u32[]{:S(2)}) copy-start(f32[128,128]{1,0:T(8,128)} %param.7) | copy-start | bytes 196612
  17.1 71.3 %all-to-all-start = ((bf16[128,4,2176]{2,1,0:T(4,128)(2,1)}), bf16[128,4,2176]{2,1,0:T(4,128)(2,1)S(1)}, u32[]{:S(2)}, u32[]{:S(2)}) async-start(bf16[128,4,2176]{2,1,0:T(4,128)(2,1)} %pad_maximum_fusion), calls=%async_computation | async-start | bytes 4456448 | tf_op jit(solution)/shard_map/all_to_all | solution.py:17
  97.3 77.4 %all-to-all-start.1 = ((bf16[128,4,2048]{2,1,0:T(4,128)(2,1)}), bf16[128,4,2048]{2,1,0:T(4,128)(2,1)}, u32[]{:S(2)}, u32[]{:S(2)}) async-start(bf16[128,4,2048]{2,1,0:T(4,128)(2,1)} %reshape.83), calls=%async_computation.1 | async-start | bytes 4194304 | tf_op jit(solution)/shard_map/all_to_all | solution.py:17
  110.4 5.8 %copy-start.3 = (bf16[128,128]{0,1:T(8,128)(2,1)}, bf16[128,128]{0,1:T(8,128)(2,1)S(1)}, u32[]{:S(2)}) copy-start(bf16[128,128]{0,1:T(8,128)(2,1)S(1)} %multiply_convert_fusion) | copy-start | bytes 98308
  116.2 14.8 %collective-permute-start = (f32[8,4,16,128]{3,2,1,0:T(8,128)}, f32[8,4,16,128]{3,2,1,0:T(8,128)S(1)}, u32[]{:S(2)}, u32[]{:S(2)}) collective-permute-start(f32[8,4,16,128]{3,2,1,0:T(8,128)} %get-tuple-element.3), channel_id=1, source_target_pairs={{0,2},{2,4},{4,6},{6,0},{8,10},{10,12},{12,14},{14,8},{16,18},{18,... | collective-permute-start | bytes 786440 | tf_op jit(solution)/shard_map/ppermute | solution.py:39
  117.7 13.7 %collective-permute-start.2 = (f32[8,4,16,128]{3,2,1,0:T(8,128)}, f32[8,4,16,128]{3,2,1,0:T(8,128)}, u32[]{:S(2)}, u32[]{:S(2)}) collective-permute-start(f32[8,4,16,128]{3,2,1,0:T(8,128)} %get-tuple-element.4), channel_id=1, source_target_pairs={{0,6},{2,0},{4,2},{6,4},{8,14},{10,8},{12,10},{14,12},{16,22},{18,... | collective-permute-start | bytes 786440 | tf_op jit(solution)/shard_map/ppermute | solution.py:39
  119.5 21.1 %collective-permute-start.1 = (f32[8,4,16,128]{3,2,1,0:T(8,128)S(1)}, f32[8,4,16,128]{3,2,1,0:T(8,128)}, u32[]{:S(2)}, u32[]{:S(2)}) collective-permute-start(f32[8,4,16,128]{3,2,1,0:T(8,128)S(1)} %get-tuple-element.5), channel_id=1, source_target_pairs={{0,4},{2,6},{4,0},{6,2},{8,12},{10,14},{12,8},{14,10},{16,20},{18,... | collective-permute-start | bytes 786440 | tf_op jit(solution)/shard_map/ppermute | solution.py:39
  142.4 26.9 %copy-start.2 = (bf16[2048,128]{1,0:T(8,128)(2,1)S(1)}, bf16[2048,128]{1,0:T(8,128)(2,1)}, u32[]{:S(2)}) copy-start(bf16[2048,128]{1,0:T(8,128)(2,1)} %param.9) | copy-start | bytes 1572868
  142.4 6.7 %collective-permute-start.3 = (f32[8,16,128]{2,1,0:T(8,128)}, f32[8,16,128]{2,1,0:T(8,128)}, u32[]{:S(2)}, u32[]{:S(2)}) collective-permute-start(f32[8,16,128]{2,1,0:T(8,128)} %get-tuple-element.6), channel_id=1, source_target_pairs={{0,8},{2,10},{4,12},{6,14},{8,16},{10,18},{12,20},{14,22},{16,24},... | collective-permute-start | bytes 196616 | tf_op jit(solution)/shard_map/ppermute | solution.py:39
  143.9 5.2 %collective-permute-start.5 = (f32[8,16,128]{2,1,0:T(8,128)}, f32[8,16,128]{2,1,0:T(8,128)}, u32[]{:S(2)}, u32[]{:S(2)}) collective-permute-start(f32[8,16,128]{2,1,0:T(8,128)} %get-tuple-element.7), channel_id=1, source_target_pairs={{0,24},{2,26},{4,28},{6,30},{8,0},{10,2},{12,4},{14,6},{16,8},{18,... | collective-permute-start | bytes 196616 | tf_op jit(solution)/shard_map/ppermute | solution.py:39
  145.7 6.3 %collective-permute-start.4 = (f32[8,16,128]{2,1,0:T(8,128)}, f32[8,16,128]{2,1,0:T(8,128)}, u32[]{:S(2)}, u32[]{:S(2)}) collective-permute-start(f32[8,16,128]{2,1,0:T(8,128)} %get-tuple-element.8), channel_id=1, source_target_pairs={{0,16},{2,18},{4,20},{6,22},{8,24},{10,26},{12,28},{14,30},{16,0},... | collective-permute-start | bytes 196616 | tf_op jit(solution)/shard_map/ppermute | solution.py:39
  146.8 22.5 %copy-start.4 = (bf16[128,128]{0,1:T(8,128)(2,1)S(1)}, bf16[128,128]{0,1:T(8,128)(2,1)}, u32[]{:S(2)}) copy-start(bf16[128,128]{0,1:T(8,128)(2,1)} %copy-done.3) | copy-start | bytes 98308
  152.9 10.9 %collective-permute-start.6 = (f32[16,128]{1,0:T(8,128)S(1)}, f32[16,128]{1,0:T(8,128)S(1)}, u32[]{:S(2)}, u32[]{:S(2)}) collective-permute-start(f32[16,128]{1,0:T(8,128)S(1)} %get-tuple-element.9), channel_id=1, source_target_pairs={{0,32},{2,34},{4,36},{6,38},{8,40},{10,42},{12,44},{14,46},{16,48}... | collective-permute-start | bytes 24584 | tf_op jit(solution)/shard_map/ppermute | solution.py:39
  153.9 14.4 %collective-permute-start.12 = (f32[16,128]{1,0:T(8,128)S(1)}, f32[16,128]{1,0:T(8,128)S(1)}, u32[]{:S(2)}, u32[]{:S(2)}) collective-permute-start(f32[16,128]{1,0:T(8,128)S(1)} %get-tuple-element.10), channel_id=1, source_target_pairs={{0,224},{2,226},{4,228},{6,230},{8,232},{10,234},{12,236},{14,238}... | collective-permute-start | bytes 24584 | tf_op jit(solution)/shard_map/ppermute | solution.py:39
  155.5 15.0 %collective-permute-start.11 = (f32[16,128]{1,0:T(8,128)S(1)}, f32[16,128]{1,0:T(8,128)S(1)}, u32[]{:S(2)}, u32[]{:S(2)}) collective-permute-start(f32[16,128]{1,0:T(8,128)S(1)} %get-tuple-element.11), channel_id=1, source_target_pairs={{0,192},{2,194},{4,196},{6,198},{8,200},{10,202},{12,204},{14,206}... | collective-permute-start | bytes 24584 | tf_op jit(solution)/shard_map/ppermute | solution.py:39
  159.2 11.3 %collective-permute-start.10 = (f32[16,128]{1,0:T(8,128)S(1)}, f32[16,128]{1,0:T(8,128)S(1)}, u32[]{:S(2)}, u32[]{:S(2)}) collective-permute-start(f32[16,128]{1,0:T(8,128)S(1)} %get-tuple-element.12), channel_id=1, source_target_pairs={{0,160},{2,162},{4,164},{6,166},{8,168},{10,170},{12,172},{14,174}... | collective-permute-start | bytes 24584 | tf_op jit(solution)/shard_map/ppermute | solution.py:39
  163.8 7.6 %collective-permute-start.9 = (f32[16,128]{1,0:T(8,128)S(1)}, f32[16,128]{1,0:T(8,128)S(1)}, u32[]{:S(2)}, u32[]{:S(2)}) collective-permute-start(f32[16,128]{1,0:T(8,128)S(1)} %get-tuple-element.13), channel_id=1, source_target_pairs={{0,128},{2,130},{4,132},{6,134},{8,136},{10,138},{12,140},{14,142}... | collective-permute-start | bytes 24584 | tf_op jit(solution)/shard_map/ppermute | solution.py:39
  163.8 7.6 %collective-permute-start.8 = (f32[16,128]{1,0:T(8,128)S(1)}, f32[16,128]{1,0:T(8,128)S(1)}, u32[]{:S(2)}, u32[]{:S(2)}) collective-permute-start(f32[16,128]{1,0:T(8,128)S(1)} %get-tuple-element.14), channel_id=1, source_target_pairs={{0,96},{2,98},{4,100},{6,102},{8,104},{10,106},{12,108},{14,110},{... | collective-permute-start | bytes 24584 | tf_op jit(solution)/shard_map/ppermute | solution.py:39
  168.3 5.8 %collective-permute-start.7 = (f32[16,128]{1,0:T(8,128)S(1)}, f32[16,128]{1,0:T(8,128)S(1)}, u32[]{:S(2)}, u32[]{:S(2)}) collective-permute-start(f32[16,128]{1,0:T(8,128)S(1)} %get-tuple-element.15), channel_id=1, source_target_pairs={{0,64},{2,66},{4,68},{6,70},{8,72},{10,74},{12,76},{14,78},{16,80}... | collective-permute-start | bytes 24584 | tf_op jit(solution)/shard_map/ppermute | solution.py:39

commit v3 on v1

v3 whole, which is shorter than its diff:
```python
import functools

import jax
import jax.numpy as jnp
from jax import lax
from jax.experimental import pallas as pl
from jax.experimental.pallas import tpu as pltpu
from jax.sharding import PartitionSpec as P

F32 = jnp.float32
BF16 = jnp.bfloat16
I32 = jnp.int32
LANES = 128
HALVES = 2
STEP = 256

NN = ((1,), (0,))
NT = ((1,), (1,))
TN = ((0,), (0,))


def matmul(a, b, dims):
    return lax.dot_general(a, b, (dims, ((), ())), preferred_element_type=F32)


def iota(shape, dim):
    return lax.broadcasted_iota(I32, shape, dim)


def params():
    return pltpu.CompilerParams(vmem_limit_bytes=40 * 1024 * 1024)


def slots_of(wanted, tok_rows, most):
    cap = wanted.shape[1]
    owners = jnp.broadcast_to(wanted // tok_rows, (8, cap))
    lane = iota((8, cap), 1)
    rank = jnp.zeros((8, cap), I32)
    for back in range(1, most):
        same = (pltpu.roll(owners, back, 1) == owners) & (lane >= back)
        rank = rank + same.astype(I32)
    return owners[:1], rank[:1], wanted % tok_rows + 1


def place_rows(rows, wanted, tok_rows, most):
    owners, rank, _ = slots_of(wanted, tok_rows, most)
    first = owners * (HALVES * most) + rank
    target = jnp.concatenate([first + half * most for half in range(HALVES)], axis=1)
    return iota((rows, target.shape[1]), 0) == target


def lists_kernel(tok_rows, most, picks_ref, out_ref):
    owners, rank, marks = slots_of(picks_ref[...], tok_rows, most)
    cap = owners.shape[1]
    rows = out_ref.shape[0]
    left = jnp.where(iota((rows, cap), 0) == owners, marks, 0).astype(F32).astype(BF16)
    right = (iota((LANES, cap), 0) == rank).astype(F32).astype(BF16)
    out_ref[...] = matmul(left, right, NT)


def raw_kernel(tok_rows, most, picks_ref, up_ref, weight_ref, out_ref, place_ref):
    step = pl.program_id(0)
    rows, cap = out_ref.shape[0], up_ref.shape[0]
    half_width = weight_ref.shape[1] * pl.num_programs(0)

    @pl.when(step == 0)
    def _():
        wanted = picks_ref[...]
        hot = place_rows(rows, wanted, tok_rows, most)
        place_ref[...] = hot.astype(F32).astype(BF16)
        if out_ref.shape[1] > half_width:
            marks = slots_of(wanted, tok_rows, most)[2]
            both = jnp.concatenate([marks] * HALVES, axis=1)
            named = jnp.where(hot, both, 0).astype(F32).astype(BF16)
            ones = jnp.ones((LANES, HALVES * cap), BF16)
            out_ref[:, half_width:] = matmul(named, ones, NT).astype(BF16)

    up = up_ref[...]
    parts = [matmul(up, weight_ref[half], NT).astype(BF16) for half in range(HALVES)]
    columns = pl.ds(pl.multiple_of(step * STEP, STEP), STEP)
    out_ref[:, columns] = matmul(place_ref[...], jnp.concatenate(parts, axis=0), NN).astype(BF16)


def split_halves(gated, most):
    half = iota(gated.shape, 0) // most % HALVES
    return jnp.concatenate(
        [jnp.where(half == h, gated, 0.0).astype(BF16) for h in range(HALVES)], axis=1
    )


def owner_kernel(most, lists, got_ref, marks_ref, tokens_ref, logits_ref, send_ref, gated_ref, grad_ref):
    rows = send_ref.shape[0]
    half_width = got_ref.shape[1]
    lane = iota((rows, LANES), 1)
    row = iota((rows, LANES), 0)
    of_expert = (row // (HALVES * most) == lane).astype(F32).astype(BF16)
    if lists:
        spread = matmul(of_expert, marks_ref[...].astype(BF16), NN)
        marks = jnp.sum(jnp.where(lane == row % most, spread, 0.0), axis=1, keepdims=True)
    else:
        marks = marks_ref[...].astype(F32)
    chosen = marks == (lane + 1).astype(F32)

    logits = logits_ref[...]
    raised = jnp.exp(logits - jnp.max(logits, axis=1, keepdims=True))
    probs = raised / jnp.sum(raised, axis=1, keepdims=True)
    gates = matmul(of_expert, probs.astype(BF16), NT)
    gated = jnp.where(chosen, gates, 0.0)
    gated_ref[...] = gated.astype(BF16)
    tokens = tokens_ref[...]
    stack = jnp.concatenate(
        [tokens[:, h * half_width : (h + 1) * half_width] for h in range(HALVES)], axis=0
    )
    send_ref[:, :half_width] = matmul(split_halves(gated, most), stack, NN).astype(BF16)

    products = matmul(got_ref[...], stack, NT)
    half = row // most % HALVES
    own = products[:, :LANES]
    for h in range(1, HALVES):
        own = jnp.where(half == h, products[:, h * LANES : (h + 1) * LANES], own)
    own = jnp.where(chosen, own, 0.0)
    whole = own + pltpu.roll(own, most, 0)
    gate_grad = jnp.where(half == HALVES - 1, whole, 0.0).astype(BF16)
    score_grad = matmul(gate_grad, of_expert, TN)
    inner_sum = jnp.sum(probs * score_grad, axis=1, keepdims=True)
    logit_grad = (probs * (score_grad - inner_sum)).astype(BF16)
    grad_ref[...] = logit_grad
    shares = matmul(tokens, logit_grad, TN)
    blocks = rows // 8
    shares = shares.reshape(blocks, 16, LANES)
    for b in range(2):
        part = shares[:, 8 * b : 8 * (b + 1), :].reshape(rows, LANES)
        send_ref[:, half_width + b * LANES : half_width + (b + 1) * LANES] = part.astype(BF16)


def token_kernel(most, got_ref, gated_ref, grad_ref, router_ref, out_ref):
    half_width = got_ref.shape[1]
    tok_rows = out_ref.shape[0]
    expert_part = matmul(split_halves(gated_ref[...].astype(F32), most), got_ref[...], TN)
    for h in range(HALVES):
        columns = slice(h * half_width, (h + 1) * half_width)
        router_part = matmul(grad_ref[...], router_ref[columns, :], NT)
        out_ref[:, columns] = (expert_part[h * tok_rows : (h + 1) * tok_rows] + router_part).astype(BF16)


def final_kernel(tok_rows, most, got_ref, shares_ref, picks_ref, up_ref, out_ref, router_ref, place_ref):
    rows, cap = got_ref.shape[0], up_ref.shape[0]
    chunk, half = pl.program_id(0), pl.program_id(1)

    @pl.when((chunk == 0) & (half == 0))
    def _():
        hot = place_rows(rows, picks_ref[...], tok_rows, most).astype(F32).astype(BF16)
        for h in range(HALVES):
            place_ref[h] = hot[:, h * cap : (h + 1) * cap]
        for b in range(2):
            part = shares_ref[:, b * LANES : (b + 1) * LANES].astype(F32)
            router_ref[8 * b : 8 * (b + 1), :] = jnp.sum(part.reshape(rows // 8, 8, LANES), axis=0)

    picked = matmul(place_ref[half], got_ref[...], TN).astype(BF16)
    out_ref[...] = matmul(picked, up_ref[...], TN).astype(BF16)


def exchange(x, blocks):
    x = x.reshape(blocks, x.shape[0] // blocks, x.shape[1])
    x = lax.all_to_all(x, "expert", split_axis=0, concat_axis=0, tiled=True)
    return x.reshape(-1, x.shape[2])


def local(tokens, logits, weights, router_weight, expert_picks, cotangent):
    experts = lax.axis_size("expert")
    tok_rows, width = tokens.shape
    hidden = weights.shape[2]
    cap = expert_picks.shape[1]
    most = 2 * cap // experts
    rows = experts * most * HALVES
    half_width = width // HALVES
    weight = weights[0].reshape(HALVES, half_width, hidden)
    upstream = cotangent[0]
    full = lambda *shape: pl.BlockSpec(shape, lambda *_: (0,) * len(shape))
    shape_of = jax.ShapeDtypeStruct

    def raw_grads(columns):
        return pl.pallas_call(
            functools.partial(raw_kernel, tok_rows, most),
            grid=(half_width // STEP,),
            in_specs=[
                full(1, cap),
                full(cap, hidden),
                pl.BlockSpec((HALVES, STEP, hidden), lambda i: (0, i, 0)),
            ],
            out_specs=full(rows, columns),
            out_shape=shape_of((rows, columns), BF16),
            scratch_shapes=[pltpu.VMEM((rows, HALVES * cap), BF16)],
            compiler_params=params(),
            name="raw_grads",
        )(expert_picks, upstream, weight)

    def owner_step(got, marks, lists):
        marks_spec = full(experts, LANES) if lists else pl.BlockSpec((rows, LANES), lambda i: (0, half_width // LANES))
        return pl.pallas_call(
            functools.partial(owner_kernel, most, lists),
            grid=(1,),
            in_specs=[pl.BlockSpec((rows, half_width), lambda i: (0, 0)), marks_spec, full(tok_rows, width), full(tok_rows, experts)],
            out_specs=[full(rows, half_width + 2 * LANES), full(rows, LANES), full(tok_rows, experts)],
            out_shape=[
                shape_of((rows, half_width + 2 * LANES), BF16),
                shape_of((rows, LANES), BF16),
                shape_of((tok_rows, experts), BF16),
            ],
            compiler_params=params(),
            name="owner_step",
        )(got, marks, tokens, logits)

    def token_step(got, gated, grad):
        return pl.pallas_call(
            functools.partial(token_kernel, most),
            grid=(1,),
            in_specs=[full(rows, half_width), full(rows, LANES), full(tok_rows, experts), full(width, experts)],
            out_specs=full(tok_rows, width),
            out_shape=shape_of((tok_rows, width), BF16),
            compiler_params=params(),
            cost_estimate=pl.CostEstimate(flops=10**9, bytes_accessed=4 * 10**6, transcendentals=0),
            name="token_step",
        )(got, gated, grad, router_weight)

    def final_step(got):
        chunks = 2
        piece = half_width // chunks
        return pl.pallas_call(
            functools.partial(final_kernel, tok_rows, most),
            grid=(chunks, HALVES),
            in_specs=[
                pl.BlockSpec((rows, piece), lambda i, h: (0, i)),
                pl.BlockSpec((rows, 2 * LANES), lambda i, h: (0, half_width // (2 * LANES))),
                full(1, cap),
                full(cap, hidden),
            ],
            out_specs=[
                pl.BlockSpec((piece, hidden), lambda i, h: (h * chunks + i, 0)),
                full(width // experts, experts),
            ],
            out_shape=[shape_of((width, hidden), BF16), shape_of((width // experts, experts), F32)],
            scratch_shapes=[pltpu.VMEM((HALVES, rows, cap), BF16)],
            compiler_params=params(),
            name="final_step",
        )(got, got, expert_picks, upstream)

    def rest(got, marks, lists):
        send, gated, grad = owner_step(got, marks, lists)
        got_rows = exchange(send, experts)
        token_grad = token_step(got, gated, grad)
        weight_grad, router_grad = final_step(got_rows)
        return token_grad, weight_grad[None], router_grad

    def ids_inside():
        got = exchange(raw_grads(half_width + LANES), experts)
        return rest(got, got, False)

    def ids_first():
        named = pl.pallas_call(
            functools.partial(lists_kernel, tok_rows, most),
            out_shape=shape_of((experts, LANES), F32),
            name="lists",
        )(expert_picks)
        lists = exchange(named, experts)
        return rest(exchange(raw_grads(half_width), experts), lists, True)

    return lax.cond(lax.axis_index("dp") == 0, ids_inside, ids_first)


def solution(mesh):
    in_specs = (
        P(("dp", "expert"), None),
        P(("dp", "expert"), None),
        P("expert", None, None),
        P(),
        P(("dp", "expert"), None),
        P(("dp", "expert"), None, None),
    )
    out_specs = (
        P(("dp", "expert"), None),
        P(("dp", "expert"), None, None),
        P(("dp", "expert"), None),
    )
    return jax.shard_map(local, mesh=mesh, in_specs=in_specs, out_specs=out_specs, check_vma=False)
```

time: 194 us -> 155 us (0.80); the launches traced: 191 us -> 155 us
  blocking collectives: 0 us -> 51.1 us
  waiting for transfers between devices: 95 us -> 56.5 us
  starting transfers between devices: 48.9 us -> 23.3 us
  matrix products: 21.7 us -> 0 us
  Pallas kernels: 0 us -> 18.5 us
  local copies, waits for them, and re-layouts: 18.7 us -> 4.43 us
  other arithmetic: 5.51 us -> 0 us
    all_to_all x0 -> x1, blocking collectives: none -> 51.1 us  [exchange(): x = lax.all_to_all(x, 'expert', split_axis=0, concat_axis=0, tiled=True)]
    all_to_all x4 -> x2, waiting for transfers between devices: 95 us -> 56.5 us  [exchange(): x = lax.all_to_all(x, 'expert', split_axis=0, concat_axis=0, tiled=True)]
    all_to_all x4 -> x2, starting transfers between devices: 48.9 us -> 23.3 us  [exchange(): x = lax.all_to_all(x, 'expert', split_axis=0, concat_axis=0, tiled=True)]
    dot_general x9 -> x0, matrix products: 21.7 us -> none  [matmul(): return lax.dot_general(a, b, (dims, ((), ())), preferred_element_type=F32)]
    pallas_call x0 -> x5, Pallas kernels: none -> 18.5 us  [the longest x1 5.91 us: raw_grads(): pl.pallas_call(functools.partial(raw_kernel, tok_rows, most), grid=(half_...]
    reshape x4 -> x0, local copies, waits for them, and re-layouts: 12.3 us -> none  [the longest x1 4.12 us: local(): send_rows.reshape(experts, most, width)]
    cond x0 -> x14, local copies, waits for them, and re-layouts: none -> 4.43 us
    dot_general x1 -> x0, local copies, waits for them, and re-layouts: 2.58 us -> none  [matmul(): return lax.dot_general(a, b, (dims, ((), ())), preferred_element_type=F32)]
  transfers between devices with their start and end apart: 4 -> 2, of which waited for: 4 -> 2; matrix products, arithmetic and copies ran while one was open for 20% -> 0% of each run, Pallas kernels for 0% -> 6%
where the time goes in v3:
time: 155 us
  waiting for transfers between devices  56.5 us (36%)
  blocking collectives  51.1 us (33%)
  starting transfers between devices  23.3 us (15%)
  Pallas kernels  18.5 us (12%)
  local copies, waits for them, and re-layouts  4.43 us (3%)
    all_to_all x2, waiting for transfers between devices, exchange(): x = lax.all_to_all(x, 'expert', split_axis=0, concat_axis=0, tiled=True)  56.5 us
    all_to_all x1, blocking collectives, exchange(): x = lax.all_to_all(x, 'expert', split_axis=0, concat_axis=0, tiled=True)  51.1 us
    all_to_all x2, starting transfers between devices, exchange(): x = lax.all_to_all(x, 'expert', split_axis=0, concat_axis=0, tiled=True)  23.3 us
    pallas_call x1, Pallas kernels, raw_grads(): pl.pallas_call(functools.partial(raw_kernel, tok_rows, most), grid=(half_...  5.91 us
    pallas_call x1, Pallas kernels, final_step(): pl.pallas_call(functools.partial(final_kernel, tok_rows, most), grid=(chu...  5.69 us
    cond x14, local copies, waits for them, and re-layouts  4.43 us
  transfers between devices with their start and end apart: 2, of which 2 were waited for; matrix products, arithmetic and copies ran while one was open for 0% of the time, Pallas kernels for 6%

profile of v3, /device:TPU:1, one launch (start us, length us, event | category | flops | bytes accessed | tf_op | source)
XLA Modules:
  0.0 154.6 jit_solution(6397243990893114645)
XLA Ops:
  0.6 153.9 %conditional.1 = (f32[16,128]{1,0:T(8,128)}, bf16[128,2048]{1,0:T(8,128)(2,1)}, bf16[1,2048,1024]{2,1,0:T(8,128)(2,1)}) conditional(s32[]{:T(128)} %convert_element_type.3, (s32[1,256]{1,0:T(1,128)}, bf16[256,1024]{1,0:T(8,128)(2,1)}, bf16[2,1024,1024]{2,1,0:T(8,128)(2,1)}, bf16[128,2048]{1,0:T(8,128)(2,1)}, f32[128,128]{1,0:T(8,128)}, ...), branch_computations={%region_0.0_spmd, %region_1.0_spmd} | conditional | flops 1000000000 | bytes 47979036 | solution.py:268
  0.6 1.6 %lists.1 = f32[128,128]{1,0:T(8,128)} custom-call(s32[1,256]{1,0:T(1,128)} %get-tuple-element.24.picks_ref), custom_call_target="tpu_custom_call" | custom-call | tf_op jit(solution)/shard_map/cond/branch_0_fun/lists/pallas_call | solution.py:260
  2.2 16.3 %all-to-all-start.1 = ((f32[128,1,128]{2,1,0:T(1,128)}), f32[128,1,128]{2,1,0:T(1,128)S(1)}, u32[]{:S(2)}, u32[]{:S(2)}) async-start(f32[128,1,128]{2,1,0:T(1,128)} %bitcast.32), calls=%async_computation.1 | async-start | bytes 131072 | tf_op jit(solution)/shard_map/cond/branch_0_fun/all_to_all | solution.py:165
  18.6 5.9 %raw_grads.2 = bf16[1024,1024]{1,0:T(8,128)(2,1)S(1)} custom-call(s32[1,256]{1,0:T(1,128)} %get-tuple-element.24.picks_ref, bf16[256,1024]{1,0:T(8,128)(2,1)} %get-tuple-element.25.up_ref, bf16[2,1024,1024]{2,1,0:T(8,128)(2,1)} %get-tuple-element.26.weight_ref), custom_call_target="tpu_custom_call" | custom-call | tf_op jit(solution)/shard_map/cond/branch_0_fun/raw_grads/pallas_call | solution.py:183
  24.5 0.0 copy-start.6
  24.5 0.0 copy-start.8
  24.5 4.8 %all-to-all-done.1 = f32[128,1,128]{2,1,0:T(1,128)S(1)} async-done(((f32[128,1,128]{2,1,0:T(1,128)}), f32[128,1,128]{2,1,0:T(1,128)S(1)}, u32[]{:S(2)}, u32[]{:S(2)}) %all-to-all-start.1) | async-done | bytes 65568 | tf_op jit(solution)/shard_map/cond/branch_0_fun/all_to_all | solution.py:165
  29.3 51.1 %all_to_all.20 = bf16[128,8,1024]{2,1,0:T(8,128)(2,1)S(1)} all-to-all(bf16[128,8,1024]{2,1,0:T(8,128)(2,1)S(1)} %bitcast.24), channel_id=1, replica_groups=mesh['expert'=128,'dp'=2] {'expert'}, dimensions={0} | all-to-all | bytes 4194304 | tf_op jit(solution)/shard_map/cond/branch_0_fun/all_to_all | solution.py:165
  80.4 0.0 copy-done.6
  80.4 0.0 copy-done.8
  80.4 2.6 %owner_step.2 = (bf16[1024,1280]{1,0:T(8,128)(2,1)S(1)}, bf16[1024,128]{1,0:T(8,128)(2,1)S(1)}, bf16[128,128]{1,0:T(8,128)(2,1)S(1)}) custom-call(bf16[1024,1024]{1,0:T(8,128)(2,1)S(1)} %bitcast.22, f32[128,128]{1,0:T(8,128)S(1)} %bitcast.27, bf16[128,2048]{1,0:T(8,128)(2,1)S(1)} %copy-done.6, f32[128,128]{1,0:T(8,128)S(1)} %copy-done.8), custom_call_target="tpu_custom_call" | custom-call | tf_op jit(solution)/shard_map/cond/branch_0_fun/owner_step/pallas_call | solution.py:200
  83.0 0.0 copy-start
  83.0 1.3 copy-done
  84.3 0.0 copy-start.2
  84.3 1.5 copy-done.2
  85.8 0.0 copy-start.4
  85.8 7.0 %all-to-all-start.2 = ((bf16[128,8,1280]{2,1,0:T(8,128)(2,1)}), bf16[128,8,1280]{2,1,0:T(8,128)(2,1)S(1)}, u32[]{:S(2)}, u32[]{:S(2)}) async-start(bf16[128,8,1280]{2,1,0:T(8,128)(2,1)} %bitcast.25), calls=%async_computation.2 | async-start | bytes 5242880 | tf_op jit(solution)/shard_map/cond/branch_0_fun/all_to_all | solution.py:165
  92.8 0.0 copy-start.10
  92.8 0.0 copy-start.1
  92.8 1.6 %copy-done.1 = bf16[128,8,1024]{2,1,0:T(8,128)(2,1)S(1)} copy-done((bf16[128,8,1024]{2,1,0:T(8,128)(2,1)S(1)}, bf16[128,8,1024]{2,1,0:T(8,128)(2,1)}, u32[]{:S(2)}) %copy-start.1) | copy-done | bytes 2097176 | tf_op jit(solution)/shard_map/cond
  94.4 2.7 %token_step.2 = bf16[128,2048]{1,0:T(8,128)(2,1)} custom-call(bf16[1024,1024]{1,0:T(8,128)(2,1)S(1)} %bitcast.23, bf16[1024,128]{1,0:T(8,128)(2,1)S(1)} %get-tuple-element.29.gated_ref, bf16[128,128]{1,0:T(8,128)(2,1)S(1)} %get-tuple-element.30.grad_ref, bf16[2048,128]{1,0:T(8,128)(2,1)} %get-tuple-element.31.router_ref), custom_call_target="tpu_custom_call" | custom-call | flops 1000000000 | bytes 4000000 | tf_op jit(solution)/shard_map/cond/branch_0_fun/token_step/pallas_call | solution.py:215
  97.2 51.7 %all-to-all-done.2 = bf16[128,8,1280]{2,1,0:T(8,128)(2,1)S(1)} async-done(((bf16[128,8,1280]{2,1,0:T(8,128)(2,1)}), bf16[128,8,1280]{2,1,0:T(8,128)(2,1)S(1)}, u32[]{:S(2)}, u32[]{:S(2)}) %all-to-all-start.2) | async-done | bytes 2621472 | tf_op jit(solution)/shard_map/cond/branch_0_fun/all_to_all | solution.py:165
  148.9 0.0 copy-done.4
  148.9 0.0 copy-done.10
  148.9 5.7 %final_step.2 = (bf16[2048,1024]{1,0:T(8,128)(2,1)}, f32[16,128]{1,0:T(8,128)}) custom-call(bf16[1024,1280]{1,0:T(8,128)(2,1)S(1)} %bitcast.19, bf16[1024,1280]{1,0:T(8,128)(2,1)S(1)} %bitcast.20, s32[1,256]{1,0:T(1,128)S(1)} %copy-done.10, bf16[256,1024]{1,0:T(8,128)(2,1)S(1)} %copy-done.4), custom_call_target="tpu_custom_call" | custom-call | tf_op jit(solution)/shard_map/cond/branch_0_fun/final_step/pallas_call | solution.py:229
Async XLA Ops:
  2.2 27.0 %all-to-all-start.1 = ((f32[128,1,128]{2,1,0:T(1,128)}), f32[128,1,128]{2,1,0:T(1,128)S(1)}, u32[]{:S(2)}, u32[]{:S(2)}) async-start(f32[128,1,128]{2,1,0:T(1,128)} %bitcast.32), calls=%async_computation.1 | async-start | bytes 131072 | tf_op jit(solution)/shard_map/cond/branch_0_fun/all_to_all | solution.py:165
  24.5 55.9 %copy-start.6 = (bf16[128,2048]{1,0:T(8,128)(2,1)S(1)}, bf16[128,2048]{1,0:T(8,128)(2,1)}, u32[]{:S(2)}) copy-start(bf16[128,2048]{1,0:T(8,128)(2,1)} %get-tuple-element.27.tokens_ref) | copy-start | bytes 1572868 | tf_op jit(solution)/shard_map/cond
  24.5 55.9 %copy-start.8 = (f32[128,128]{1,0:T(8,128)S(1)}, f32[128,128]{1,0:T(8,128)}, u32[]{:S(2)}) copy-start(f32[128,128]{1,0:T(8,128)} %get-tuple-element.28.logits_ref) | copy-start | bytes 196612 | tf_op jit(solution)/shard_map/cond
  83.0 1.3 copy-start
  84.3 1.5 copy-start.2
  85.8 63.1 %copy-start.4 = (bf16[256,1024]{1,0:T(8,128)(2,1)S(1)}, bf16[256,1024]{1,0:T(8,128)(2,1)}, u32[]{:S(2)}) copy-start(bf16[256,1024]{1,0:T(8,128)(2,1)} %get-tuple-element.25.up_ref) | copy-start | bytes 1572868 | tf_op jit(solution)/shard_map/cond
  85.8 63.1 %all-to-all-start.2 = ((bf16[128,8,1280]{2,1,0:T(8,128)(2,1)}), bf16[128,8,1280]{2,1,0:T(8,128)(2,1)S(1)}, u32[]{:S(2)}, u32[]{:S(2)}) async-start(bf16[128,8,1280]{2,1,0:T(8,128)(2,1)} %bitcast.25), calls=%async_computation.2 | async-start | bytes 5242880 | tf_op jit(solution)/shard_map/cond/branch_0_fun/all_to_all | solution.py:165
  92.8 56.0 %copy-start.10 = (s32[1,256]{1,0:T(1,128)S(1)}, s32[1,256]{1,0:T(1,128)}, u32[]{:S(2)}) copy-start(s32[1,256]{1,0:T(1,128)} %get-tuple-element.24.picks_ref) | copy-start | bytes 3076 | tf_op jit(solution)/shard_map/cond
  92.8 1.6 %copy-start.1 = (bf16[128,8,1024]{2,1,0:T(8,128)(2,1)S(1)}, bf16[128,8,1024]{2,1,0:T(8,128)(2,1)}, u32[]{:S(2)}) copy-start(bf16[128,8,1024]{2,1,0:T(8,128)(2,1)} %copy-done) | copy-start | bytes 6291460 | tf_op jit(solution)/shard_map/cond

commit v4 on v3

--- a/solution.py
+++ b/solution.py
@@ -27,8 +27,8 @@
     return lax.broadcasted_iota(I32, shape, dim)
 
 
-def params():
-    return pltpu.CompilerParams(vmem_limit_bytes=40 * 1024 * 1024)
+def params(mebibytes=60):
+    return pltpu.CompilerParams(vmem_limit_bytes=mebibytes * 1024 * 1024)
 
 
 def slots_of(wanted, tok_rows, most):
@@ -49,16 +49,16 @@
     return iota((rows, target.shape[1]), 0) == target
 
 
-def lists_kernel(tok_rows, most, picks_ref, out_ref):
-    owners, rank, marks = slots_of(picks_ref[...], tok_rows, most)
+def name_lists(wanted, owners_count, tok_rows, most):
+    owners, rank, marks = slots_of(wanted, tok_rows, most)
     cap = owners.shape[1]
-    rows = out_ref.shape[0]
-    left = jnp.where(iota((rows, cap), 0) == owners, marks, 0).astype(F32).astype(BF16)
+    left = jnp.where(iota((owners_count, cap), 0) == owners, marks, 0).astype(F32).astype(BF16)
     right = (iota((LANES, cap), 0) == rank).astype(F32).astype(BF16)
-    out_ref[...] = matmul(left, right, NT)
-
-
-def raw_kernel(tok_rows, most, picks_ref, up_ref, weight_ref, out_ref, place_ref):
+    return matmul(left, right, NT)
+
+
+def raw_kernel(tok_rows, most, picks_ref, up_ref, weight_ref, out_ref, *rest):
+    place_ref = rest[-1]
     step = pl.program_id(0)
     rows, cap = out_ref.shape[0], up_ref.shape[0]
     half_width = weight_ref.shape[1] * pl.num_programs(0)
@@ -68,7 +68,9 @@
         wanted = picks_ref[...]
         hot = place_rows(rows, wanted, tok_rows, most)
         place_ref[...] = hot.astype(F32).astype(BF16)
-        if out_ref.shape[1] > half_width:
+        if len(rest) > 1:
+            rest[0][...] = name_lists(wanted, rest[0].shape[0], tok_rows, most)
+        else:
             marks = slots_of(wanted, tok_rows, most)[2]
             both = jnp.concatenate([marks] * HALVES, axis=1)
             named = jnp.where(hot, both, 0).astype(F32).astype(BF16)
@@ -133,9 +135,11 @@
         send_ref[:, half_width + b * LANES : half_width + (b + 1) * LANES] = part.astype(BF16)
 
 
-def token_kernel(most, got_ref, gated_ref, grad_ref, router_ref, out_ref):
+def token_kernel(most, picks_ref, got_ref, gated_ref, grad_ref, router_ref, out_ref, place_ref):
     half_width = got_ref.shape[1]
     tok_rows = out_ref.shape[0]
+    hot = place_rows(got_ref.shape[0], picks_ref[...], tok_rows, most)
+    place_ref[...] = hot.astype(F32).T.astype(BF16)
     expert_part = matmul(split_halves(gated_ref[...].astype(F32), most), got_ref[...], TN)
     for h in range(HALVES):
         columns = slice(h * half_width, (h + 1) * half_width)
@@ -143,20 +147,18 @@
         out_ref[:, columns] = (expert_part[h * tok_rows : (h + 1) * tok_rows] + router_part).astype(BF16)
 
 
-def final_kernel(tok_rows, most, got_ref, shares_ref, picks_ref, up_ref, out_ref, router_ref, place_ref):
+def final_kernel(got_ref, shares_ref, place_ref, up_ref, out_ref, router_ref):
     rows, cap = got_ref.shape[0], up_ref.shape[0]
     chunk, half = pl.program_id(0), pl.program_id(1)
 
     @pl.when((chunk == 0) & (half == 0))
     def _():
-        hot = place_rows(rows, picks_ref[...], tok_rows, most).astype(F32).astype(BF16)
-        for h in range(HALVES):
-            place_ref[h] = hot[:, h * cap : (h + 1) * cap]
         for b in range(2):
             part = shares_ref[:, b * LANES : (b + 1) * LANES].astype(F32)
             router_ref[8 * b : 8 * (b + 1), :] = jnp.sum(part.reshape(rows // 8, 8, LANES), axis=0)
 
-    picked = matmul(place_ref[half], got_ref[...], TN).astype(BF16)
+    picks = pl.ds(pl.multiple_of(half * cap, cap), cap)
+    picked = matmul(place_ref[picks, :], got_ref[...], NN).astype(BF16)
     out_ref[...] = matmul(picked, up_ref[...], TN).astype(BF16)
 
 
@@ -179,8 +181,9 @@
     full = lambda *shape: pl.BlockSpec(shape, lambda *_: (0,) * len(shape))
     shape_of = jax.ShapeDtypeStruct
 
-    def raw_grads(columns):
-        return pl.pallas_call(
+    def raw_grads(lists):
+        columns = half_width if lists else half_width + LANES
+        out = pl.pallas_call(
             functools.partial(raw_kernel, tok_rows, most),
             grid=(half_width // STEP,),
             in_specs=[
@@ -188,12 +191,13 @@
                 full(cap, hidden),
                 pl.BlockSpec((HALVES, STEP, hidden), lambda i: (0, i, 0)),
             ],
-            out_specs=full(rows, columns),
-            out_shape=shape_of((rows, columns), BF16),
+            out_specs=[full(rows, columns)] + [full(experts, LANES)] * lists,
+            out_shape=[shape_of((rows, columns), BF16)] + [shape_of((experts, LANES), F32)] * lists,
             scratch_shapes=[pltpu.VMEM((rows, HALVES * cap), BF16)],
             compiler_params=params(),
             name="raw_grads",
         )(expert_picks, upstream, weight)
+        return out
 
     def owner_step(got, marks, lists):
         marks_spec = full(experts, LANES) if lists else pl.BlockSpec((rows, LANES), lambda i: (0, half_width // LANES))
@@ -215,24 +219,30 @@
         return pl.pallas_call(
             functools.partial(token_kernel, most),
             grid=(1,),
-            in_specs=[full(rows, half_width), full(rows, LANES), full(tok_rows, experts), full(width, experts)],
-            out_specs=full(tok_rows, width),
-            out_shape=shape_of((tok_rows, width), BF16),
-            compiler_params=params(),
+            in_specs=[
+                full(1, cap),
+                full(rows, half_width),
+                full(rows, LANES),
+                full(tok_rows, experts),
+                full(width, experts),
+            ],
+            out_specs=[full(tok_rows, width), full(HALVES * cap, rows)],
+            out_shape=[shape_of((tok_rows, width), BF16), shape_of((HALVES * cap, rows), BF16)],
+            compiler_params=params(32),
             cost_estimate=pl.CostEstimate(flops=10**9, bytes_accessed=4 * 10**6, transcendentals=0),
             name="token_step",
-        )(got, gated, grad, router_weight)
-
-    def final_step(got):
+        )(expert_picks, got, gated, grad, router_weight)
+
+    def final_step(got, place):
         chunks = 2
         piece = half_width // chunks
         return pl.pallas_call(
-            functools.partial(final_kernel, tok_rows, most),
+            final_kernel,
             grid=(chunks, HALVES),
             in_specs=[
                 pl.BlockSpec((rows, piece), lambda i, h: (0, i)),
                 pl.BlockSpec((rows, 2 * LANES), lambda i, h: (0, half_width // (2 * LANES))),
-                full(1, cap),
+                full(HALVES * cap, rows),
                 full(cap, hidden),
             ],
             out_specs=[
@@ -240,30 +250,26 @@
                 full(width // experts, experts),
             ],
             out_shape=[shape_of((width, hidden), BF16), shape_of((width // experts, experts), F32)],
-            scratch_shapes=[pltpu.VMEM((HALVES, rows, cap), BF16)],
-            compiler_params=params(),
+            compiler_params=params(32),
             name="final_step",
-        )(got, got, expert_picks, upstream)
+        )(got, got, place, upstream)
 
     def rest(got, marks, lists):
         send, gated, grad = owner_step(got, marks, lists)
         got_rows = exchange(send, experts)
-        token_grad = token_step(got, gated, grad)
-        weight_grad, router_grad = final_step(got_rows)
+        token_grad, place = token_step(got, gated, grad)
+        weight_grad, router_grad = final_step(got_rows, place)
         return token_grad, weight_grad[None], router_grad
 
     def ids_inside():
-        got = exchange(raw_grads(half_width + LANES), experts)
+        (raw,) = raw_grads(False)
+        got = exchange(raw, experts)
         return rest(got, got, False)
 
     def ids_first():
-        named = pl.pallas_call(
-            functools.partial(lists_kernel, tok_rows, most),
-            out_shape=shape_of((experts, LANES), F32),
-            name="lists",
-        )(expert_picks)
+        raw, named = raw_grads(True)
         lists = exchange(named, experts)
-        return rest(exchange(raw_grads(half_width), experts), lists, True)
+        return rest(exchange(raw, experts), lists, True)
 
     return lax.cond(lax.axis_index("dp") == 0, ids_inside, ids_first)
 

time: 155 us -> 155 us (level)
  blocking collectives: 51.1 us -> 74.1 us
  starting transfers between devices: 23.3 us -> 7.02 us
  waiting for transfers between devices: 56.5 us -> 48 us
  Pallas kernels: 18.5 us -> 20.9 us
    all_to_all x1 -> x2, blocking collectives: 51.1 us -> 74.1 us  [exchange(): x = lax.all_to_all(x, 'expert', split_axis=0, concat_axis=0, tiled=True)]
    all_to_all x2 -> x1, starting transfers between devices: 23.3 us -> 7.02 us  [exchange(): x = lax.all_to_all(x, 'expert', split_axis=0, concat_axis=0, tiled=True)]
    all_to_all x2 -> x1, waiting for transfers between devices: 56.5 us -> 48 us  [exchange(): x = lax.all_to_all(x, 'expert', split_axis=0, concat_axis=0, tiled=True)]
    pallas_call x1, Pallas kernels: 2.59 us -> 5.68 us  [owner_step(): pl.pallas_call(functools.partial(owner_kernel, most, lists), grid=(1,), i...]
    pallas_call x2 -> x1, Pallas kernels: 7.25 us -> 5.02 us  [final_step(): pl.pallas_call(final_kernel, grid=(chunks, HALVES), in_specs=[pl.BlockSpe...]
    cond x14 -> x18, local copies, waits for them, and re-layouts: 4.43 us -> 3.82 us
  transfers between devices with their start and end apart: 2 -> 1, of which waited for: 2 -> 1; matrix products, arithmetic and copies ran while one was open for 0% -> 0% of each run, Pallas kernels for 6% -> 2%
where the time goes in v4:
time: 155 us
  blocking collectives  74.1 us (48%)
  waiting for transfers between devices  48 us (31%)
  Pallas kernels  20.9 us (13%)
  starting transfers between devices  7.02 us (5%)
  local copies, waits for them, and re-layouts  3.82 us (2%)
    all_to_all x2, blocking collectives, exchange(): x = lax.all_to_all(x, 'expert', split_axis=0, concat_axis=0, tiled=True)  74.1 us
    all_to_all x1, waiting for transfers between devices, exchange(): x = lax.all_to_all(x, 'expert', split_axis=0, concat_axis=0, tiled=True)  48 us
    pallas_call x1, Pallas kernels, raw_grads(): pl.pallas_call(functools.partial(raw_kernel, tok_rows, most), grid=(half_...  7.33 us
    all_to_all x1, starting transfers between devices, exchange(): x = lax.all_to_all(x, 'expert', split_axis=0, concat_axis=0, tiled=True)  7.02 us
    pallas_call x1, Pallas kernels, owner_step(): pl.pallas_call(functools.partial(owner_kernel, most, lists), grid=(1,), i...  5.68 us
    pallas_call x1, Pallas kernels, final_step(): pl.pallas_call(final_kernel, grid=(chunks, HALVES), in_specs=[pl.BlockSpe...  5.02 us
    cond x18, local copies, waits for them, and re-layouts  3.82 us
  transfers between devices with their start and end apart: 1, of which 1 were waited for; matrix products, arithmetic and copies ran while one was open for 0% of the time, Pallas kernels for 2%

profile of v4, /device:TPU:1, one launch (start us, length us, event | category | flops | bytes accessed | tf_op | source)
XLA Modules:
  0.0 154.6 jit_solution(18155256068934537452)
XLA Ops:
  0.6 153.9 %conditional.1 = (bf16[128,2048]{1,0:T(8,128)(2,1)}, f32[16,128]{1,0:T(8,128)}, bf16[1,2048,1024]{2,1,0:T(8,128)(2,1)}) conditional(s32[]{:T(128)} %convert_element_type.3, (s32[1,256]{1,0:T(1,128)}, bf16[256,1024]{1,0:T(8,128)(2,1)}, bf16[2,1024,1024]{2,1,0:T(8,128)(2,1)}, bf16[128,2048]{1,0:T(8,128)(2,1)}, f32[128,128]{1,0:T(8,128)}, ...), branch_computations={%region_0.0_spmd, %region_1.0_spmd} | conditional | flops 1000000000 | bytes 40049204 | solution.py:274
  0.6 7.3 %raw_grads.2 = (bf16[1024,1024]{1,0:T(8,128)(2,1)}, f32[128,128]{1,0:T(8,128)}) custom-call(s32[1,256]{1,0:T(1,128)} %get-tuple-element.24.picks_ref, bf16[256,1024]{1,0:T(8,128)(2,1)} %get-tuple-element.25.up_ref, bf16[2,1024,1024]{2,1,0:T(8,128)(2,1)} %get-tuple-element.26.weight_ref), custom_call_target="tpu_custom_call" | custom-call | tf_op jit(solution)/shard_map/cond/branch_0_fun/raw_grads/pallas_call | solution.py:186
  8.0 0.0 copy-start.12
  8.0 0.0 copy-start.14
  8.0 27.6 %all_to_all.20 = f32[128,1,128]{2,1,0:T(1,128)} all-to-all(f32[128,1,128]{2,1,0:T(1,128)} %bitcast.34), channel_id=1, replica_groups=mesh['expert'=128,'dp'=2] {'expert'}, dimensions={0} | all-to-all | bytes 131072 | tf_op jit(solution)/shard_map/cond/branch_0_fun/all_to_all | solution.py:167
  35.6 46.4 %all_to_all.21 = bf16[128,8,1024]{2,1,0:T(8,128)(2,1)} all-to-all(bf16[128,8,1024]{2,1,0:T(8,128)(2,1)} %bitcast.32), channel_id=1, replica_groups=mesh['expert'=128,'dp'=2] {'expert'}, dimensions={0} | all-to-all | bytes 4194304 | tf_op jit(solution)/shard_map/cond/branch_0_fun/all_to_all | solution.py:167
  82.0 0.0 copy-done.12
  82.0 0.0 copy-done.14
  82.0 5.7 %owner_step.2 = (bf16[1024,1280]{1,0:T(8,128)(2,1)}, bf16[1024,128]{1,0:T(8,128)(2,1)}, bf16[128,128]{1,0:T(8,128)(2,1)}) custom-call(bf16[1024,1024]{1,0:T(8,128)(2,1)} %bitcast.23, f32[128,128]{1,0:T(8,128)} %bitcast.33, bf16[128,2048]{1,0:T(8,128)(2,1)S(1)} %copy-done.12, f32[128,128]{1,0:T(8,128)S(1)} %copy-done.14), custom_call_target="tpu_custom_call" | custom-call | tf_op jit(solution)/shard_map/cond/branch_0_fun/owner_step/pallas_call | solution.py:204
  87.7 0.0 copy-start.6
  87.7 0.0 copy-start.8
  87.7 0.0 copy-start.16
  87.7 0.0 copy-start.10
  87.7 7.0 %all-to-all-start.2 = ((bf16[128,8,1280]{2,1,0:T(8,128)(2,1)}), bf16[128,8,1280]{2,1,0:T(8,128)(2,1)S(1)}, u32[]{:S(2)}, u32[]{:S(2)}) async-start(bf16[128,8,1280]{2,1,0:T(8,128)(2,1)} %bitcast.30), calls=%async_computation.2 | async-start | bytes 5242880 | tf_op jit(solution)/shard_map/cond/branch_0_fun/all_to_all | solution.py:167
  94.8 0.0 copy-done.6
  94.8 0.0 copy-done.8
  94.8 0.0 copy-done.16
  94.8 0.0 copy-start.1
  94.8 1.6 %copy-done.1 = bf16[128,8,1024]{2,1,0:T(8,128)(2,1)S(1)} copy-done((bf16[128,8,1024]{2,1,0:T(8,128)(2,1)S(1)}, bf16[128,8,1024]{2,1,0:T(8,128)(2,1)}, u32[]{:S(2)}) %copy-start.1) | copy-done | bytes 2097176 | tf_op jit(solution)/shard_map/cond
  96.4 2.9 %token_step.2 = (bf16[128,2048]{1,0:T(8,128)(2,1)}, bf16[512,1024]{1,0:T(8,128)(2,1)S(1)}) custom-call(s32[1,256]{1,0:T(1,128)S(1)} %copy-done.16, bf16[1024,1024]{1,0:T(8,128)(2,1)S(1)} %bitcast.24, bf16[1024,128]{1,0:T(8,128)(2,1)S(1)} %copy-done.6, bf16[128,128]{1,0:T(8,128)(2,1)S(1)} %copy-done.8, bf16[2048,128]{1,0:T(8,128)(2,1)} %get-tuple-element.33.router_ref), custom_call_target="tpu_custom_call" | custom-call | flops 1000000000 | bytes 4000000 | tf_op jit(solution)/shard_map/cond/branch_0_fun/token_step/pallas_call | solution.py:219
  99.3 0.0 copy-start.2
  99.3 1.0 copy-done.2
  100.3 48.0 %all-to-all-done.2 = bf16[128,8,1280]{2,1,0:T(8,128)(2,1)S(1)} async-done(((bf16[128,8,1280]{2,1,0:T(8,128)(2,1)}), bf16[128,8,1280]{2,1,0:T(8,128)(2,1)S(1)}, u32[]{:S(2)}, u32[]{:S(2)}) %all-to-all-start.2) | async-done | bytes 2621472 | tf_op jit(solution)/shard_map/cond/branch_0_fun/all_to_all | solution.py:167
  148.3 0.0 copy-done.10
  148.3 0.0 copy-start.3
  148.3 1.2 copy-done.3
  149.5 5.0 %final_step.2 = (bf16[2048,1024]{1,0:T(8,128)(2,1)}, f32[16,128]{1,0:T(8,128)}) custom-call(bf16[1024,1280]{1,0:T(8,128)(2,1)S(1)} %bitcast.16, bf16[1024,1280]{1,0:T(8,128)(2,1)S(1)} %bitcast.17, bf16[512,1024]{1,0:T(8,128)(2,1)S(1)} %copy-done.3, bf16[256,1024]{1,0:T(8,128)(2,1)S(1)} %copy-done.10), custom_call_target="tpu_custom_call" | custom-call | tf_op jit(solution)/shard_map/cond/branch_0_fun/final_step/pallas_call | solution.py:239
Async XLA Ops:
  8.0 74.1 %copy-start.12 = (bf16[128,2048]{1,0:T(8,128)(2,1)S(1)}, bf16[128,2048]{1,0:T(8,128)(2,1)}, u32[]{:S(2)}) copy-start(bf16[128,2048]{1,0:T(8,128)(2,1)} %get-tuple-element.29.tokens_ref) | copy-start | bytes 1572868 | tf_op jit(solution)/shard_map/cond
  8.0 74.1 %copy-start.14 = (f32[128,128]{1,0:T(8,128)S(1)}, f32[128,128]{1,0:T(8,128)}, u32[]{:S(2)}) copy-start(f32[128,128]{1,0:T(8,128)} %get-tuple-element.30.logits_ref) | copy-start | bytes 196612 | tf_op jit(solution)/shard_map/cond
  87.7 7.0 %copy-start.6 = (bf16[1024,128]{1,0:T(8,128)(2,1)S(1)}, bf16[1024,128]{1,0:T(8,128)(2,1)}, u32[]{:S(2)}) copy-start(bf16[1024,128]{1,0:T(8,128)(2,1)} %get-tuple-element.31.gated_ref) | copy-start | bytes 786436 | tf_op jit(solution)/shard_map/cond
  87.7 7.1 %copy-start.8 = (bf16[128,128]{1,0:T(8,128)(2,1)S(1)}, bf16[128,128]{1,0:T(8,128)(2,1)}, u32[]{:S(2)}) copy-start(bf16[128,128]{1,0:T(8,128)(2,1)} %get-tuple-element.32.grad_ref) | copy-start | bytes 98308 | tf_op jit(solution)/shard_map/cond
  87.7 7.1 %copy-start.16 = (s32[1,256]{1,0:T(1,128)S(1)}, s32[1,256]{1,0:T(1,128)}, u32[]{:S(2)}) copy-start(s32[1,256]{1,0:T(1,128)} %get-tuple-element.24.picks_ref) | copy-start | bytes 3076 | tf_op jit(solution)/shard_map/cond
  87.7 60.6 %copy-start.10 = (bf16[256,1024]{1,0:T(8,128)(2,1)S(1)}, bf16[256,1024]{1,0:T(8,128)(2,1)}, u32[]{:S(2)}) copy-start(bf16[256,1024]{1,0:T(8,128)(2,1)} %get-tuple-element.25.up_ref) | copy-start | bytes 1572868 | tf_op jit(solution)/shard_map/cond
  87.7 60.6 %all-to-all-start.2 = ((bf16[128,8,1280]{2,1,0:T(8,128)(2,1)}), bf16[128,8,1280]{2,1,0:T(8,128)(2,1)S(1)}, u32[]{:S(2)}, u32[]{:S(2)}) async-start(bf16[128,8,1280]{2,1,0:T(8,128)(2,1)} %bitcast.30), calls=%async_computation.2 | async-start | bytes 5242880 | tf_op jit(solution)/shard_map/cond/branch_0_fun/all_to_all | solution.py:167
  94.8 1.6 %copy-start.1 = (bf16[128,8,1024]{2,1,0:T(8,128)(2,1)S(1)}, bf16[128,8,1024]{2,1,0:T(8,128)(2,1)}, u32[]{:S(2)}) copy-start(bf16[128,8,1024]{2,1,0:T(8,128)(2,1)} %all_to_all.21) | copy-start | bytes 6291460 | tf_op jit(solution)/shard_map/cond
  99.3 1.0 copy-start.2
  148.3 1.2 copy-start.3

commit v5 on v3

--- a/solution.py
+++ b/solution.py
@@ -27,8 +27,8 @@
     return lax.broadcasted_iota(I32, shape, dim)
 
 
-def params():
-    return pltpu.CompilerParams(vmem_limit_bytes=40 * 1024 * 1024)
+def params(mebibytes=60):
+    return pltpu.CompilerParams(vmem_limit_bytes=mebibytes * 1024 * 1024)
 
 
 def slots_of(wanted, tok_rows, most):
@@ -49,36 +49,53 @@
     return iota((rows, target.shape[1]), 0) == target
 
 
-def lists_kernel(tok_rows, most, picks_ref, out_ref):
-    owners, rank, marks = slots_of(picks_ref[...], tok_rows, most)
+def name_lists(wanted, owners_count, tok_rows, most):
+    owners, rank, marks = slots_of(wanted, tok_rows, most)
     cap = owners.shape[1]
-    rows = out_ref.shape[0]
-    left = jnp.where(iota((rows, cap), 0) == owners, marks, 0).astype(F32).astype(BF16)
+    left = jnp.where(iota((owners_count, cap), 0) == owners, marks, 0).astype(F32).astype(BF16)
     right = (iota((LANES, cap), 0) == rank).astype(F32).astype(BF16)
-    out_ref[...] = matmul(left, right, NT)
-
-
-def raw_kernel(tok_rows, most, picks_ref, up_ref, weight_ref, out_ref, place_ref):
+    return matmul(left, right, NT)
+
+
+def raw_kernel(tok_rows, most, steps, picks_ref, up_ref, weight_ref, out_ref, *rest):
+    place_ref, made_ref, sems = rest[-3:]
     step = pl.program_id(0)
     rows, cap = out_ref.shape[0], up_ref.shape[0]
-    half_width = weight_ref.shape[1] * pl.num_programs(0)
+    half_width = steps * STEP
+
+    def sent(columns, at):
+        return pltpu.make_async_copy(made_ref.at[:, columns], out_ref.at[:, columns], sems.at[at])
+
+    def block(at):
+        return pl.ds(pl.multiple_of(at * STEP, STEP), STEP)
 
     @pl.when(step == 0)
     def _():
         wanted = picks_ref[...]
         hot = place_rows(rows, wanted, tok_rows, most)
         place_ref[...] = hot.astype(F32).astype(BF16)
-        if out_ref.shape[1] > half_width:
+        if len(rest) > 3:
+            rest[0][...] = name_lists(wanted, rest[0].shape[0], tok_rows, most)
+        else:
             marks = slots_of(wanted, tok_rows, most)[2]
             both = jnp.concatenate([marks] * HALVES, axis=1)
             named = jnp.where(hot, both, 0).astype(F32).astype(BF16)
             ones = jnp.ones((LANES, HALVES * cap), BF16)
-            out_ref[:, half_width:] = matmul(named, ones, NT).astype(BF16)
+            made_ref[:, half_width:] = matmul(named, ones, NT).astype(BF16)
+            sent(pl.ds(half_width, LANES), steps).start()
 
     up = up_ref[...]
     parts = [matmul(up, weight_ref[half], NT).astype(BF16) for half in range(HALVES)]
-    columns = pl.ds(pl.multiple_of(step * STEP, STEP), STEP)
-    out_ref[:, columns] = matmul(place_ref[...], jnp.concatenate(parts, axis=0), NN).astype(BF16)
+    raw = matmul(place_ref[...], jnp.concatenate(parts, axis=0), NN)
+    made_ref[:, block(step)] = raw.astype(BF16)
+    sent(block(step), step).start()
+
+    @pl.when(step == steps - 1)
+    def _():
+        for at in range(steps):
+            sent(block(at), at).wait()
+        if made_ref.shape[1] > half_width:
+            sent(pl.ds(half_width, LANES), steps).wait()
 
 
 def split_halves(gated, most):
@@ -88,9 +105,11 @@
     )
 
 
-def owner_kernel(most, lists, got_ref, marks_ref, tokens_ref, logits_ref, send_ref, gated_ref, grad_ref):
-    rows = send_ref.shape[0]
-    half_width = got_ref.shape[1]
+def owner_kernel(most, lists, raw_ref, marks_ref, tokens_ref, logits_ref, out_ref, *rest):
+    gated_ref, grad_ref, got_ref, send_ref, sems = rest
+    rows, half_width = got_ref.shape
+    fetch = pltpu.make_async_copy(raw_ref.at[:, pl.ds(0, half_width)], got_ref, sems.at[2])
+    fetch.start()
     lane = iota((rows, LANES), 1)
     row = iota((rows, LANES), 0)
     of_expert = (row // (HALVES * most) == lane).astype(F32).astype(BF16)
@@ -112,7 +131,11 @@
         [tokens[:, h * half_width : (h + 1) * half_width] for h in range(HALVES)], axis=0
     )
     send_ref[:, :half_width] = matmul(split_halves(gated, most), stack, NN).astype(BF16)
-
+    columns = pl.ds(0, half_width)
+    first = pltpu.make_async_copy(send_ref.at[:, columns], out_ref.at[:, columns], sems.at[0])
+    first.start()
+
+    fetch.wait()
     products = matmul(got_ref[...], stack, NT)
     half = row // most % HALVES
     own = products[:, :LANES]
@@ -131,6 +154,11 @@
     for b in range(2):
         part = shares[:, 8 * b : 8 * (b + 1), :].reshape(rows, LANES)
         send_ref[:, half_width + b * LANES : half_width + (b + 1) * LANES] = part.astype(BF16)
+    columns = pl.ds(half_width, 2 * LANES)
+    second = pltpu.make_async_copy(send_ref.at[:, columns], out_ref.at[:, columns], sems.at[1])
+    second.start()
+    first.wait()
+    second.wait()
 
 
 def token_kernel(most, got_ref, gated_ref, grad_ref, router_ref, out_ref):
@@ -179,33 +207,44 @@
     full = lambda *shape: pl.BlockSpec(shape, lambda *_: (0,) * len(shape))
     shape_of = jax.ShapeDtypeStruct
 
-    def raw_grads(columns):
-        return pl.pallas_call(
-            functools.partial(raw_kernel, tok_rows, most),
+    def raw_grads(lists):
+        columns = half_width if lists else half_width + LANES
+        out = pl.pallas_call(
+            functools.partial(raw_kernel, tok_rows, most, half_width // STEP),
             grid=(half_width // STEP,),
             in_specs=[
                 full(1, cap),
                 full(cap, hidden),
                 pl.BlockSpec((HALVES, STEP, hidden), lambda i: (0, i, 0)),
             ],
-            out_specs=full(rows, columns),
-            out_shape=shape_of((rows, columns), BF16),
-            scratch_shapes=[pltpu.VMEM((rows, HALVES * cap), BF16)],
+            out_specs=[pl.BlockSpec(memory_space=pltpu.HBM)] + [full(experts, LANES)] * lists,
+            out_shape=[shape_of((rows, columns), BF16)] + [shape_of((experts, LANES), F32)] * lists,
+            scratch_shapes=[
+                pltpu.VMEM((rows, HALVES * cap), BF16),
+                pltpu.VMEM((rows, columns), BF16),
+                pltpu.SemaphoreType.DMA((half_width // STEP + 1,)),
+            ],
             compiler_params=params(),
             name="raw_grads",
         )(expert_picks, upstream, weight)
+        return out
 
     def owner_step(got, marks, lists):
         marks_spec = full(experts, LANES) if lists else pl.BlockSpec((rows, LANES), lambda i: (0, half_width // LANES))
         return pl.pallas_call(
             functools.partial(owner_kernel, most, lists),
             grid=(1,),
-            in_specs=[pl.BlockSpec((rows, half_width), lambda i: (0, 0)), marks_spec, full(tok_rows, width), full(tok_rows, experts)],
-            out_specs=[full(rows, half_width + 2 * LANES), full(rows, LANES), full(tok_rows, experts)],
+            in_specs=[pl.BlockSpec(memory_space=pltpu.HBM), marks_spec, full(tok_rows, width), full(tok_rows, experts)],
+            out_specs=[pl.BlockSpec(memory_space=pltpu.HBM), full(rows, LANES), full(tok_rows, experts)],
             out_shape=[
                 shape_of((rows, half_width + 2 * LANES), BF16),
                 shape_of((rows, LANES), BF16),
                 shape_of((tok_rows, experts), BF16),
+            ],
+            scratch_shapes=[
+                pltpu.VMEM((rows, half_width), BF16),
+                pltpu.VMEM((rows, half_width + 2 * LANES), BF16),
+                pltpu.SemaphoreType.DMA((3,)),
             ],
             compiler_params=params(),
             name="owner_step",
@@ -218,7 +257,7 @@
             in_specs=[full(rows, half_width), full(rows, LANES), full(tok_rows, experts), full(width, experts)],
             out_specs=full(tok_rows, width),
             out_shape=shape_of((tok_rows, width), BF16),
-            compiler_params=params(),
+            compiler_params=params(40),
             cost_estimate=pl.CostEstimate(flops=10**9, bytes_accessed=4 * 10**6, transcendentals=0),
             name="token_step",
         )(got, gated, grad, router_weight)
@@ -241,7 +280,7 @@
             ],
             out_shape=[shape_of((width, hidden), BF16), shape_of((width // experts, experts), F32)],
             scratch_shapes=[pltpu.VMEM((HALVES, rows, cap), BF16)],
-            compiler_params=params(),
+            compiler_params=params(40),
             name="final_step",
         )(got, got, expert_picks, upstream)
 
@@ -253,17 +292,14 @@
         return token_grad, weight_grad[None], router_grad
 
     def ids_inside():
-        got = exchange(raw_grads(half_width + LANES), experts)
+        (raw,) = raw_grads(False)
+        got = exchange(raw, experts)
         return rest(got, got, False)
 
     def ids_first():
-        named = pl.pallas_call(
-            functools.partial(lists_kernel, tok_rows, most),
-            out_shape=shape_of((experts, LANES), F32),
-            name="lists",
-        )(expert_picks)
+        raw, named = raw_grads(True)
         lists = exchange(named, experts)
-        return rest(exchange(raw_grads(half_width), experts), lists, True)
+        return rest(exchange(raw, experts), lists, True)
 
     return lax.cond(lax.axis_index("dp") == 0, ids_inside, ids_first)
 

time: 155 us -> 156 us (level)
  blocking collectives: 51.1 us -> 73.6 us
  starting transfers between devices: 23.3 us -> 6.82 us
  waiting for transfers between devices: 56.5 us -> 48.9 us
  Pallas kernels: 18.5 us -> 23.3 us
  local copies, waits for them, and re-layouts: 4.43 us -> 1.62 us
    all_to_all x1 -> x2, blocking collectives: 51.1 us -> 73.6 us  [exchange(): x = lax.all_to_all(x, 'expert', split_axis=0, concat_axis=0, tiled=True)]
    all_to_all x2 -> x1, starting transfers between devices: 23.3 us -> 6.82 us  [exchange(): x = lax.all_to_all(x, 'expert', split_axis=0, concat_axis=0, tiled=True)]
    all_to_all x2 -> x1, waiting for transfers between devices: 56.5 us -> 48.9 us  [exchange(): x = lax.all_to_all(x, 'expert', split_axis=0, concat_axis=0, tiled=True)]
    pallas_call x1, Pallas kernels: 2.59 us -> 7.23 us  [owner_step(): pl.pallas_call(functools.partial(owner_kernel, most, lists), grid=(1,), i...]
    cond x14, local copies, waits for them, and re-layouts: 4.43 us -> 1.62 us
    pallas_call x2 -> x1, Pallas kernels: 7.47 us -> 7.68 us  [raw_grads(): pl.pallas_call(functools.partial(raw_kernel, tok_rows, most, half_width /...]
  transfers between devices with their start and end apart: 2 -> 1, of which waited for: 2 -> 1; matrix products, arithmetic and copies ran while one was open for 0% -> 0% of each run, Pallas kernels for 6% -> 2%
where the time goes in v5:
time: 156 us; the launch traced here: 155 us
  blocking collectives  73.6 us (47%)
  waiting for transfers between devices  48.9 us (31%)
  Pallas kernels  23.3 us (15%)
  starting transfers between devices  6.82 us (4%)
  local copies, waits for them, and re-layouts  1.62 us (1%)
    all_to_all x2, blocking collectives, exchange(): x = lax.all_to_all(x, 'expert', split_axis=0, concat_axis=0, tiled=True)  73.6 us
    all_to_all x1, waiting for transfers between devices, exchange(): x = lax.all_to_all(x, 'expert', split_axis=0, concat_axis=0, tiled=True)  48.9 us
    pallas_call x1, Pallas kernels, raw_grads(): pl.pallas_call(functools.partial(raw_kernel, tok_rows, most, half_width /...  7.68 us
    pallas_call x1, Pallas kernels, owner_step(): pl.pallas_call(functools.partial(owner_kernel, most, lists), grid=(1,), i...  7.23 us
    all_to_all x1, starting transfers between devices, exchange(): x = lax.all_to_all(x, 'expert', split_axis=0, concat_axis=0, tiled=True)  6.82 us
    pallas_call x1, Pallas kernels, final_step(): pl.pallas_call(functools.partial(final_kernel, tok_rows, most), grid=(chu...  5.69 us
  transfers between devices with their start and end apart: 1, of which 1 were waited for; matrix products, arithmetic and copies ran while one was open for 0% of the time, Pallas kernels for 2%

profile of v5, /device:TPU:1, one launch (start us, length us, event | category | flops | bytes accessed | tf_op | source)
XLA Modules:
  0.0 155.0 jit_solution(8984009650671455804)
XLA Ops:
  0.6 154.4 %conditional.1 = (f32[16,128]{1,0:T(8,128)}, bf16[128,2048]{1,0:T(8,128)(2,1)}, bf16[1,2048,1024]{2,1,0:T(8,128)(2,1)}) conditional(s32[]{:T(128)} %convert_element_type.3, (s32[1,256]{1,0:T(1,128)}, bf16[256,1024]{1,0:T(8,128)(2,1)}, bf16[2,1024,1024]{2,1,0:T(8,128)(2,1)}, bf16[128,2048]{1,0:T(8,128)(2,1)}, f32[128,128]{1,0:T(8,128)}, ...), branch_computations={%region_0.0_spmd, %region_1.0_spmd} | conditional | flops 1000000000 | bytes 31660540 | solution.py:304
  0.6 7.7 %raw_grads.2 = (bf16[1024,1024]{1,0:T(8,128)(2,1)}, f32[128,128]{1,0:T(8,128)}) custom-call(s32[1,256]{1,0:T(1,128)} %get-tuple-element.24.picks_ref, bf16[256,1024]{1,0:T(8,128)(2,1)} %get-tuple-element.25.up_ref, bf16[2,1024,1024]{2,1,0:T(8,128)(2,1)} %get-tuple-element.26.weight_ref), custom_call_target="tpu_custom_call" | custom-call | tf_op jit(solution)/shard_map/cond/branch_0_fun/raw_grads/pallas_call | solution.py:212
  8.3 0.0 copy-start.8
  8.3 0.0 copy-start.10
  8.4 27.7 %all_to_all.20 = f32[128,1,128]{2,1,0:T(1,128)} all-to-all(f32[128,1,128]{2,1,0:T(1,128)} %bitcast.32), channel_id=1, replica_groups=mesh['expert'=128,'dp'=2] {'expert'}, dimensions={0} | all-to-all | bytes 131072 | tf_op jit(solution)/shard_map/cond/branch_0_fun/all_to_all | solution.py:193
  36.1 45.9 %all_to_all.21 = bf16[128,8,1024]{2,1,0:T(8,128)(2,1)} all-to-all(bf16[128,8,1024]{2,1,0:T(8,128)(2,1)} %bitcast.30), channel_id=1, replica_groups=mesh['expert'=128,'dp'=2] {'expert'}, dimensions={0} | all-to-all | bytes 4194304 | tf_op jit(solution)/shard_map/cond/branch_0_fun/all_to_all | solution.py:193
  82.0 0.0 copy-done.8
  82.0 0.0 copy-done.10
  82.0 7.2 %owner_step.2 = (bf16[1024,1280]{1,0:T(8,128)(2,1)}, bf16[1024,128]{1,0:T(8,128)(2,1)}, bf16[128,128]{1,0:T(8,128)(2,1)}) custom-call(bf16[1024,1024]{1,0:T(8,128)(2,1)} %bitcast.21, f32[128,128]{1,0:T(8,128)} %bitcast.31, bf16[128,2048]{1,0:T(8,128)(2,1)S(1)} %copy-done.8, f32[128,128]{1,0:T(8,128)S(1)} %copy-done.10), custom_call_target="tpu_custom_call" | custom-call | tf_op jit(solution)/shard_map/cond/branch_0_fun/owner_step/pallas_call | solution.py:234
  89.2 0.0 copy-start.4
  89.2 0.0 copy-start.5
  89.2 0.0 copy-start.6
  89.2 6.8 %all-to-all-start.2 = ((bf16[128,8,1280]{2,1,0:T(8,128)(2,1)}), bf16[128,8,1280]{2,1,0:T(8,128)(2,1)S(1)}, u32[]{:S(2)}, u32[]{:S(2)}) async-start(bf16[128,8,1280]{2,1,0:T(8,128)(2,1)} %bitcast.28), calls=%async_computation.2 | async-start | bytes 5242880 | tf_op jit(solution)/shard_map/cond/branch_0_fun/all_to_all | solution.py:193
  96.1 0.0 copy-start.12
  96.1 0.0 copy-done.4
  96.1 0.0 copy-done.5
  96.1 0.0 copy-start.1
  96.1 1.6 %copy-done.1 = bf16[128,8,1024]{2,1,0:T(8,128)(2,1)S(1)} copy-done((bf16[128,8,1024]{2,1,0:T(8,128)(2,1)S(1)}, bf16[128,8,1024]{2,1,0:T(8,128)(2,1)}, u32[]{:S(2)}) %copy-start.1) | copy-done | bytes 2097176 | tf_op jit(solution)/shard_map/cond
  97.7 2.7 %token_step.2 = bf16[128,2048]{1,0:T(8,128)(2,1)} custom-call(bf16[1024,1024]{1,0:T(8,128)(2,1)S(1)} %bitcast.22, bf16[1024,128]{1,0:T(8,128)(2,1)S(1)} %copy-done.4, bf16[128,128]{1,0:T(8,128)(2,1)S(1)} %copy-done.5, bf16[2048,128]{1,0:T(8,128)(2,1)} %get-tuple-element.33.router_ref), custom_call_target="tpu_custom_call" | custom-call | flops 1000000000 | bytes 4000000 | tf_op jit(solution)/shard_map/cond/branch_0_fun/token_step/pallas_call | solution.py:254
  100.4 48.9 %all-to-all-done.2 = bf16[128,8,1280]{2,1,0:T(8,128)(2,1)S(1)} async-done(((bf16[128,8,1280]{2,1,0:T(8,128)(2,1)}), bf16[128,8,1280]{2,1,0:T(8,128)(2,1)S(1)}, u32[]{:S(2)}, u32[]{:S(2)}) %all-to-all-start.2) | async-done | bytes 2621472 | tf_op jit(solution)/shard_map/cond/branch_0_fun/all_to_all | solution.py:193
  149.3 0.0 copy-done.6
  149.3 0.0 copy-done.12
  149.3 5.7 %final_step.2 = (bf16[2048,1024]{1,0:T(8,128)(2,1)}, f32[16,128]{1,0:T(8,128)}) custom-call(bf16[1024,1280]{1,0:T(8,128)(2,1)S(1)} %bitcast.19, bf16[1024,1280]{1,0:T(8,128)(2,1)S(1)} %bitcast.20, s32[1,256]{1,0:T(1,128)S(1)} %copy-done.12, bf16[256,1024]{1,0:T(8,128)(2,1)S(1)} %copy-done.6), custom_call_target="tpu_custom_call" | custom-call | tf_op jit(solution)/shard_map/cond/branch_0_fun/final_step/pallas_call | solution.py:268
Async XLA Ops:
  8.3 73.6 %copy-start.8 = (bf16[128,2048]{1,0:T(8,128)(2,1)S(1)}, bf16[128,2048]{1,0:T(8,128)(2,1)}, u32[]{:S(2)}) copy-start(bf16[128,2048]{1,0:T(8,128)(2,1)} %get-tuple-element.29.tokens_ref) | copy-start | bytes 1572868 | tf_op jit(solution)/shard_map/cond
  8.3 73.6 %copy-start.10 = (f32[128,128]{1,0:T(8,128)S(1)}, f32[128,128]{1,0:T(8,128)}, u32[]{:S(2)}) copy-start(f32[128,128]{1,0:T(8,128)} %get-tuple-element.30.logits_ref) | copy-start | bytes 196612 | tf_op jit(solution)/shard_map/cond
  89.2 6.9 %copy-start.4 = (bf16[1024,128]{1,0:T(8,128)(2,1)S(1)}, bf16[1024,128]{1,0:T(8,128)(2,1)}, u32[]{:S(2)}) copy-start(bf16[1024,128]{1,0:T(8,128)(2,1)} %get-tuple-element.31.gated_ref) | copy-start | bytes 786436 | tf_op jit(solution)/shard_map/cond
  89.2 6.9 %copy-start.5 = (bf16[128,128]{1,0:T(8,128)(2,1)S(1)}, bf16[128,128]{1,0:T(8,128)(2,1)}, u32[]{:S(2)}) copy-start(bf16[128,128]{1,0:T(8,128)(2,1)} %get-tuple-element.32.grad_ref) | copy-start | bytes 98308 | tf_op jit(solution)/shard_map/cond
  89.2 60.1 %copy-start.6 = (bf16[256,1024]{1,0:T(8,128)(2,1)S(1)}, bf16[256,1024]{1,0:T(8,128)(2,1)}, u32[]{:S(2)}) copy-start(bf16[256,1024]{1,0:T(8,128)(2,1)} %get-tuple-element.25.up_ref) | copy-start | bytes 1572868 | tf_op jit(solution)/shard_map/cond
  89.2 60.1 %all-to-all-start.2 = ((bf16[128,8,1280]{2,1,0:T(8,128)(2,1)}), bf16[128,8,1280]{2,1,0:T(8,128)(2,1)S(1)}, u32[]{:S(2)}, u32[]{:S(2)}) async-start(bf16[128,8,1280]{2,1,0:T(8,128)(2,1)} %bitcast.28), calls=%async_computation.2 | async-start | bytes 5242880 | tf_op jit(solution)/shard_map/cond/branch_0_fun/all_to_all | solution.py:193
  96.1 53.2 %copy-start.12 = (s32[1,256]{1,0:T(1,128)S(1)}, s32[1,256]{1,0:T(1,128)}, u32[]{:S(2)}) copy-start(s32[1,256]{1,0:T(1,128)} %get-tuple-element.24.picks_ref) | copy-start | bytes 3076 | tf_op jit(solution)/shard_map/cond
  96.1 1.6 %copy-start.1 = (bf16[128,8,1024]{2,1,0:T(8,128)(2,1)S(1)}, bf16[128,8,1024]{2,1,0:T(8,128)(2,1)}, u32[]{:S(2)}) copy-start(bf16[128,8,1024]{2,1,0:T(8,128)(2,1)} %all_to_all.21) | copy-start | bytes 6291460 | tf_op jit(solution)/shard_map/cond

commit v6 on v4

--- a/solution.py
+++ b/solution.py
@@ -27,7 +27,7 @@
     return lax.broadcasted_iota(I32, shape, dim)
 
 
-def params(mebibytes=60):
+def params(mebibytes=40):
     return pltpu.CompilerParams(vmem_limit_bytes=mebibytes * 1024 * 1024)
 
 
@@ -90,7 +90,7 @@
     )
 
 
-def owner_kernel(most, lists, got_ref, marks_ref, tokens_ref, logits_ref, send_ref, gated_ref, grad_ref):
+def owner_kernel(most, lists, got_ref, marks_ref, tokens_ref, logits_ref, router_ref, send_ref, token_ref):
     rows = send_ref.shape[0]
     half_width = got_ref.shape[1]
     lane = iota((rows, LANES), 1)
@@ -108,12 +108,12 @@
     probs = raised / jnp.sum(raised, axis=1, keepdims=True)
     gates = matmul(of_expert, probs.astype(BF16), NT)
     gated = jnp.where(chosen, gates, 0.0)
-    gated_ref[...] = gated.astype(BF16)
     tokens = tokens_ref[...]
     stack = jnp.concatenate(
         [tokens[:, h * half_width : (h + 1) * half_width] for h in range(HALVES)], axis=0
     )
-    send_ref[:, :half_width] = matmul(split_halves(gated, most), stack, NN).astype(BF16)
+    gated = split_halves(gated, most)
+    send_ref[:, :half_width] = matmul(gated, stack, NN).astype(BF16)
 
     products = matmul(got_ref[...], stack, NT)
     half = row // most % HALVES
@@ -126,7 +126,6 @@
     score_grad = matmul(gate_grad, of_expert, TN)
     inner_sum = jnp.sum(probs * score_grad, axis=1, keepdims=True)
     logit_grad = (probs * (score_grad - inner_sum)).astype(BF16)
-    grad_ref[...] = logit_grad
     shares = matmul(tokens, logit_grad, TN)
     blocks = rows // 8
     shares = shares.reshape(blocks, 16, LANES)
@@ -134,31 +133,29 @@
         part = shares[:, 8 * b : 8 * (b + 1), :].reshape(rows, LANES)
         send_ref[:, half_width + b * LANES : half_width + (b + 1) * LANES] = part.astype(BF16)
 
-
-def token_kernel(most, picks_ref, got_ref, gated_ref, grad_ref, router_ref, out_ref, place_ref):
-    half_width = got_ref.shape[1]
-    tok_rows = out_ref.shape[0]
-    hot = place_rows(got_ref.shape[0], picks_ref[...], tok_rows, most)
-    place_ref[...] = hot.astype(F32).T.astype(BF16)
-    expert_part = matmul(split_halves(gated_ref[...].astype(F32), most), got_ref[...], TN)
+    expert_part = matmul(gated, got_ref[...], TN)
+    tok_rows = tokens.shape[0]
     for h in range(HALVES):
         columns = slice(h * half_width, (h + 1) * half_width)
-        router_part = matmul(grad_ref[...], router_ref[columns, :], NT)
-        out_ref[:, columns] = (expert_part[h * tok_rows : (h + 1) * tok_rows] + router_part).astype(BF16)
-
-
-def final_kernel(got_ref, shares_ref, place_ref, up_ref, out_ref, router_ref):
+        router_part = matmul(logit_grad, router_ref[columns, :], NT)
+        part = expert_part[h * tok_rows : (h + 1) * tok_rows] + router_part
+        token_ref[:, columns] = part.astype(BF16)
+
+
+def final_kernel(tok_rows, most, got_ref, shares_ref, picks_ref, up_ref, out_ref, router_ref, place_ref):
     rows, cap = got_ref.shape[0], up_ref.shape[0]
     chunk, half = pl.program_id(0), pl.program_id(1)
 
     @pl.when((chunk == 0) & (half == 0))
     def _():
+        hot = place_rows(rows, picks_ref[...], tok_rows, most).astype(F32).astype(BF16)
+        for h in range(HALVES):
+            place_ref[h] = hot[:, h * cap : (h + 1) * cap]
         for b in range(2):
             part = shares_ref[:, b * LANES : (b + 1) * LANES].astype(F32)
             router_ref[8 * b : 8 * (b + 1), :] = jnp.sum(part.reshape(rows // 8, 8, LANES), axis=0)
 
-    picks = pl.ds(pl.multiple_of(half * cap, cap), cap)
-    picked = matmul(place_ref[picks, :], got_ref[...], NN).astype(BF16)
+    picked = matmul(place_ref[half], got_ref[...], TN).astype(BF16)
     out_ref[...] = matmul(picked, up_ref[...], TN).astype(BF16)
 
 
@@ -200,49 +197,39 @@
         return out
 
     def owner_step(got, marks, lists):
-        marks_spec = full(experts, LANES) if lists else pl.BlockSpec((rows, LANES), lambda i: (0, half_width // LANES))
+        if lists:
+            marks_spec = full(experts, LANES)
+        else:
+            marks_spec = pl.BlockSpec((rows, LANES), lambda i: (0, half_width // LANES))
         return pl.pallas_call(
             functools.partial(owner_kernel, most, lists),
             grid=(1,),
-            in_specs=[pl.BlockSpec((rows, half_width), lambda i: (0, 0)), marks_spec, full(tok_rows, width), full(tok_rows, experts)],
-            out_specs=[full(rows, half_width + 2 * LANES), full(rows, LANES), full(tok_rows, experts)],
+            in_specs=[
+                full(rows, half_width),
+                marks_spec,
+                full(tok_rows, width),
+                full(tok_rows, experts),
+                full(width, experts),
+            ],
+            out_specs=[full(rows, half_width + 2 * LANES), full(tok_rows, width)],
             out_shape=[
                 shape_of((rows, half_width + 2 * LANES), BF16),
-                shape_of((rows, LANES), BF16),
-                shape_of((tok_rows, experts), BF16),
+                shape_of((tok_rows, width), BF16),
             ],
             compiler_params=params(),
             name="owner_step",
-        )(got, marks, tokens, logits)
-
-    def token_step(got, gated, grad):
-        return pl.pallas_call(
-            functools.partial(token_kernel, most),
-            grid=(1,),
-            in_specs=[
-                full(1, cap),
-                full(rows, half_width),
-                full(rows, LANES),
-                full(tok_rows, experts),
-                full(width, experts),
-            ],
-            out_specs=[full(tok_rows, width), full(HALVES * cap, rows)],
-            out_shape=[shape_of((tok_rows, width), BF16), shape_of((HALVES * cap, rows), BF16)],
-            compiler_params=params(32),
-            cost_estimate=pl.CostEstimate(flops=10**9, bytes_accessed=4 * 10**6, transcendentals=0),
-            name="token_step",
-        )(expert_picks, got, gated, grad, router_weight)
-
-    def final_step(got, place):
+        )(got, marks, tokens, logits, router_weight)
+
+    def final_step(got):
         chunks = 2
         piece = half_width // chunks
         return pl.pallas_call(
-            final_kernel,
+            functools.partial(final_kernel, tok_rows, most),
             grid=(chunks, HALVES),
             in_specs=[
                 pl.BlockSpec((rows, piece), lambda i, h: (0, i)),
                 pl.BlockSpec((rows, 2 * LANES), lambda i, h: (0, half_width // (2 * LANES))),
-                full(HALVES * cap, rows),
+                full(1, cap),
                 full(cap, hidden),
             ],
             out_specs=[
@@ -250,15 +237,14 @@
                 full(width // experts, experts),
             ],
             out_shape=[shape_of((width, hidden), BF16), shape_of((width // experts, experts), F32)],
-            compiler_params=params(32),
+            scratch_shapes=[pltpu.VMEM((HALVES, rows, cap), BF16)],
+            compiler_params=params(),
             name="final_step",
-        )(got, got, place, upstream)
+        )(got, got, expert_picks, upstream)
 
     def rest(got, marks, lists):
-        send, gated, grad = owner_step(got, marks, lists)
-        got_rows = exchange(send, experts)
-        token_grad, place = token_step(got, gated, grad)
-        weight_grad, router_grad = final_step(got_rows, place)
+        send, token_grad = owner_step(got, marks, lists)
+        weight_grad, router_grad = final_step(exchange(send, experts))
         return token_grad, weight_grad[None], router_grad
 
     def ids_inside():

time: 155 us -> 154 us (level)
  blocking collectives: 74.1 us -> 137 us
  waiting for transfers between devices: 48 us -> 0 us
  starting transfers between devices: 7.02 us -> 0 us
  Pallas kernels: 20.9 us -> 16.5 us
  local copies, waits for them, and re-layouts: 3.82 us -> 0.03 us
    all_to_all x2 -> x3, blocking collectives: 74.1 us -> 137 us  [exchange(): x = lax.all_to_all(x, 'expert', split_axis=0, concat_axis=0, tiled=True)]
    all_to_all x1 -> x0, waiting for transfers between devices: 48 us -> none  [exchange(): x = lax.all_to_all(x, 'expert', split_axis=0, concat_axis=0, tiled=True)]
    all_to_all x1 -> x0, starting transfers between devices: 7.02 us -> none  [exchange(): x = lax.all_to_all(x, 'expert', split_axis=0, concat_axis=0, tiled=True)]
    cond x18 -> x10, local copies, waits for them, and re-layouts: 3.82 us -> 0.03 us
    pallas_call x2 -> x1, Pallas kernels: 7.91 us -> 5.7 us  [final_step(): pl.pallas_call(functools.partial(final_kernel, tok_rows, most), grid=(chu...]
  transfers between devices with their start and end apart: 1 -> 0, of which waited for: 1 -> 0; matrix products, arithmetic and copies ran while one was open for 0% -> 0% of each run, Pallas kernels for 2% -> 0%
where the time goes in v6:
time: 154 us
  blocking collectives  137 us (89%)
  Pallas kernels  16.5 us (11%)
    all_to_all x3, blocking collectives, exchange(): x = lax.all_to_all(x, 'expert', split_axis=0, concat_axis=0, tiled=True)  137 us
    pallas_call x1, Pallas kernels, raw_grads(): pl.pallas_call(functools.partial(raw_kernel, tok_rows, most), grid=(half_...  6.02 us
    pallas_call x1, Pallas kernels, final_step(): pl.pallas_call(functools.partial(final_kernel, tok_rows, most), grid=(chu...  5.7 us
    pallas_call x1, Pallas kernels, owner_step(): pl.pallas_call(functools.partial(owner_kernel, most, lists), grid=(1,), i...  4.76 us

profile of v6, /device:TPU:1, one launch (start us, length us, event | category | flops | bytes accessed | tf_op | source)
XLA Modules:
  0.0 153.8 jit_solution(6868048864204624039)
XLA Ops:
  0.6 153.1 %conditional.1 = (bf16[128,2048]{1,0:T(8,128)(2,1)}, f32[16,128]{1,0:T(8,128)}, bf16[1,2048,1024]{2,1,0:T(8,128)(2,1)}) conditional(s32[]{:T(128)} %convert_element_type.3, (s32[1,256]{1,0:T(1,128)}, bf16[256,1024]{1,0:T(8,128)(2,1)}, bf16[2,1024,1024]{2,1,0:T(8,128)(2,1)}, bf16[128,2048]{1,0:T(8,128)(2,1)}, f32[128,128]{1,0:T(8,128)}, ...), branch_computations={%region_0.0_spmd, %region_1.0_spmd} | conditional | bytes 16519332 | solution.py:260
  0.6 6.0 %raw_grads.2 = (bf16[1024,1024]{1,0:T(8,128)(2,1)S(1)}, f32[128,128]{1,0:T(8,128)S(1)}) custom-call(s32[1,256]{1,0:T(1,128)} %get-tuple-element.24.picks_ref, bf16[256,1024]{1,0:T(8,128)(2,1)} %get-tuple-element.25.up_ref, bf16[2,1024,1024]{2,1,0:T(8,128)(2,1)} %get-tuple-element.26.weight_ref), custom_call_target="tpu_custom_call" | custom-call | tf_op jit(solution)/shard_map/cond/branch_0_fun/raw_grads/pallas_call | solution.py:183
  6.7 0.0 copy-start.2
  6.7 0.0 copy-start.4
  6.7 0.0 copy-start.6
  6.7 27.0 %all_to_all.20 = f32[128,1,128]{2,1,0:T(1,128)S(1)} all-to-all(f32[128,1,128]{2,1,0:T(1,128)S(1)} %bitcast.28), channel_id=1, replica_groups=mesh['expert'=128,'dp'=2] {'expert'}, dimensions={0} | all-to-all | bytes 131072 | tf_op jit(solution)/shard_map/cond/branch_0_fun/all_to_all | solution.py:164
  33.7 46.7 %all_to_all.21 = bf16[128,8,1024]{2,1,0:T(8,128)(2,1)S(1)} all-to-all(bf16[128,8,1024]{2,1,0:T(8,128)(2,1)S(1)} %bitcast.26), channel_id=1, replica_groups=mesh['expert'=128,'dp'=2] {'expert'}, dimensions={0} | all-to-all | bytes 4194304 | tf_op jit(solution)/shard_map/cond/branch_0_fun/all_to_all | solution.py:164
  80.4 0.0 copy-done.2
  80.4 0.0 copy-done.4
  80.4 0.0 copy-done.6
  80.4 4.8 %owner_step.2 = (bf16[1024,1280]{1,0:T(8,128)(2,1)S(1)}, bf16[128,2048]{1,0:T(8,128)(2,1)}) custom-call(bf16[1024,1024]{1,0:T(8,128)(2,1)S(1)} %bitcast.23, f32[128,128]{1,0:T(8,128)S(1)} %bitcast.27, bf16[128,2048]{1,0:T(8,128)(2,1)S(1)} %copy-done.2, f32[128,128]{1,0:T(8,128)S(1)} %copy-done.6, bf16[2048,128]{1,0:T(8,128)(2,1)S(1)} %copy-done.4), custom_call_target="tpu_custom_call" | custom-call | tf_op jit(solution)/shard_map/cond/branch_0_fun/owner_step/pallas_call | solution.py:204
  85.1 0.0 copy-start
  85.2 0.0 copy-start.8
  85.2 62.9 %all_to_all.22 = bf16[128,8,1280]{2,1,0:T(8,128)(2,1)S(1)} all-to-all(bf16[128,8,1280]{2,1,0:T(8,128)(2,1)S(1)} %bitcast.24), channel_id=1, replica_groups=mesh['expert'=128,'dp'=2] {'expert'}, dimensions={0} | all-to-all | bytes 5242880 | tf_op jit(solution)/shard_map/cond/branch_0_fun/all_to_all | solution.py:164
  148.0 0.0 copy-done
  148.1 0.0 copy-done.8
  148.1 5.7 %final_step.2 = (bf16[2048,1024]{1,0:T(8,128)(2,1)}, f32[16,128]{1,0:T(8,128)}) custom-call(bf16[1024,1280]{1,0:T(8,128)(2,1)S(1)} %bitcast.16, bf16[1024,1280]{1,0:T(8,128)(2,1)S(1)} %bitcast.17, s32[1,256]{1,0:T(1,128)S(1)} %copy-done.8, bf16[256,1024]{1,0:T(8,128)(2,1)S(1)} %copy-done), custom_call_target="tpu_custom_call" | custom-call | tf_op jit(solution)/shard_map/cond/branch_0_fun/final_step/pallas_call | solution.py:226
Async XLA Ops:
  6.7 73.7 %copy-start.2 = (bf16[128,2048]{1,0:T(8,128)(2,1)S(1)}, bf16[128,2048]{1,0:T(8,128)(2,1)}, u32[]{:S(2)}) copy-start(bf16[128,2048]{1,0:T(8,128)(2,1)} %get-tuple-element.29.tokens_ref) | copy-start | bytes 1572868 | tf_op jit(solution)/shard_map/cond
  6.7 73.7 %copy-start.4 = (bf16[2048,128]{1,0:T(8,128)(2,1)S(1)}, bf16[2048,128]{1,0:T(8,128)(2,1)}, u32[]{:S(2)}) copy-start(bf16[2048,128]{1,0:T(8,128)(2,1)} %get-tuple-element.31.router_ref) | copy-start | bytes 1572868 | tf_op jit(solution)/shard_map/cond
  6.7 73.7 %copy-start.6 = (f32[128,128]{1,0:T(8,128)S(1)}, f32[128,128]{1,0:T(8,128)}, u32[]{:S(2)}) copy-start(f32[128,128]{1,0:T(8,128)} %get-tuple-element.30.logits_ref) | copy-start | bytes 196612 | tf_op jit(solution)/shard_map/cond
  85.1 62.9 %copy-start = (bf16[256,1024]{1,0:T(8,128)(2,1)S(1)}, bf16[256,1024]{1,0:T(8,128)(2,1)}, u32[]{:S(2)}) copy-start(bf16[256,1024]{1,0:T(8,128)(2,1)} %get-tuple-element.25.up_ref) | copy-start | bytes 1572868 | tf_op jit(solution)/shard_map/cond
  85.2 62.9 %copy-start.8 = (s32[1,256]{1,0:T(1,128)S(1)}, s32[1,256]{1,0:T(1,128)}, u32[]{:S(2)}) copy-start(s32[1,256]{1,0:T(1,128)} %get-tuple-element.24.picks_ref) | copy-start | bytes 3076 | tf_op jit(solution)/shard_map/cond

commit v7 on v6

--- a/solution.py
+++ b/solution.py
@@ -12,7 +12,7 @@
 I32 = jnp.int32
 LANES = 128
 HALVES = 2
-STEP = 256
+STEP = 512
 
 NN = ((1,), (0,))
 NT = ((1,), (1,))
@@ -221,7 +221,7 @@
         )(got, marks, tokens, logits, router_weight)
 
     def final_step(got):
-        chunks = 2
+        chunks = 1
         piece = half_width // chunks
         return pl.pallas_call(
             functools.partial(final_kernel, tok_rows, most),

time: 154 us -> 152 us (0.987)
  Pallas kernels: 16.5 us -> 14.7 us
where the time goes in v7:
time: 152 us
  blocking collectives  137 us (90%)
  Pallas kernels  14.7 us (10%)
    all_to_all x3, blocking collectives, exchange(): x = lax.all_to_all(x, 'expert', split_axis=0, concat_axis=0, tiled=True)  137 us
    pallas_call x1, Pallas kernels, final_step(): pl.pallas_call(functools.partial(final_kernel, tok_rows, most), grid=(chu...  5.02 us
    pallas_call x1, Pallas kernels, raw_grads(): pl.pallas_call(functools.partial(raw_kernel, tok_rows, most), grid=(half_...  4.97 us
    pallas_call x1, Pallas kernels, owner_step(): pl.pallas_call(functools.partial(owner_kernel, most, lists), grid=(1,), i...  4.76 us

profile of v7, /device:TPU:1, one launch (start us, length us, event | category | flops | bytes accessed | tf_op | source)
XLA Modules:
  0.0 152.0 jit_solution(16771446726927935513)
XLA Ops:
  0.6 151.4 %conditional.1 = (bf16[128,2048]{1,0:T(8,128)(2,1)}, f32[16,128]{1,0:T(8,128)}, bf16[1,2048,1024]{2,1,0:T(8,128)(2,1)}) conditional(s32[]{:T(128)} %convert_element_type.3, (s32[1,256]{1,0:T(1,128)}, bf16[256,1024]{1,0:T(8,128)(2,1)}, bf16[2,1024,1024]{2,1,0:T(8,128)(2,1)}, bf16[128,2048]{1,0:T(8,128)(2,1)}, f32[128,128]{1,0:T(8,128)}, ...), branch_computations={%region_0.0_spmd, %region_1.0_spmd} | conditional | bytes 16519332 | solution.py:260
  0.6 5.0 %raw_grads.2 = (bf16[1024,1024]{1,0:T(8,128)(2,1)S(1)}, f32[128,128]{1,0:T(8,128)S(1)}) custom-call(s32[1,256]{1,0:T(1,128)} %get-tuple-element.24.picks_ref, bf16[256,1024]{1,0:T(8,128)(2,1)} %get-tuple-element.25.up_ref, bf16[2,1024,1024]{2,1,0:T(8,128)(2,1)} %get-tuple-element.26.weight_ref), custom_call_target="tpu_custom_call" | custom-call | tf_op jit(solution)/shard_map/cond/branch_0_fun/raw_grads/pallas_call | solution.py:183
  5.6 0.0 copy-start.2
  5.6 0.0 copy-start.4
  5.6 0.0 copy-start.6
  5.7 27.0 %all_to_all.20 = f32[128,1,128]{2,1,0:T(1,128)S(1)} all-to-all(f32[128,1,128]{2,1,0:T(1,128)S(1)} %bitcast.28), channel_id=1, replica_groups=mesh['expert'=128,'dp'=2] {'expert'}, dimensions={0} | all-to-all | bytes 131072 | tf_op jit(solution)/shard_map/cond/branch_0_fun/all_to_all | solution.py:164
  32.7 46.7 %all_to_all.21 = bf16[128,8,1024]{2,1,0:T(8,128)(2,1)S(1)} all-to-all(bf16[128,8,1024]{2,1,0:T(8,128)(2,1)S(1)} %bitcast.26), channel_id=1, replica_groups=mesh['expert'=128,'dp'=2] {'expert'}, dimensions={0} | all-to-all | bytes 4194304 | tf_op jit(solution)/shard_map/cond/branch_0_fun/all_to_all | solution.py:164
  79.3 0.0 copy-done.2
  79.3 0.0 copy-done.4
  79.3 0.0 copy-done.6
  79.3 4.8 %owner_step.2 = (bf16[1024,1280]{1,0:T(8,128)(2,1)S(1)}, bf16[128,2048]{1,0:T(8,128)(2,1)}) custom-call(bf16[1024,1024]{1,0:T(8,128)(2,1)S(1)} %bitcast.23, f32[128,128]{1,0:T(8,128)S(1)} %bitcast.27, bf16[128,2048]{1,0:T(8,128)(2,1)S(1)} %copy-done.2, f32[128,128]{1,0:T(8,128)S(1)} %copy-done.6, bf16[2048,128]{1,0:T(8,128)(2,1)S(1)} %copy-done.4), custom_call_target="tpu_custom_call" | custom-call | tf_op jit(solution)/shard_map/cond/branch_0_fun/owner_step/pallas_call | solution.py:204
  84.1 0.0 copy-start
  84.1 0.0 copy-start.8
  84.1 62.9 %all_to_all.22 = bf16[128,8,1280]{2,1,0:T(8,128)(2,1)S(1)} all-to-all(bf16[128,8,1280]{2,1,0:T(8,128)(2,1)S(1)} %bitcast.24), channel_id=1, replica_groups=mesh['expert'=128,'dp'=2] {'expert'}, dimensions={0} | all-to-all | bytes 5242880 | tf_op jit(solution)/shard_map/cond/branch_0_fun/all_to_all | solution.py:164
  147.0 0.0 copy-done
  147.0 0.0 copy-done.8
  147.0 5.0 %final_step.2 = (bf16[2048,1024]{1,0:T(8,128)(2,1)}, f32[16,128]{1,0:T(8,128)}) custom-call(bf16[1024,1280]{1,0:T(8,128)(2,1)S(1)} %bitcast.16, bf16[1024,1280]{1,0:T(8,128)(2,1)S(1)} %bitcast.17, s32[1,256]{1,0:T(1,128)S(1)} %copy-done.8, bf16[256,1024]{1,0:T(8,128)(2,1)S(1)} %copy-done), custom_call_target="tpu_custom_call" | custom-call | tf_op jit(solution)/shard_map/cond/branch_0_fun/final_step/pallas_call | solution.py:226
Async XLA Ops:
  5.6 73.7 %copy-start.2 = (bf16[128,2048]{1,0:T(8,128)(2,1)S(1)}, bf16[128,2048]{1,0:T(8,128)(2,1)}, u32[]{:S(2)}) copy-start(bf16[128,2048]{1,0:T(8,128)(2,1)} %get-tuple-element.29.tokens_ref) | copy-start | bytes 1572868 | tf_op jit(solution)/shard_map/cond
  5.6 73.7 %copy-start.4 = (bf16[2048,128]{1,0:T(8,128)(2,1)S(1)}, bf16[2048,128]{1,0:T(8,128)(2,1)}, u32[]{:S(2)}) copy-start(bf16[2048,128]{1,0:T(8,128)(2,1)} %get-tuple-element.31.router_ref) | copy-start | bytes 1572868 | tf_op jit(solution)/shard_map/cond
  5.6 73.7 %copy-start.6 = (f32[128,128]{1,0:T(8,128)S(1)}, f32[128,128]{1,0:T(8,128)}, u32[]{:S(2)}) copy-start(f32[128,128]{1,0:T(8,128)} %get-tuple-element.30.logits_ref) | copy-start | bytes 196612 | tf_op jit(solution)/shard_map/cond
  84.1 62.9 %copy-start = (bf16[256,1024]{1,0:T(8,128)(2,1)S(1)}, bf16[256,1024]{1,0:T(8,128)(2,1)}, u32[]{:S(2)}) copy-start(bf16[256,1024]{1,0:T(8,128)(2,1)} %get-tuple-element.25.up_ref) | copy-start | bytes 1572868 | tf_op jit(solution)/shard_map/cond
  84.1 62.9 %copy-start.8 = (s32[1,256]{1,0:T(1,128)S(1)}, s32[1,256]{1,0:T(1,128)}, u32[]{:S(2)}) copy-start(s32[1,256]{1,0:T(1,128)} %get-tuple-element.24.picks_ref) | copy-start | bytes 3076 | tf_op jit(solution)/shard_map/cond

commit v8 on v7

--- a/solution.py
+++ b/solution.py
@@ -90,51 +90,51 @@
     )
 
 
-def owner_kernel(most, lists, got_ref, marks_ref, tokens_ref, logits_ref, router_ref, send_ref, token_ref):
-    rows = send_ref.shape[0]
-    half_width = got_ref.shape[1]
-    lane = iota((rows, LANES), 1)
-    row = iota((rows, LANES), 0)
-    of_expert = (row // (HALVES * most) == lane).astype(F32).astype(BF16)
-    if lists:
-        spread = matmul(of_expert, marks_ref[...].astype(BF16), NN)
-        marks = jnp.sum(jnp.where(lane == row % most, spread, 0.0), axis=1, keepdims=True)
-    else:
-        marks = marks_ref[...].astype(F32)
-    chosen = marks == (lane + 1).astype(F32)
-
-    logits = logits_ref[...]
+def softmax(logits):
     raised = jnp.exp(logits - jnp.max(logits, axis=1, keepdims=True))
-    probs = raised / jnp.sum(raised, axis=1, keepdims=True)
-    gates = matmul(of_expert, probs.astype(BF16), NT)
-    gated = jnp.where(chosen, gates, 0.0)
-    tokens = tokens_ref[...]
-    stack = jnp.concatenate(
+    return raised / jnp.sum(raised, axis=1, keepdims=True)
+
+
+def stacked(tokens):
+    half_width = tokens.shape[1] // HALVES
+    return jnp.concatenate(
         [tokens[:, h * half_width : (h + 1) * half_width] for h in range(HALVES)], axis=0
     )
-    gated = split_halves(gated, most)
-    send_ref[:, :half_width] = matmul(gated, stack, NN).astype(BF16)
-
-    products = matmul(got_ref[...], stack, NT)
-    half = row // most % HALVES
+
+
+def experts_of(rows, most):
+    hot = iota((rows, LANES), 0) // (HALVES * most) == iota((rows, LANES), 1)
+    return hot.astype(F32).astype(BF16)
+
+
+def gated_tokens(most, chosen, probs):
+    of_expert = experts_of(chosen.shape[0], most)
+    gates = matmul(of_expert, probs.astype(BF16), NT)
+    return split_halves(jnp.where(chosen, gates, 0.0), most)
+
+
+def gradients(most, chosen, probs, tokens, got):
+    rows = got.shape[0]
+    products = matmul(got, stacked(tokens), NT)
+    half = iota((rows, LANES), 0) // most % HALVES
     own = products[:, :LANES]
     for h in range(1, HALVES):
         own = jnp.where(half == h, products[:, h * LANES : (h + 1) * LANES], own)
     own = jnp.where(chosen, own, 0.0)
     whole = own + pltpu.roll(own, most, 0)
     gate_grad = jnp.where(half == HALVES - 1, whole, 0.0).astype(BF16)
-    score_grad = matmul(gate_grad, of_expert, TN)
+    score_grad = matmul(gate_grad, experts_of(rows, most), TN)
     inner_sum = jnp.sum(probs * score_grad, axis=1, keepdims=True)
     logit_grad = (probs * (score_grad - inner_sum)).astype(BF16)
-    shares = matmul(tokens, logit_grad, TN)
-    blocks = rows // 8
-    shares = shares.reshape(blocks, 16, LANES)
-    for b in range(2):
-        part = shares[:, 8 * b : 8 * (b + 1), :].reshape(rows, LANES)
-        send_ref[:, half_width + b * LANES : half_width + (b + 1) * LANES] = part.astype(BF16)
-
-    expert_part = matmul(gated, got_ref[...], TN)
-    tok_rows = tokens.shape[0]
+    shares = matmul(tokens, logit_grad, TN).reshape(rows // 8, 16, LANES)
+    parts = [shares[:, 8 * b : 8 * (b + 1), :].reshape(rows, LANES).astype(BF16) for b in range(2)]
+    return logit_grad, parts
+
+
+def token_grads(got, gated, logit_grad, router_ref, token_ref):
+    half_width = got.shape[1]
+    tok_rows = token_ref.shape[0]
+    expert_part = matmul(gated, got, TN)
     for h in range(HALVES):
         columns = slice(h * half_width, (h + 1) * half_width)
         router_part = matmul(logit_grad, router_ref[columns, :], NT)
@@ -142,7 +142,51 @@
         token_ref[:, columns] = part.astype(BF16)
 
 
-def final_kernel(tok_rows, most, got_ref, shares_ref, picks_ref, up_ref, out_ref, router_ref, place_ref):
+def owner_kernel(most, got_ref, marks_ref, tokens_ref, logits_ref, send_ref, gated_ref, grad_ref):
+    rows, half_width = got_ref.shape
+    chosen = marks_ref[...].astype(F32) == (iota((rows, LANES), 1) + 1).astype(F32)
+    probs = softmax(logits_ref[...])
+    tokens = tokens_ref[...]
+    gated = gated_tokens(most, chosen, probs)
+    gated_ref[...] = gated
+    send_ref[:, :half_width] = matmul(gated, stacked(tokens), NN).astype(BF16)
+    logit_grad, parts = gradients(most, chosen, probs, tokens, got_ref[...])
+    grad_ref[...] = logit_grad
+    for b, part in enumerate(parts):
+        send_ref[:, half_width + b * LANES : half_width + (b + 1) * LANES] = part
+
+
+def rows_kernel(most, lists_ref, tokens_ref, logits_ref, send_ref, gated_ref, chosen_ref):
+    rows = send_ref.shape[0]
+    lane = iota((rows, LANES), 1)
+    spread = matmul(experts_of(rows, most), lists_ref[...].astype(BF16), NN)
+    slot = lane == iota((rows, LANES), 0) % most
+    marks = jnp.sum(jnp.where(slot, spread, 0.0), axis=1, keepdims=True)
+    chosen = marks == (lane + 1).astype(F32)
+    chosen_ref[...] = chosen.astype(F32).astype(BF16)
+    gated = gated_tokens(most, chosen, softmax(logits_ref[...]))
+    gated_ref[...] = gated
+    send_ref[...] = matmul(gated, stacked(tokens_ref[...]), NN).astype(BF16)
+
+
+def grads_kernel(most, *refs):
+    got_ref, _, gated_ref, chosen_ref, tokens_ref, logits_ref, router_ref, shares_ref, token_ref = refs
+    chosen = chosen_ref[...].astype(F32) > 0.5
+    probs = softmax(logits_ref[...])
+    got = got_ref[...]
+    logit_grad, parts = gradients(most, chosen, probs, tokens_ref[...], got)
+    for b, part in enumerate(parts):
+        shares_ref[:, b * LANES : (b + 1) * LANES] = part
+    token_grads(got, gated_ref[...], logit_grad, router_ref, token_ref)
+
+
+def final_kernel(tok_rows, most, *refs):
+    got_ref, shares_ref, picks_ref, up_ref, *extra = refs
+    *extra, place_ref = extra
+    if len(extra) > 2:
+        raw_ref, gated_ref, grad_ref, weight_ref, out_ref, router_ref, token_ref = extra
+    else:
+        out_ref, router_ref = extra
     rows, cap = got_ref.shape[0], up_ref.shape[0]
     chunk, half = pl.program_id(0), pl.program_id(1)
 
@@ -154,6 +198,12 @@
         for b in range(2):
             part = shares_ref[:, b * LANES : (b + 1) * LANES].astype(F32)
             router_ref[8 * b : 8 * (b + 1), :] = jnp.sum(part.reshape(rows // 8, 8, LANES), axis=0)
+
+    if len(extra) > 2:
+
+        @pl.when((chunk == 0) & (half == 0))
+        def _():
+            token_grads(raw_ref[...], gated_ref[...], grad_ref[...], weight_ref, token_ref)
 
     picked = matmul(place_ref[half], got_ref[...], TN).astype(BF16)
     out_ref[...] = matmul(picked, up_ref[...], TN).astype(BF16)
@@ -196,31 +246,71 @@
         )(expert_picks, upstream, weight)
         return out
 
-    def owner_step(got, marks, lists):
-        if lists:
-            marks_spec = full(experts, LANES)
-        else:
-            marks_spec = pl.BlockSpec((rows, LANES), lambda i: (0, half_width // LANES))
+    columns = half_width + 2 * LANES
+
+    def owner_step(got):
         return pl.pallas_call(
-            functools.partial(owner_kernel, most, lists),
+            functools.partial(owner_kernel, most),
+            grid=(1,),
+            in_specs=[
+                pl.BlockSpec((rows, half_width), lambda i: (0, 0)),
+                pl.BlockSpec((rows, LANES), lambda i: (0, half_width // LANES)),
+                full(tok_rows, width),
+                full(tok_rows, experts),
+            ],
+            out_specs=[full(rows, columns), full(rows, HALVES * tok_rows), full(tok_rows, experts)],
+            out_shape=[
+                shape_of((rows, columns), BF16),
+                shape_of((rows, HALVES * tok_rows), BF16),
+                shape_of((tok_rows, experts), BF16),
+            ],
+            compiler_params=params(),
+            name="owner_step",
+        )(got, got, tokens, logits)
+
+    def rows_step(lists):
+        return pl.pallas_call(
+            functools.partial(rows_kernel, most),
+            grid=(1,),
+            in_specs=[full(experts, LANES), full(tok_rows, width), full(tok_rows, experts)],
+            out_specs=[
+                pl.BlockSpec((rows, half_width), lambda i: (0, 0)),
+                full(rows, HALVES * tok_rows),
+                full(rows, tok_rows),
+            ],
+            out_shape=[
+                shape_of((rows, columns), BF16),
+                shape_of((rows, HALVES * tok_rows), BF16),
+                shape_of((rows, tok_rows), BF16),
+            ],
+            compiler_params=params(),
+            name="rows_step",
+        )(lists, tokens, logits)
+
+    def grads_step(got, send, gated, chosen):
+        return pl.pallas_call(
+            functools.partial(grads_kernel, most),
             grid=(1,),
             in_specs=[
                 full(rows, half_width),
-                marks_spec,
+                pl.BlockSpec(memory_space=pl.ANY),
+                full(rows, HALVES * tok_rows),
+                full(rows, tok_rows),
                 full(tok_rows, width),
                 full(tok_rows, experts),
                 full(width, experts),
             ],
-            out_specs=[full(rows, half_width + 2 * LANES), full(tok_rows, width)],
-            out_shape=[
-                shape_of((rows, half_width + 2 * LANES), BF16),
-                shape_of((tok_rows, width), BF16),
-            ],
-            compiler_params=params(),
-            name="owner_step",
-        )(got, marks, tokens, logits, router_weight)
-
-    def final_step(got):
+            out_specs=[
+                pl.BlockSpec((rows, 2 * LANES), lambda i: (0, half_width // (2 * LANES))),
+                full(tok_rows, width),
+            ],
+            out_shape=[shape_of((rows, columns), BF16), shape_of((tok_rows, width), BF16)],
+            input_output_aliases={1: 0},
+            compiler_params=params(),
+            name="grads_step",
+        )(got, send, gated, chosen, tokens, logits, router_weight)
+
+    def final_step(got, known=()):
         chunks = 1
         piece = half_width // chunks
         return pl.pallas_call(
@@ -231,31 +321,40 @@
                 pl.BlockSpec((rows, 2 * LANES), lambda i, h: (0, half_width // (2 * LANES))),
                 full(1, cap),
                 full(cap, hidden),
-            ],
+            ]
+            + [
+                full(rows, half_width),
+                full(rows, HALVES * tok_rows),
+                full(tok_rows, experts),
+                full(width, experts),
+            ][: len(known)],
             out_specs=[
                 pl.BlockSpec((piece, hidden), lambda i, h: (h * chunks + i, 0)),
                 full(width // experts, experts),
-            ],
-            out_shape=[shape_of((width, hidden), BF16), shape_of((width // experts, experts), F32)],
+            ]
+            + [full(tok_rows, width)] * bool(known),
+            out_shape=[shape_of((width, hidden), BF16), shape_of((width // experts, experts), F32)]
+            + [shape_of((tok_rows, width), BF16)] * bool(known),
             scratch_shapes=[pltpu.VMEM((HALVES, rows, cap), BF16)],
             compiler_params=params(),
             name="final_step",
-        )(got, got, expert_picks, upstream)
-
-    def rest(got, marks, lists):
-        send, token_grad = owner_step(got, marks, lists)
-        weight_grad, router_grad = final_step(exchange(send, experts))
-        return token_grad, weight_grad[None], router_grad
+        )(got, got, expert_picks, upstream, *known)
 
     def ids_inside():
         (raw,) = raw_grads(False)
         got = exchange(raw, experts)
-        return rest(got, got, False)
+        send, gated, grad = owner_step(got)
+        known = (got, gated, grad, router_weight)
+        weight_grad, router_grad, token_grad = final_step(exchange(send, experts), known)
+        return token_grad, weight_grad[None], router_grad
 
     def ids_first():
         raw, named = raw_grads(True)
-        lists = exchange(named, experts)
-        return rest(exchange(raw, experts), lists, True)
+        send, gated, chosen = rows_step(exchange(named, experts))
+        raw, send = lax.optimization_barrier((raw, send))
+        send, token_grad = grads_step(exchange(raw, experts), send, gated, chosen)
+        weight_grad, router_grad = final_step(exchange(send, experts))
+        return token_grad, weight_grad[None], router_grad
 
     return lax.cond(lax.axis_index("dp") == 0, ids_inside, ids_first)
 

time: 152 us -> 149 us (0.980)
  blocking collectives: 137 us -> 133 us
    all_to_all x3, blocking collectives: 137 us -> 133 us  [exchange(): x = lax.all_to_all(x, 'expert', split_axis=0, concat_axis=0, tiled=True)]
    pallas_call x1 -> x2, Pallas kernels: 4.76 us -> 5.15 us  [the longest x1 3.98 us: grads_step(): pl.pallas_call(functools.partial(grads_kernel, most), grid=(1,), in_specs...]
where the time goes in v8:
time: 149 us; the launch traced here: 148 us
  blocking collectives  133 us (89%)
  Pallas kernels  15.2 us (10%)
    all_to_all x3, blocking collectives, exchange(): x = lax.all_to_all(x, 'expert', split_axis=0, concat_axis=0, tiled=True)  133 us
    pallas_call x1, Pallas kernels, raw_grads(): pl.pallas_call(functools.partial(raw_kernel, tok_rows, most), grid=(half_...  5.03 us
    pallas_call x1, Pallas kernels, final_step(): pl.pallas_call(functools.partial(final_kernel, tok_rows, most), grid=(chu...  5.02 us
    pallas_call x1, Pallas kernels, grads_step(): pl.pallas_call(functools.partial(grads_kernel, most), grid=(1,), in_specs...  3.98 us

profile of v8, /device:TPU:1, one launch (start us, length us, event | category | flops | bytes accessed | tf_op | source)
XLA Modules:
  0.0 148.5 jit_solution(1884800588702267165)
XLA Ops:
  0.6 147.8 %conditional.1 = (bf16[128,2048]{1,0:T(8,128)(2,1)}, f32[16,128]{1,0:T(8,128)}, bf16[2048,1024]{1,0:T(8,128)(2,1)}) conditional(s32[]{:T(128)} %convert_element_type.3, (s32[1,256]{1,0:T(1,128)}, bf16[256,1024]{1,0:T(8,128)(2,1)}, bf16[2,1024,1024]{2,1,0:T(8,128)(2,1)}, bf16[128,2048]{1,0:T(8,128)(2,1)}, f32[128,128]{1,0:T(8,128)}, ...), branch_computations={%region_0.0_spmd, %region_1.0_spmd} | conditional | bytes 16519332 | solution.py:359
  0.6 0.0 copy-start.2
  0.7 0.0 copy-start.6
  0.7 5.0 %raw_grads.2 = (bf16[1024,1024]{1,0:T(8,128)(2,1)S(1)}, f32[128,128]{1,0:T(8,128)S(1)}) custom-call(s32[1,256]{1,0:T(1,128)} %get-tuple-element.24.picks_ref.refs_2_, bf16[256,1024]{1,0:T(8,128)(2,1)} %get-tuple-element.25.up_ref.refs_3_, bf16[2,1024,1024]{2,1,0:T(8,128)(2,1)} %get-tuple-element.26.weight_ref), custom_call_target="tpu_custom_call" | custom-call | tf_op jit(solution)/shard_map/cond/branch_0_fun/raw_grads/pallas_call | solution.py:233
  5.7 0.0 copy-start.4
  5.7 27.0 %all_to_all.20 = f32[128,1,128]{2,1,0:T(1,128)S(1)} all-to-all(f32[128,1,128]{2,1,0:T(1,128)S(1)} %bitcast.28), channel_id=1, replica_groups=mesh['expert'=128,'dp'=2] {'expert'}, dimensions={0} | all-to-all | bytes 131072 | tf_op jit(solution)/shard_map/cond/branch_0_fun/all_to_all | solution.py:214
  32.7 0.0 copy-done.2
  32.7 0.0 copy-done.6
  32.7 1.2 rows_step.1
  33.9 45.4 %all_to_all.21 = bf16[128,8,1024]{2,1,0:T(8,128)(2,1)S(1)} all-to-all(bf16[128,8,1024]{2,1,0:T(8,128)(2,1)S(1)} %bitcast.26), channel_id=1, replica_groups=mesh['expert'=128,'dp'=2] {'expert'}, dimensions={0} | all-to-all | bytes 4194304 | tf_op jit(solution)/shard_map/cond/branch_0_fun/all_to_all | solution.py:214
  79.3 0.0 copy-done.4
  79.3 4.0 %grads_step.1 = (bf16[1024,1280]{1,0:T(8,128)(2,1)S(1)}, bf16[128,2048]{1,0:T(8,128)(2,1)}) custom-call(bf16[1024,1024]{1,0:T(8,128)(2,1)S(1)} %bitcast.24, bf16[1024,1280]{1,0:T(8,128)(2,1)S(1)} %get-tuple-element.33.refs_1_, bf16[1024,256]{1,0:T(8,128)(2,1)S(1)} %get-tuple-element.34.refs_2_, ...), custom_call_target="tpu_custom_call", output_to_operand_aliasing={{0}: (1, {})} | custom-call | tf_op jit(solution)/shard_map/cond/branch_0_fun/grads_step/pallas_call | solution.py:291
  83.3 0.0 copy-start
  83.3 0.0 copy-start.8
  83.3 60.1 %all_to_all.22 = bf16[128,8,1280]{2,1,0:T(8,128)(2,1)S(1)} all-to-all(bf16[128,8,1280]{2,1,0:T(8,128)(2,1)S(1)} %bitcast.22), channel_id=1, replica_groups=mesh['expert'=128,'dp'=2] {'expert'}, dimensions={0} | all-to-all | bytes 5242880 | tf_op jit(solution)/shard_map/cond/branch_0_fun/all_to_all | solution.py:214
  143.4 0.0 copy-done
  143.4 0.0 copy-done.8
  143.4 5.0 %final_step.2 = (bf16[2048,1024]{1,0:T(8,128)(2,1)}, f32[16,128]{1,0:T(8,128)}) custom-call(bf16[1024,1280]{1,0:T(8,128)(2,1)S(1)} %bitcast.20, bf16[1024,1280]{1,0:T(8,128)(2,1)S(1)} %bitcast.21, s32[1,256]{1,0:T(1,128)S(1)} %copy-done.8, bf16[256,1024]{1,0:T(8,128)(2,1)S(1)} %copy-done), custom_call_target="tpu_custom_call" | custom-call | tf_op jit(solution)/shard_map/cond/branch_0_fun/final_step/pallas_call | solution.py:316
Async XLA Ops:
  0.6 32.1 %copy-start.2 = (bf16[128,2048]{1,0:T(8,128)(2,1)S(1)}, bf16[128,2048]{1,0:T(8,128)(2,1)}, u32[]{:S(2)}) copy-start(bf16[128,2048]{1,0:T(8,128)(2,1)} %get-tuple-element.29.tokens_ref.refs_4_) | copy-start | bytes 1572868 | tf_op jit(solution)/shard_map/cond
  0.7 32.1 %copy-start.6 = (f32[128,128]{1,0:T(8,128)S(1)}, f32[128,128]{1,0:T(8,128)}, u32[]{:S(2)}) copy-start(f32[128,128]{1,0:T(8,128)} %get-tuple-element.30.logits_ref.refs_5_) | copy-start | bytes 196612 | tf_op jit(solution)/shard_map/cond
  5.7 73.6 %copy-start.4 = (bf16[2048,128]{1,0:T(8,128)(2,1)S(1)}, bf16[2048,128]{1,0:T(8,128)(2,1)}, u32[]{:S(2)}) copy-start(bf16[2048,128]{1,0:T(8,128)(2,1)} %get-tuple-element.36.refs_6_) | copy-start | bytes 1572868 | tf_op jit(solution)/shard_map/cond
  83.3 60.1 %copy-start = (bf16[256,1024]{1,0:T(8,128)(2,1)S(1)}, bf16[256,1024]{1,0:T(8,128)(2,1)}, u32[]{:S(2)}) copy-start(bf16[256,1024]{1,0:T(8,128)(2,1)} %get-tuple-element.25.up_ref.refs_3_) | copy-start | bytes 1572868 | tf_op jit(solution)/shard_map/cond
  83.3 60.1 %copy-start.8 = (s32[1,256]{1,0:T(1,128)S(1)}, s32[1,256]{1,0:T(1,128)}, u32[]{:S(2)}) copy-start(s32[1,256]{1,0:T(1,128)} %get-tuple-element.24.picks_ref.refs_2_) | copy-start | bytes 3076 | tf_op jit(solution)/shard_map/cond

commit v9 on v8

--- a/solution.py
+++ b/solution.py
@@ -57,8 +57,7 @@
     return matmul(left, right, NT)
 
 
-def raw_kernel(tok_rows, most, picks_ref, up_ref, weight_ref, out_ref, *rest):
-    place_ref = rest[-1]
+def raw_kernel(tok_rows, most, picks_ref, up_ref, weight_ref, out_ref, place_ref, *rest):
     step = pl.program_id(0)
     rows, cap = out_ref.shape[0], up_ref.shape[0]
     half_width = weight_ref.shape[1] * pl.num_programs(0)
@@ -68,7 +67,7 @@
         wanted = picks_ref[...]
         hot = place_rows(rows, wanted, tok_rows, most)
         place_ref[...] = hot.astype(F32).astype(BF16)
-        if len(rest) > 1:
+        if rest:
             rest[0][...] = name_lists(wanted, rest[0].shape[0], tok_rows, most)
         else:
             marks = slots_of(wanted, tok_rows, most)[2]
@@ -180,32 +179,21 @@
     token_grads(got, gated_ref[...], logit_grad, router_ref, token_ref)
 
 
-def final_kernel(tok_rows, most, *refs):
-    got_ref, shares_ref, picks_ref, up_ref, *extra = refs
-    *extra, place_ref = extra
-    if len(extra) > 2:
-        raw_ref, gated_ref, grad_ref, weight_ref, out_ref, router_ref, token_ref = extra
-    else:
-        out_ref, router_ref = extra
-    rows, cap = got_ref.shape[0], up_ref.shape[0]
-    chunk, half = pl.program_id(0), pl.program_id(1)
-
-    @pl.when((chunk == 0) & (half == 0))
+def final_kernel(got_ref, shares_ref, place_ref, up_ref, *refs):
+    rows = got_ref.shape[0]
+
+    @pl.when((pl.program_id(0) == 0) & (pl.program_id(1) == 0))
     def _():
-        hot = place_rows(rows, picks_ref[...], tok_rows, most).astype(F32).astype(BF16)
-        for h in range(HALVES):
-            place_ref[h] = hot[:, h * cap : (h + 1) * cap]
+        if len(refs) > 2:
+            raw_ref, gated_ref, grad_ref, weight_ref, _, _, token_ref = refs
+            token_grads(raw_ref[...], gated_ref[...], grad_ref[...], weight_ref, token_ref)
+        router_ref = refs[1] if len(refs) == 2 else refs[-2]
         for b in range(2):
             part = shares_ref[:, b * LANES : (b + 1) * LANES].astype(F32)
             router_ref[8 * b : 8 * (b + 1), :] = jnp.sum(part.reshape(rows // 8, 8, LANES), axis=0)
 
-    if len(extra) > 2:
-
-        @pl.when((chunk == 0) & (half == 0))
-        def _():
-            token_grads(raw_ref[...], gated_ref[...], grad_ref[...], weight_ref, token_ref)
-
-    picked = matmul(place_ref[half], got_ref[...], TN).astype(BF16)
+    out_ref = refs[0] if len(refs) == 2 else refs[-3]
+    picked = matmul(place_ref[...], got_ref[...], TN).astype(BF16)
     out_ref[...] = matmul(picked, up_ref[...], TN).astype(BF16)
 
 
@@ -238,9 +226,9 @@
                 full(cap, hidden),
                 pl.BlockSpec((HALVES, STEP, hidden), lambda i: (0, i, 0)),
             ],
-            out_specs=[full(rows, columns)] + [full(experts, LANES)] * lists,
-            out_shape=[shape_of((rows, columns), BF16)] + [shape_of((experts, LANES), F32)] * lists,
-            scratch_shapes=[pltpu.VMEM((rows, HALVES * cap), BF16)],
+            out_specs=[full(rows, columns), full(rows, HALVES * cap)] + [full(experts, LANES)] * lists,
+            out_shape=[shape_of((rows, columns), BF16), shape_of((rows, HALVES * cap), BF16)]
+            + [shape_of((experts, LANES), F32)] * lists,
             compiler_params=params(),
             name="raw_grads",
         )(expert_picks, upstream, weight)
@@ -310,16 +298,16 @@
             name="grads_step",
         )(got, send, gated, chosen, tokens, logits, router_weight)
 
-    def final_step(got, known=()):
+    def final_step(got, place, known=()):
         chunks = 1
         piece = half_width // chunks
         return pl.pallas_call(
-            functools.partial(final_kernel, tok_rows, most),
+            final_kernel,
             grid=(chunks, HALVES),
             in_specs=[
                 pl.BlockSpec((rows, piece), lambda i, h: (0, i)),
                 pl.BlockSpec((rows, 2 * LANES), lambda i, h: (0, half_width // (2 * LANES))),
-                full(1, cap),
+                pl.BlockSpec((rows, cap), lambda i, h: (0, h)),
                 full(cap, hidden),
             ]
             + [
@@ -335,25 +323,24 @@
             + [full(tok_rows, width)] * bool(known),
             out_shape=[shape_of((width, hidden), BF16), shape_of((width // experts, experts), F32)]
             + [shape_of((tok_rows, width), BF16)] * bool(known),
-            scratch_shapes=[pltpu.VMEM((HALVES, rows, cap), BF16)],
             compiler_params=params(),
             name="final_step",
-        )(got, got, expert_picks, upstream, *known)
+        )(got, got, place, upstream, *known)
 
     def ids_inside():
-        (raw,) = raw_grads(False)
+        raw, place = raw_grads(False)
         got = exchange(raw, experts)
         send, gated, grad = owner_step(got)
         known = (got, gated, grad, router_weight)
-        weight_grad, router_grad, token_grad = final_step(exchange(send, experts), known)
+        weight_grad, router_grad, token_grad = final_step(exchange(send, experts), place, known)
         return token_grad, weight_grad[None], router_grad
 
     def ids_first():
-        raw, named = raw_grads(True)
+        raw, place, named = raw_grads(True)
         send, gated, chosen = rows_step(exchange(named, experts))
         raw, send = lax.optimization_barrier((raw, send))
         send, token_grad = grads_step(exchange(raw, experts), send, gated, chosen)
-        weight_grad, router_grad = final_step(exchange(send, experts))
+        weight_grad, router_grad = final_step(exchange(send, experts), place)
         return token_grad, weight_grad[None], router_grad
 
     return lax.cond(lax.axis_index("dp") == 0, ids_inside, ids_first)

time: 149 us -> 148 us (level)
  no operation moved by 1% of the time
where the time goes in v9:
time: 148 us
  blocking collectives  133 us (90%)
  Pallas kernels  14.7 us (10%)
    all_to_all x3, blocking collectives, exchange(): x = lax.all_to_all(x, 'expert', split_axis=0, concat_axis=0, tiled=True)  133 us
    pallas_call x1, Pallas kernels, raw_grads(): pl.pallas_call(functools.partial(raw_kernel, tok_rows, most), grid=(half_...  5.03 us
    pallas_call x1, Pallas kernels, final_step(): pl.pallas_call(final_kernel, grid=(chunks, HALVES), in_specs=[pl.BlockSpe...  4.56 us
    pallas_call x1, Pallas kernels, grads_step(): pl.pallas_call(functools.partial(grads_kernel, most), grid=(1,), in_specs...  3.98 us

profile of v9, /device:TPU:1, one launch (start us, length us, event | category | flops | bytes accessed | tf_op | source)
XLA Modules:
  0.0 148.0 jit_solution(9766440507007255459)
XLA Ops:
  0.6 147.4 %conditional.1 = (bf16[128,2048]{1,0:T(8,128)(2,1)}, f32[16,128]{1,0:T(8,128)}, bf16[2048,1024]{1,0:T(8,128)(2,1)}) conditional(s32[]{:T(128)} %convert_element_type.3, (s32[1,256]{1,0:T(1,128)}, bf16[256,1024]{1,0:T(8,128)(2,1)}, bf16[2,1024,1024]{2,1,0:T(8,128)(2,1)}, bf16[128,2048]{1,0:T(8,128)(2,1)}, f32[128,128]{1,0:T(8,128)}, ...), branch_computations={%region_0.0_spmd, %region_1.0_spmd} | conditional | bytes 16515208 | solution.py:346
  0.6 0.0 copy-start.2
  0.7 0.0 copy-start.6
  0.7 5.0 %raw_grads.2 = (bf16[1024,1024]{1,0:T(8,128)(2,1)S(1)}, bf16[1024,512]{1,0:T(8,128)(2,1)S(1)}, f32[128,128]{1,0:T(8,128)S(1)}) custom-call(s32[1,256]{1,0:T(1,128)} %get-tuple-element.24.picks_ref, bf16[256,1024]{1,0:T(8,128)(2,1)} %get-tuple-element.25.up_ref, bf16[2,1024,1024]{2,1,0:T(8,128)(2,1)} %get-tuple-element.26.weight_ref), custom_call_target="tpu_custom_call" | custom-call | tf_op jit(solution)/shard_map/cond/branch_0_fun/raw_grads/pallas_call | solution.py:221
  5.7 0.0 copy-start.4
  5.7 27.0 %all_to_all.20 = f32[128,1,128]{2,1,0:T(1,128)S(1)} all-to-all(f32[128,1,128]{2,1,0:T(1,128)S(1)} %bitcast.28), channel_id=1, replica_groups=mesh['expert'=128,'dp'=2] {'expert'}, dimensions={0} | all-to-all | bytes 131072 | tf_op jit(solution)/shard_map/cond/branch_0_fun/all_to_all | solution.py:202
  32.7 0.0 copy-done.2
  32.7 0.0 copy-done.6
  32.7 1.2 rows_step.1
  33.9 45.4 %all_to_all.21 = bf16[128,8,1024]{2,1,0:T(8,128)(2,1)S(1)} all-to-all(bf16[128,8,1024]{2,1,0:T(8,128)(2,1)S(1)} %bitcast.26), channel_id=1, replica_groups=mesh['expert'=128,'dp'=2] {'expert'}, dimensions={0} | all-to-all | bytes 4194304 | tf_op jit(solution)/shard_map/cond/branch_0_fun/all_to_all | solution.py:202
  79.3 0.0 copy-done.4
  79.3 4.0 %grads_step.1 = (bf16[1024,1280]{1,0:T(8,128)(2,1)S(1)}, bf16[128,2048]{1,0:T(8,128)(2,1)}) custom-call(bf16[1024,1024]{1,0:T(8,128)(2,1)S(1)} %bitcast.23, bf16[1024,1280]{1,0:T(8,128)(2,1)S(1)} %get-tuple-element.33.refs_1_, bf16[1024,256]{1,0:T(8,128)(2,1)S(1)} %get-tuple-element.34.refs_2_, ...), custom_call_target="tpu_custom_call", output_to_operand_aliasing={{0}: (1, {})} | custom-call | tf_op jit(solution)/shard_map/cond/branch_0_fun/grads_step/pallas_call | solution.py:279
  83.3 0.0 copy-start
  83.3 60.1 %all_to_all.22 = bf16[128,8,1280]{2,1,0:T(8,128)(2,1)S(1)} all-to-all(bf16[128,8,1280]{2,1,0:T(8,128)(2,1)S(1)} %bitcast.22), channel_id=1, replica_groups=mesh['expert'=128,'dp'=2] {'expert'}, dimensions={0} | all-to-all | bytes 5242880 | tf_op jit(solution)/shard_map/cond/branch_0_fun/all_to_all | solution.py:202
  143.4 0.0 copy-done
  143.4 4.6 %final_step.2 = (bf16[2048,1024]{1,0:T(8,128)(2,1)}, f32[16,128]{1,0:T(8,128)}) custom-call(bf16[1024,1280]{1,0:T(8,128)(2,1)S(1)} %bitcast.20, bf16[1024,1280]{1,0:T(8,128)(2,1)S(1)} %bitcast.21, bf16[1024,512]{1,0:T(8,128)(2,1)S(1)} %get-tuple-element.39.place_ref, bf16[256,1024]{1,0:T(8,128)(2,1)S(1)} %copy-done), custom_call_target="tpu_custom_call" | custom-call | tf_op jit(solution)/shard_map/cond/branch_0_fun/final_step/pallas_call | solution.py:304
Async XLA Ops:
  0.6 32.1 %copy-start.2 = (bf16[128,2048]{1,0:T(8,128)(2,1)S(1)}, bf16[128,2048]{1,0:T(8,128)(2,1)}, u32[]{:S(2)}) copy-start(bf16[128,2048]{1,0:T(8,128)(2,1)} %get-tuple-element.29.tokens_ref.refs_4_) | copy-start | bytes 1572868 | tf_op jit(solution)/shard_map/cond
  0.7 32.1 %copy-start.6 = (f32[128,128]{1,0:T(8,128)S(1)}, f32[128,128]{1,0:T(8,128)}, u32[]{:S(2)}) copy-start(f32[128,128]{1,0:T(8,128)} %get-tuple-element.30.logits_ref.refs_5_) | copy-start | bytes 196612 | tf_op jit(solution)/shard_map/cond
  5.7 73.6 %copy-start.4 = (bf16[2048,128]{1,0:T(8,128)(2,1)S(1)}, bf16[2048,128]{1,0:T(8,128)(2,1)}, u32[]{:S(2)}) copy-start(bf16[2048,128]{1,0:T(8,128)(2,1)} %get-tuple-element.36.refs_6_) | copy-start | bytes 1572868 | tf_op jit(solution)/shard_map/cond
  83.3 60.1 %copy-start = (bf16[256,1024]{1,0:T(8,128)(2,1)S(1)}, bf16[256,1024]{1,0:T(8,128)(2,1)}, u32[]{:S(2)}) copy-start(bf16[256,1024]{1,0:T(8,128)(2,1)} %get-tuple-element.25.up_ref) | copy-start | bytes 1572868 | tf_op jit(solution)/shard_map/cond

commit v10 on v9

--- a/solution.py
+++ b/solution.py
@@ -49,15 +49,16 @@
     return iota((rows, target.shape[1]), 0) == target
 
 
-def name_lists(wanted, owners_count, tok_rows, most):
-    owners, rank, marks = slots_of(wanted, tok_rows, most)
+def lists_kernel(tok_rows, most, picks_ref, out_ref):
+    owners, rank, marks = slots_of(picks_ref[...], tok_rows, most)
     cap = owners.shape[1]
-    left = jnp.where(iota((owners_count, cap), 0) == owners, marks, 0).astype(F32).astype(BF16)
+    owner = iota((out_ref.shape[0], cap), 0)
+    left = jnp.where(owner == owners, marks, 0).astype(F32).astype(BF16)
     right = (iota((LANES, cap), 0) == rank).astype(F32).astype(BF16)
-    return matmul(left, right, NT)
-
-
-def raw_kernel(tok_rows, most, picks_ref, up_ref, weight_ref, out_ref, place_ref, *rest):
+    out_ref[...] = matmul(left, right, NT)
+
+
+def raw_kernel(tok_rows, most, picks_ref, up_ref, weight_ref, out_ref, place_ref):
     step = pl.program_id(0)
     rows, cap = out_ref.shape[0], up_ref.shape[0]
     half_width = weight_ref.shape[1] * pl.num_programs(0)
@@ -67,9 +68,7 @@
         wanted = picks_ref[...]
         hot = place_rows(rows, wanted, tok_rows, most)
         place_ref[...] = hot.astype(F32).astype(BF16)
-        if rest:
-            rest[0][...] = name_lists(wanted, rest[0].shape[0], tok_rows, most)
-        else:
+        if out_ref.shape[1] > half_width:
             marks = slots_of(wanted, tok_rows, most)[2]
             both = jnp.concatenate([marks] * HALVES, axis=1)
             named = jnp.where(hot, both, 0).astype(F32).astype(BF16)
@@ -216,8 +215,7 @@
     full = lambda *shape: pl.BlockSpec(shape, lambda *_: (0,) * len(shape))
     shape_of = jax.ShapeDtypeStruct
 
-    def raw_grads(lists):
-        columns = half_width if lists else half_width + LANES
+    def raw_grads(columns, picks):
         out = pl.pallas_call(
             functools.partial(raw_kernel, tok_rows, most),
             grid=(half_width // STEP,),
@@ -226,12 +224,11 @@
                 full(cap, hidden),
                 pl.BlockSpec((HALVES, STEP, hidden), lambda i: (0, i, 0)),
             ],
-            out_specs=[full(rows, columns), full(rows, HALVES * cap)] + [full(experts, LANES)] * lists,
-            out_shape=[shape_of((rows, columns), BF16), shape_of((rows, HALVES * cap), BF16)]
-            + [shape_of((experts, LANES), F32)] * lists,
+            out_specs=[full(rows, columns), full(rows, HALVES * cap)],
+            out_shape=[shape_of((rows, columns), BF16), shape_of((rows, HALVES * cap), BF16)],
             compiler_params=params(),
             name="raw_grads",
-        )(expert_picks, upstream, weight)
+        )(picks, upstream, weight)
         return out
 
     columns = half_width + 2 * LANES
@@ -328,7 +325,7 @@
         )(got, got, place, upstream, *known)
 
     def ids_inside():
-        raw, place = raw_grads(False)
+        raw, place = raw_grads(half_width + LANES, expert_picks)
         got = exchange(raw, experts)
         send, gated, grad = owner_step(got)
         known = (got, gated, grad, router_weight)
@@ -336,9 +333,14 @@
         return token_grad, weight_grad[None], router_grad
 
     def ids_first():
-        raw, place, named = raw_grads(True)
+        named = pl.pallas_call(
+            functools.partial(lists_kernel, tok_rows, most),
+            out_shape=shape_of((experts, LANES), F32),
+            name="lists",
+        )(expert_picks)
         send, gated, chosen = rows_step(exchange(named, experts))
-        raw, send = lax.optimization_barrier((raw, send))
+        picks, send = lax.optimization_barrier((expert_picks, send))
+        raw, place = raw_grads(half_width, picks)
         send, token_grad = grads_step(exchange(raw, experts), send, gated, chosen)
         weight_grad, router_grad = final_step(exchange(send, experts), place)
         return token_grad, weight_grad[None], router_grad

time: 148 us -> 145 us (0.980)
  blocking collectives: 133 us -> 127 us
  Pallas kernels: 14.7 us -> 17.2 us
    all_to_all x3, blocking collectives: 133 us -> 127 us  [exchange(): x = lax.all_to_all(x, 'expert', split_axis=0, concat_axis=0, tiled=True)]
    pallas_call x0 -> x1, Pallas kernels: none -> 1.56 us  [ids_first(): pl.pallas_call(functools.partial(lists_kernel, tok_rows, most), out_shape...]
where the time goes in v10:
time: 145 us
  blocking collectives  127 us (88%)
  Pallas kernels  17.2 us (12%)
    all_to_all x3, blocking collectives, exchange(): x = lax.all_to_all(x, 'expert', split_axis=0, concat_axis=0, tiled=True)  127 us
    pallas_call x1, Pallas kernels, raw_grads(): pl.pallas_call(functools.partial(raw_kernel, tok_rows, most), grid=(half_...  4.86 us
    pallas_call x1, Pallas kernels, final_step(): pl.pallas_call(final_kernel, grid=(chunks, HALVES), in_specs=[pl.BlockSpe...  4.56 us
    pallas_call x1, Pallas kernels, grads_step(): pl.pallas_call(functools.partial(grads_kernel, most), grid=(1,), in_specs...  3.98 us

profile of v10, /device:TPU:1, one launch (start us, length us, event | category | flops | bytes accessed | tf_op | source)
XLA Modules:
  0.0 144.6 jit_solution(8496328659262158889)
XLA Ops:
  0.6 144.0 %conditional.1 = (bf16[128,2048]{1,0:T(8,128)(2,1)}, f32[16,128]{1,0:T(8,128)}, bf16[2048,1024]{1,0:T(8,128)(2,1)}) conditional(s32[]{:T(128)} %convert_element_type.3, (s32[1,256]{1,0:T(1,128)}, bf16[128,2048]{1,0:T(8,128)(2,1)}, f32[128,128]{1,0:T(8,128)}, bf16[256,1024]{1,0:T(8,128)(2,1)}, bf16[2,1024,1024]{2,1,0:T(8,128)(2,1)}, ...), branch_computations={%region_0.0_spmd, %region_1.0_spmd} | conditional | bytes 16515208 | solution.py:348
  0.6 1.6 %lists.1 = f32[128,128]{1,0:T(8,128)} custom-call(s32[1,256]{1,0:T(1,128)} %get-tuple-element.28.picks_ref), custom_call_target="tpu_custom_call" | custom-call | tf_op jit(solution)/shard_map/cond/branch_0_fun/lists/pallas_call | solution.py:336
  2.2 27.4 %all_to_all.20 = f32[128,1,128]{2,1,0:T(1,128)S(1)} all-to-all(f32[128,1,128]{2,1,0:T(1,128)} %bitcast.32), channel_id=1, replica_groups=mesh['expert'=128,'dp'=2] {'expert'}, dimensions={0} | all-to-all | bytes 131072 | tf_op jit(solution)/shard_map/cond/branch_0_fun/all_to_all | solution.py:201
  29.6 2.2 %rows_step.1 = (bf16[1024,1280]{1,0:T(8,128)(2,1)S(1)}, bf16[1024,256]{1,0:T(8,128)(2,1)S(1)}, bf16[1024,128]{1,0:T(8,128)(2,1)S(1)}) custom-call(f32[128,128]{1,0:T(8,128)S(1)} %bitcast.27, bf16[128,2048]{1,0:T(8,128)(2,1)} %get-tuple-element.25.tokens_ref.refs_4_, f32[128,128]{1,0:T(8,128)} %get-tuple-element.26.logits_ref.refs_5_), custom_call_target="tpu_custom_call" | custom-call | tf_op jit(solution)/shard_map/cond/branch_0_fun/rows_step/pallas_call | solution.py:257
  31.9 4.9 %raw_grads.2 = (bf16[1024,1024]{1,0:T(8,128)(2,1)S(1)}, bf16[1024,512]{1,0:T(8,128)(2,1)S(1)}) custom-call(s32[1,256]{1,0:T(1,128)} %get-tuple-element.28.picks_ref, bf16[256,1024]{1,0:T(8,128)(2,1)} %get-tuple-element.29.up_ref, bf16[2,1024,1024]{2,1,0:T(8,128)(2,1)} %get-tuple-element.30.weight_ref), custom_call_target="tpu_custom_call" | custom-call | tf_op jit(solution)/shard_map/cond/branch_0_fun/raw_grads/pallas_call | solution.py:219
  36.7 0.0 copy-start.2
  36.7 0.0 copy-start.4
  36.8 0.0 copy-start.6
  36.8 42.6 %all_to_all.21 = bf16[128,8,1024]{2,1,0:T(8,128)(2,1)S(1)} all-to-all(bf16[128,8,1024]{2,1,0:T(8,128)(2,1)S(1)} %bitcast.26), channel_id=1, replica_groups=mesh['expert'=128,'dp'=2] {'expert'}, dimensions={0} | all-to-all | bytes 4194304 | tf_op jit(solution)/shard_map/cond/branch_0_fun/all_to_all | solution.py:201
  79.3 0.0 copy-done.2
  79.3 0.0 copy-done.4
  79.3 0.0 copy-done.6
  79.3 4.0 %grads_step.1 = (bf16[1024,1280]{1,0:T(8,128)(2,1)S(1)}, bf16[128,2048]{1,0:T(8,128)(2,1)}) custom-call(bf16[1024,1024]{1,0:T(8,128)(2,1)S(1)} %bitcast.23, bf16[1024,1280]{1,0:T(8,128)(2,1)S(1)} %get-tuple-element.32.refs_1_, bf16[1024,256]{1,0:T(8,128)(2,1)S(1)} %get-tuple-element.33.refs_2_, ...), custom_call_target="tpu_custom_call", output_to_operand_aliasing={{0}: (1, {})} | custom-call | tf_op jit(solution)/shard_map/cond/branch_0_fun/grads_step/pallas_call | solution.py:276
  83.3 0.0 copy-start
  83.3 56.7 %all_to_all.22 = bf16[128,8,1280]{2,1,0:T(8,128)(2,1)S(1)} all-to-all(bf16[128,8,1280]{2,1,0:T(8,128)(2,1)S(1)} %bitcast.22), channel_id=1, replica_groups=mesh['expert'=128,'dp'=2] {'expert'}, dimensions={0} | all-to-all | bytes 5242880 | tf_op jit(solution)/shard_map/cond/branch_0_fun/all_to_all | solution.py:201
  140.0 0.0 copy-done
  140.0 4.6 %final_step.2 = (bf16[2048,1024]{1,0:T(8,128)(2,1)}, f32[16,128]{1,0:T(8,128)}) custom-call(bf16[1024,1280]{1,0:T(8,128)(2,1)S(1)} %bitcast.20, bf16[1024,1280]{1,0:T(8,128)(2,1)S(1)} %bitcast.21, bf16[1024,512]{1,0:T(8,128)(2,1)S(1)} %get-tuple-element.38.place_ref, bf16[256,1024]{1,0:T(8,128)(2,1)S(1)} %copy-done), custom_call_target="tpu_custom_call" | custom-call | tf_op jit(solution)/shard_map/cond/branch_0_fun/final_step/pallas_call | solution.py:301
Async XLA Ops:
  36.7 42.6 %copy-start.2 = (bf16[128,2048]{1,0:T(8,128)(2,1)S(1)}, bf16[128,2048]{1,0:T(8,128)(2,1)}, u32[]{:S(2)}) copy-start(bf16[128,2048]{1,0:T(8,128)(2,1)} %get-tuple-element.25.tokens_ref.refs_4_) | copy-start | bytes 1572868 | tf_op jit(solution)/shard_map/cond
  36.7 42.6 %copy-start.4 = (bf16[2048,128]{1,0:T(8,128)(2,1)S(1)}, bf16[2048,128]{1,0:T(8,128)(2,1)}, u32[]{:S(2)}) copy-start(bf16[2048,128]{1,0:T(8,128)(2,1)} %get-tuple-element.35.refs_6_) | copy-start | bytes 1572868 | tf_op jit(solution)/shard_map/cond
  36.8 42.6 %copy-start.6 = (f32[128,128]{1,0:T(8,128)S(1)}, f32[128,128]{1,0:T(8,128)}, u32[]{:S(2)}) copy-start(f32[128,128]{1,0:T(8,128)} %get-tuple-element.26.logits_ref.refs_5_) | copy-start | bytes 196612 | tf_op jit(solution)/shard_map/cond
  83.3 56.7 %copy-start = (bf16[256,1024]{1,0:T(8,128)(2,1)S(1)}, bf16[256,1024]{1,0:T(8,128)(2,1)}, u32[]{:S(2)}) copy-start(bf16[256,1024]{1,0:T(8,128)(2,1)} %get-tuple-element.29.up_ref) | copy-start | bytes 1572868 | tf_op jit(solution)/shard_map/cond

commit v11 on v10

--- a/solution.py
+++ b/solution.py
@@ -12,6 +12,7 @@
 I32 = jnp.int32
 LANES = 128
 HALVES = 2
+PARTS = 2
 STEP = 512
 
 NN = ((1,), (0,))
@@ -179,6 +180,7 @@
 
 
 def final_kernel(got_ref, shares_ref, place_ref, up_ref, *refs):
+    *refs, picked_ref = refs
     rows = got_ref.shape[0]
 
     @pl.when((pl.program_id(0) == 0) & (pl.program_id(1) == 0))
@@ -192,8 +194,15 @@
             router_ref[8 * b : 8 * (b + 1), :] = jnp.sum(part.reshape(rows // 8, 8, LANES), axis=0)
 
     out_ref = refs[0] if len(refs) == 2 else refs[-3]
-    picked = matmul(place_ref[...], got_ref[...], TN).astype(BF16)
-    out_ref[...] = matmul(picked, up_ref[...], TN).astype(BF16)
+
+    @pl.when(pl.program_id(1) == 0)
+    def _():
+        picked = matmul(place_ref[...], got_ref[...], TN).astype(BF16)
+        for part in range(PARTS):
+            size = picked.shape[1] // PARTS
+            picked_ref[part] = picked[:, part * size : (part + 1) * size]
+
+    out_ref[...] = matmul(picked_ref[pl.program_id(1)], up_ref[...], TN).astype(BF16)
 
 
 def exchange(x, blocks):
@@ -296,15 +305,14 @@
         )(got, send, gated, chosen, tokens, logits, router_weight)
 
     def final_step(got, place, known=()):
-        chunks = 1
-        piece = half_width // chunks
+        piece = half_width // PARTS
         return pl.pallas_call(
             final_kernel,
-            grid=(chunks, HALVES),
+            grid=(HALVES, PARTS),
             in_specs=[
-                pl.BlockSpec((rows, piece), lambda i, h: (0, i)),
-                pl.BlockSpec((rows, 2 * LANES), lambda i, h: (0, half_width // (2 * LANES))),
-                pl.BlockSpec((rows, cap), lambda i, h: (0, h)),
+                pl.BlockSpec((rows, half_width), lambda h, i: (0, 0)),
+                pl.BlockSpec((rows, 2 * LANES), lambda h, i: (0, half_width // (2 * LANES))),
+                pl.BlockSpec((rows, cap), lambda h, i: (0, h)),
                 full(cap, hidden),
             ]
             + [
@@ -314,12 +322,13 @@
                 full(width, experts),
             ][: len(known)],
             out_specs=[
-                pl.BlockSpec((piece, hidden), lambda i, h: (h * chunks + i, 0)),
+                pl.BlockSpec((piece, hidden), lambda h, i: (h * PARTS + i, 0)),
                 full(width // experts, experts),
             ]
             + [full(tok_rows, width)] * bool(known),
             out_shape=[shape_of((width, hidden), BF16), shape_of((width // experts, experts), F32)]
             + [shape_of((tok_rows, width), BF16)] * bool(known),
+            scratch_shapes=[pltpu.VMEM((PARTS, cap, piece), BF16)],
             compiler_params=params(),
             name="final_step",
         )(got, got, place, upstream, *known)

time: 145 us -> 146 us (level)
  no operation moved by 1% of the time
where the time goes in v11:
time: 146 us; the launch traced here: 145 us
  blocking collectives  127 us (87%)
  Pallas kernels  17.8 us (12%)
    all_to_all x3, blocking collectives, exchange(): x = lax.all_to_all(x, 'expert', split_axis=0, concat_axis=0, tiled=True)  127 us
    pallas_call x1, Pallas kernels, final_step(): pl.pallas_call(final_kernel, grid=(HALVES, PARTS), in_specs=[pl.BlockSpec...  5.23 us
    pallas_call x1, Pallas kernels, raw_grads(): pl.pallas_call(functools.partial(raw_kernel, tok_rows, most), grid=(half_...  4.86 us
    pallas_call x1, Pallas kernels, grads_step(): pl.pallas_call(functools.partial(grads_kernel, most), grid=(1,), in_specs...  3.98 us

profile of v11, /device:TPU:1, one launch (start us, length us, event | category | flops | bytes accessed | tf_op | source)
XLA Modules:
  0.0 145.3 jit_solution(14522461853411376479)
XLA Ops:
  0.6 144.6 %conditional.1 = (bf16[128,2048]{1,0:T(8,128)(2,1)}, f32[16,128]{1,0:T(8,128)}, bf16[2048,1024]{1,0:T(8,128)(2,1)}) conditional(s32[]{:T(128)} %convert_element_type.3, (s32[1,256]{1,0:T(1,128)}, bf16[128,2048]{1,0:T(8,128)(2,1)}, f32[128,128]{1,0:T(8,128)}, bf16[256,1024]{1,0:T(8,128)(2,1)}, bf16[2,1024,1024]{2,1,0:T(8,128)(2,1)}, ...), branch_computations={%region_0.0_spmd, %region_1.0_spmd} | conditional | bytes 16515208 | solution.py:357
  0.6 1.6 %lists.1 = f32[128,128]{1,0:T(8,128)} custom-call(s32[1,256]{1,0:T(1,128)} %get-tuple-element.28.picks_ref), custom_call_target="tpu_custom_call" | custom-call | tf_op jit(solution)/shard_map/cond/branch_0_fun/lists/pallas_call | solution.py:345
  2.2 27.4 %all_to_all.20 = f32[128,1,128]{2,1,0:T(1,128)S(1)} all-to-all(f32[128,1,128]{2,1,0:T(1,128)} %bitcast.32), channel_id=1, replica_groups=mesh['expert'=128,'dp'=2] {'expert'}, dimensions={0} | all-to-all | bytes 131072 | tf_op jit(solution)/shard_map/cond/branch_0_fun/all_to_all | solution.py:210
  29.6 2.2 %rows_step.1 = (bf16[1024,1280]{1,0:T(8,128)(2,1)S(1)}, bf16[1024,256]{1,0:T(8,128)(2,1)S(1)}, bf16[1024,128]{1,0:T(8,128)(2,1)S(1)}) custom-call(f32[128,128]{1,0:T(8,128)S(1)} %bitcast.27, bf16[128,2048]{1,0:T(8,128)(2,1)} %get-tuple-element.25.tokens_ref.refs_4_, f32[128,128]{1,0:T(8,128)} %get-tuple-element.26.logits_ref.refs_5_), custom_call_target="tpu_custom_call" | custom-call | tf_op jit(solution)/shard_map/cond/branch_0_fun/rows_step/pallas_call | solution.py:266
  31.9 4.9 %raw_grads.2 = (bf16[1024,1024]{1,0:T(8,128)(2,1)S(1)}, bf16[1024,512]{1,0:T(8,128)(2,1)S(1)}) custom-call(s32[1,256]{1,0:T(1,128)} %get-tuple-element.28.picks_ref, bf16[256,1024]{1,0:T(8,128)(2,1)} %get-tuple-element.29.up_ref, bf16[2,1024,1024]{2,1,0:T(8,128)(2,1)} %get-tuple-element.30.weight_ref), custom_call_target="tpu_custom_call" | custom-call | tf_op jit(solution)/shard_map/cond/branch_0_fun/raw_grads/pallas_call | solution.py:228
  36.7 0.0 copy-start.2
  36.7 0.0 copy-start.4
  36.8 0.0 copy-start.6
  36.8 42.6 %all_to_all.21 = bf16[128,8,1024]{2,1,0:T(8,128)(2,1)S(1)} all-to-all(bf16[128,8,1024]{2,1,0:T(8,128)(2,1)S(1)} %bitcast.26), channel_id=1, replica_groups=mesh['expert'=128,'dp'=2] {'expert'}, dimensions={0} | all-to-all | bytes 4194304 | tf_op jit(solution)/shard_map/cond/branch_0_fun/all_to_all | solution.py:210
  79.3 0.0 copy-done.2
  79.3 0.0 copy-done.4
  79.3 0.0 copy-done.6
  79.3 4.0 %grads_step.1 = (bf16[1024,1280]{1,0:T(8,128)(2,1)S(1)}, bf16[128,2048]{1,0:T(8,128)(2,1)}) custom-call(bf16[1024,1024]{1,0:T(8,128)(2,1)S(1)} %bitcast.23, bf16[1024,1280]{1,0:T(8,128)(2,1)S(1)} %get-tuple-element.32.refs_1_, bf16[1024,256]{1,0:T(8,128)(2,1)S(1)} %get-tuple-element.33.refs_2_, ...), custom_call_target="tpu_custom_call", output_to_operand_aliasing={{0}: (1, {})} | custom-call | tf_op jit(solution)/shard_map/cond/branch_0_fun/grads_step/pallas_call | solution.py:285
  83.3 0.0 copy-start
  83.3 56.7 %all_to_all.22 = bf16[128,8,1280]{2,1,0:T(8,128)(2,1)S(1)} all-to-all(bf16[128,8,1280]{2,1,0:T(8,128)(2,1)S(1)} %bitcast.22), channel_id=1, replica_groups=mesh['expert'=128,'dp'=2] {'expert'}, dimensions={0} | all-to-all | bytes 5242880 | tf_op jit(solution)/shard_map/cond/branch_0_fun/all_to_all | solution.py:210
  140.0 0.0 copy-done
  140.0 5.2 %final_step.2 = (bf16[2048,1024]{1,0:T(8,128)(2,1)}, f32[16,128]{1,0:T(8,128)}) custom-call(bf16[1024,1280]{1,0:T(8,128)(2,1)S(1)} %bitcast.20, bf16[1024,1280]{1,0:T(8,128)(2,1)S(1)} %bitcast.21, bf16[1024,512]{1,0:T(8,128)(2,1)S(1)} %get-tuple-element.38.place_ref, bf16[256,1024]{1,0:T(8,128)(2,1)S(1)} %copy-done), custom_call_target="tpu_custom_call" | custom-call | tf_op jit(solution)/shard_map/cond/branch_0_fun/final_step/pallas_call | solution.py:309
Async XLA Ops:
  36.7 42.6 %copy-start.2 = (bf16[128,2048]{1,0:T(8,128)(2,1)S(1)}, bf16[128,2048]{1,0:T(8,128)(2,1)}, u32[]{:S(2)}) copy-start(bf16[128,2048]{1,0:T(8,128)(2,1)} %get-tuple-element.25.tokens_ref.refs_4_) | copy-start | bytes 1572868 | tf_op jit(solution)/shard_map/cond
  36.7 42.6 %copy-start.4 = (bf16[2048,128]{1,0:T(8,128)(2,1)S(1)}, bf16[2048,128]{1,0:T(8,128)(2,1)}, u32[]{:S(2)}) copy-start(bf16[2048,128]{1,0:T(8,128)(2,1)} %get-tuple-element.35.refs_6_) | copy-start | bytes 1572868 | tf_op jit(solution)/shard_map/cond
  36.8 42.6 %copy-start.6 = (f32[128,128]{1,0:T(8,128)S(1)}, f32[128,128]{1,0:T(8,128)}, u32[]{:S(2)}) copy-start(f32[128,128]{1,0:T(8,128)} %get-tuple-element.26.logits_ref.refs_5_) | copy-start | bytes 196612 | tf_op jit(solution)/shard_map/cond
  83.3 56.7 %copy-start = (bf16[256,1024]{1,0:T(8,128)(2,1)S(1)}, bf16[256,1024]{1,0:T(8,128)(2,1)}, u32[]{:S(2)}) copy-start(bf16[256,1024]{1,0:T(8,128)(2,1)} %get-tuple-element.29.up_ref) | copy-start | bytes 1572868 | tf_op jit(solution)/shard_map/cond
